TPU v7x, 128 devices: a whole 4x4x4 slice. The times are simulated.
128 devices in a mesh: role: 8 (over z_hi, x), tp: 16 (over y, z_lo, core).
Axes of the slice: x: 4, y: 4, z: 4 (z_hi: 2, z_lo: 2; z = z_hi * 2 + z_lo), core: 2. Of those that a mesh axis runs over, the one named last changes fastest.
Arguments:
- text_embed: bfloat16 [8192, 8192], P('role', 'tp')
- vision_rows: bfloat16 [2048, 8192], P('role', 'tp'), may hold values from -6 to 6
- vision_group: int32 [2048], P('role'), may hold values from 0 to 7, as said below
- vision_slot: int32 [2048], P('role'), may hold values from 0 to 1023, as said below
- request_blocks: int32 [8, 8], P('role'), may hold values from 1 to 32, as said below
- ship_page: int32 [512], P('role'), may hold values from 0 to 16383, as said below
- paged_cache: bfloat16 [16384, 16, 2048], P(('role', 'tp')), may hold values from -6 to 6
- block_table: int32 [128, 256], P('role'), may hold values from -1 to 16383, as said below
- cache_len: int32 [128], P('role'), may hold values from 0 to 4096
- step_embed: bfloat16 [4, 128, 8192], P(None, 'role', 'tp')
- norm_gain: bfloat16 [8192], replicated, may hold values from 0.25 to 1.75
- query_weight: bfloat16 [8192, 8192], P(None, 'tp')
- keyvalue_weight: bfloat16 [8192, 2048], P(None, 'tp')
Outputs:
- prefill_out: bfloat16 [8192, 8192], P('role', 'tp')
- decode_out: bfloat16 [4, 128, 8192], P(None, 'role', 'tp')
Inputs may be any that keep to these rules, and one draw needn't show every extreme that they name: `vision_group`: of one group's 256 image rows at most 64 go to any one group, and one group receives exactly 64 from every group. `vision_slot`: image rows sent to one group have distinct positions. `request_blocks`: each row sums to 64; each group has one request of exactly 32 pages. `ship_page`: all named pages are distinct. Device number role * 16 + tp holds 128 consecutive pages. All pages of one request go to one group, and the requests of one group go to distinct groups (possibly its own), and of one group's 64 pages at most 2 go to any one device. `block_table`: rows of group h name only pages h * 2048 to (h + 1) * 2048 - 1, each of them exactly once over the group's rows; row r names its pages in order in its first ceil(cache_len[r] / 16) entries and -1 after them.
All inputs are finite; a program needn't handle non-finite values.
Results may differ from a plain program's by a relative error of at most 0.0055.
The roundings to bfloat16 on the way count: a program that leaves them out, or rounds other values in their place, can miss the bound.
Values may be sent and summed in bfloat16 or wider, within the bound.
No kernel may reach another device: no remote copies, remote signals or barrier semaphores. Data moves between devices by JAX's collectives and lax.ppermute only.
A program may use at most 256 MiB of HBM per device.

v0:
```python
import jax
import jax.numpy as jnp
from jax import lax
from jax.experimental import pallas as pl
from jax.experimental.pallas import tpu as pltpu
from jax.sharding import PartitionSpec as P

HEAD_SIZE = 128
KV_HEADS = 8
PAGE_TOKENS = 16
EPS = 1e-06
LOW = -1e30
SCALE = HEAD_SIZE ** (-0.5)
BF = jnp.bfloat16
F32 = jnp.float32
EXP2_SCALE = SCALE * 1.4426950408889634
LN2 = 0.6931471805599453
TP = 16
ROLE = 8
STAT_ROWS = 16

CORE = 1


def params(mebibytes):
    return pltpu.CompilerParams(vmem_limit_bytes=mebibytes * 2**20)


def vmem():
    return pl.BlockSpec(memory_space=pltpu.VMEM)


def smem():
    return pl.BlockSpec(memory_space=pltpu.SMEM)


def hbm():
    return pl.BlockSpec(memory_space=pl.ANY)


def swap(x, axis, mask):
    size = TP if axis == "tp" else ROLE
    return lax.ppermute(x, axis, [(i, i ^ mask) for i in range(size)])


def over_chips(x):
    return [x] + [swap(x, "tp", 2 * i) for i in range(1, 8)]


def more(held, axis, mask):
    return jnp.concatenate([held, swap(held, axis, mask)], axis=0)


def doubling(x, axis, masks):
    held = x[None]
    for mask in masks:
        held = more(held, axis, mask)
    return held


def offsets(masks):
    table = [0]
    for mask in masks:
        table = table + [v ^ mask for v in table]
    return table


ROLE_MASKS = (4, 1, 3)
ROLE_OFFSETS = offsets(ROLE_MASKS)


def nt_dot(a, b):
    return lax.dot_general(a, b, (((1,), (1,)), ((), ())), preferred_element_type=F32)


def nn_dot(a, b):
    return jnp.dot(a, b, preferred_element_type=F32)


def eye(n):
    return lax.broadcasted_iota(jnp.int32, (n, n), 0) == lax.broadcasted_iota(
        jnp.int32, (n, n), 1
    )


def to_row(column):
    n = column.shape[0]
    return jnp.sum(jnp.where(eye(n), column, 0.0), axis=0, keepdims=True)


def to_column(row):
    n = row.shape[1]
    return jnp.sum(jnp.where(eye(n), row, 0.0), axis=1, keepdims=True)


def split3(x):
    high = x.astype(BF)
    rest = x - high.astype(F32)
    middle = rest.astype(BF)
    low = (rest - middle.astype(F32)).astype(BF)
    return high, middle, low


def stat_block(level):
    parts = jnp.concatenate(
        [to_row(level[:128]), to_row(level[128:]), jnp.zeros((6, 128), F32)], axis=0
    )
    high, middle, low = split3(parts)
    return jnp.concatenate(
        [
            high[:2].astype(F32),
            middle[:2].astype(F32),
            low[:2].astype(F32),
            jnp.zeros((10, 128), F32),
        ],
        axis=0,
    ).astype(BF)


def stat_rows(block):
    wide = block.astype(F32)
    return wide[0:2] + wide[2:4] + wide[4:6]


def pick_kernel(group, slot, rows, out):
    count = group.shape[1]
    capacity = 2 * count // ROLE
    onehot = group[...] == lax.broadcasted_iota(jnp.int32, (ROLE, 1), 0)
    before = lax.broadcasted_iota(jnp.int32, (count, count), 0) < lax.broadcasted_iota(
        jnp.int32, (count, count), 1
    )
    rank = nn_dot(onehot.astype(F32).astype(BF), before.astype(F32).astype(BF))
    rank = jnp.sum(jnp.where(onehot, rank, 0.0), axis=0, keepdims=True).astype(jnp.int32)
    place = group[...] * capacity + rank
    picked = place == lax.broadcasted_iota(jnp.int32, (ROLE * capacity, 1), 0)
    picked = picked.astype(F32).astype(BF)
    chosen = nn_dot(picked, rows[...]).astype(BF)
    code = slot[...] + 1
    line = lax.broadcasted_iota(jnp.int32, (16, 1), 0)
    codes = jnp.where(line == 0, code // 32, jnp.where(line == 1, code % 32, 0))
    codes = nt_dot(codes.astype(F32).astype(BF), picked).astype(BF)
    for g in range(ROLE):
        out[g, :capacity, :] = chosen[g * capacity : (g + 1) * capacity]
        out[g, capacity:, :] = codes


def pick_rows(group, slot, rows):
    count, width = rows.shape
    capacity = 2 * count // ROLE
    return pl.pallas_call(
        pick_kernel,
        in_specs=[vmem()] * 3,
        out_specs=vmem(),
        out_shape=jax.ShapeDtypeStruct((ROLE, capacity + 16, width), BF),
        compiler_params=params(16),
        cost_estimate=pl.CostEstimate(flops=2 * 10**8, bytes_accessed=2**20, transcendentals=0),
        name="pick_rows",
    )(group.reshape(1, count), slot.reshape(1, count), rows)


def land_kernel(role, arrived, text, merged, squares):
    capacity = arrived.shape[1] - 16
    total = ROLE * capacity
    lane = lax.broadcasted_iota(jnp.int32, (1, total), 1)
    slots = jnp.zeros((1, total), F32)
    for s in range(ROLE):
        codes = arrived[s, capacity:, :].astype(F32)
        code = jnp.broadcast_to(codes[0:1] * 32.0 + codes[1:2], (8, total))
        shift = ((s + ROLE - role[0]) % ROLE) * capacity
        slots = jnp.where(lane // capacity == s, pltpu.roll(code, shift, 1)[0:1], slots)
    slots = slots.astype(jnp.int32) - 1
    rows = arrived[:, :capacity, :].reshape(total, arrived.shape[2])
    lines = []
    for n in range(text.shape[0] // 256):
        at = slice(n * 256, (n + 1) * 256)
        row = lax.broadcasted_iota(jnp.int32, (256, 1), 0) + n * 256
        landing = jnp.where(row == slots, 1.0, 0.0)
        hit = jnp.sum(landing, axis=1, keepdims=True) > 0.0
        block = jnp.where(hit, nn_dot(landing.astype(BF), rows), text[at, :].astype(F32))
        merged[at, :] = block.astype(BF)
        square = jnp.broadcast_to(jnp.sum(block * block, axis=1, keepdims=True), (256, 128))
        lines += [to_row(square[:128]), to_row(square[128:])]
    high, middle, rest = split3(jnp.concatenate(lines, axis=0))
    squares[...] = jnp.concatenate(
        [high.astype(F32), middle.astype(F32), rest.astype(F32), jnp.zeros((8, 128), F32)], axis=0
    ).astype(BF)


def land_rows(role, arrived, text):
    return pl.pallas_call(
        land_kernel,
        in_specs=[smem()] + [vmem()] * 2,
        out_specs=[vmem()] * 2,
        out_shape=[
            jax.ShapeDtypeStruct(text.shape, BF),
            jax.ShapeDtypeStruct((32, 128), BF),
        ],
        compiler_params=params(24),
        cost_estimate=pl.CostEstimate(flops=10**9, bytes_accessed=6 * 2**20, transcendentals=0),
        name="land_rows",
    )(role, arrived, text)


def step_kernel(order, low, xs, gain, wq, wa, wb, q_out, a_out, b_out, scale, acc):
    i = pl.program_id(0)

    @pl.when(i == 0)
    def _():
        total = jnp.zeros((xs.shape[1], 512), F32)
        for k in range(TP):
            wide = xs[k].astype(F32)
            total = total + wide * wide
        total = jnp.sum(total, axis=1, keepdims=True)
        scale[...] = jnp.broadcast_to(
            lax.rsqrt(total / (TP * xs.shape[2]) + EPS), scale.shape
        )
        acc[...] = jnp.zeros_like(acc)

    factor = jnp.broadcast_to(scale[:, :1], (xs.shape[1], 512))
    total_q = acc[:, :512]
    total_a = acc[:, 512:640]
    total_b = acc[:, 640:768]
    for j in range(4):
        place = low[0] ^ j
        block = j // 2 + 2 * i + 8 * (j % 2)
        rows = pl.ds(pl.multiple_of(place * 512, 512), 512)
        normed = (xs[block].astype(F32) * factor * gain[0, place].astype(F32)).astype(BF)
        total_q = total_q + nn_dot(normed, wq[rows, :])
        total_a = total_a + nn_dot(normed, wa[rows, :])
        total_b = total_b + nn_dot(normed, wb[rows, :])
    acc[:, :512] = total_q
    acc[:, 512:640] = total_a
    acc[:, 640:768] = total_b

    @pl.when(i == 3)
    def _():
        q_out[...] = acc[:, :512].astype(BF)
        a_out[...] = acc[:, 512:640].astype(BF)
        b_out[...] = acc[:, 640:768].astype(BF)


def step_project(order, low, xs, gain, wq, wa, wb):
    rows = xs.shape[1]
    return pl.pallas_call(
        step_kernel,
        grid_spec=pltpu.PrefetchScalarGridSpec(
            num_scalar_prefetch=2,
            grid=(4,),
            in_specs=[
                pl.BlockSpec(xs.shape, lambda i, o, l: (0, 0, 0)),
                pl.BlockSpec((1, 4, 1, 512), lambda i, o, l: (o[i], 0, 0, 0)),
                pl.BlockSpec((2048, 512), lambda i, o, l: (o[i], 0)),
                pl.BlockSpec((2048, 128), lambda i, o, l: (o[i], 0)),
                pl.BlockSpec((2048, 128), lambda i, o, l: (o[i], 0)),
            ],
            out_specs=[
                pl.BlockSpec((rows, 512), lambda i, o, l: (0, 0)),
                pl.BlockSpec((rows, 128), lambda i, o, l: (0, 0)),
                pl.BlockSpec((rows, 128), lambda i, o, l: (0, 0)),
            ],
            scratch_shapes=[pltpu.VMEM((rows, 128), F32), pltpu.VMEM((rows, 768), F32)],
        ),
        out_shape=[
            jax.ShapeDtypeStruct((rows, 512), BF),
            jax.ShapeDtypeStruct((rows, 128), BF),
            jax.ShapeDtypeStruct((rows, 128), BF),
        ],
        compiler_params=params(58),
        cost_estimate=pl.CostEstimate(
            flops=2 * rows * 8192 * 768, bytes_accessed=14 * 2**20, transcendentals=0
        ),
        name="step_project",
    )(order, low, xs, gain.reshape(4, 4, 1, 512), wq, wa, wb)


def row_factors(ssq, line, scale):
    factor = lax.rsqrt(ssq[...] / (TP * 512) + EPS)
    for n in range(scale.shape[0] // 128):
        scale[n * 128 : (n + 1) * 128, :] = jnp.broadcast_to(
            to_column(factor[line + n : line + n + 1]), (128, 128)
        )


def all_blocks(text, gain, weights, scale, xbuf, wbuf, xsem, wsem, acc):
    blocks, rows = text.shape[0], text.shape[1]
    for n in range(blocks):
        pltpu.make_async_copy(text.at[n], xbuf.at[n], xsem.at[n]).start()
        at = 0
        for k, weight in enumerate(weights):
            width = weight.shape[1]
            pltpu.make_async_copy(
                weight.at[pl.ds(n * 512, 512)], wbuf.at[n, :, pl.ds(at, width)], wsem.at[n, k]
            ).start()
            at += width

    def wait(n):
        pltpu.make_async_copy(xbuf.at[n], xbuf.at[n], xsem.at[n]).wait()
        at = 0
        for k, weight in enumerate(weights):
            part = wbuf.at[n, :, pl.ds(at, weight.shape[1])]
            pltpu.make_async_copy(part, part, wsem.at[n, k]).wait()
            at += weight.shape[1]

    def pair(i, carry):
        for n in (2 * i, 2 * i + 1):
            wait(n)
        gains = [gain[2 * i].astype(F32), gain[2 * i + 1].astype(F32)]
        for r in range(rows // 256):
            at = slice(r * 256, (r + 1) * 256)
            factor = scale[at, :1]
            product = None
            for k in range(2):
                normed = (xbuf[2 * i + k, at, :].astype(F32) * factor * gains[k]).astype(BF)
                term = nn_dot(normed, wbuf[2 * i + k])
                product = term if product is None else product + term
            acc[at, :] += product
        return carry

    acc[...] = jnp.zeros_like(acc)
    lax.fori_loop(0, blocks // 2, pair, 0)


def all_scratch(blocks, rows, width, kinds):
    return [
        pltpu.VMEM((blocks, rows, 512), BF),
        pltpu.VMEM((blocks, 512, width), BF),
        pltpu.VMEM((rows, 128), F32),
        pltpu.SemaphoreType.DMA((blocks,)),
        pltpu.SemaphoreType.DMA((blocks, kinds)),
        pltpu.VMEM((rows, width), F32),
    ]


def keys_kernel(
    core, start, group, text, ssq, gain, wa, wb, q, token_row,
    keys, values, out, xbuf, wbuf, scale, xsem, wsem, acc,
):
    row_factors(ssq, 0, scale)
    all_blocks(text, gain, (wa, wb), scale, xbuf, wbuf, xsem, wsem, acc)
    for n in range(acc.shape[0] // 256):
        at = slice(n * 256, (n + 1) * 256)
        own, other = acc[at, :128], acc[at, 128:]
        keys[at, :] = jnp.where(core[0] == 0, own, other).astype(BF)
        values[at, :] = jnp.where(core[0] == 0, other, own).astype(BF)
    fresh_groups(group, start, q, keys, values, token_row, out)


def finish_keys(core, start, group, text, ssq, gain, weights, q, token_row):
    blocks, rows, _ = text.shape
    return pl.pallas_call(
        keys_kernel,
        in_specs=[smem()] * 3 + [hbm()] + [vmem()] * 2 + [hbm()] * 2 + [vmem()] * 2,
        out_specs=[vmem()] * 3,
        out_shape=[
            jax.ShapeDtypeStruct((rows, 128), BF),
            jax.ShapeDtypeStruct((rows, 128), BF),
            jax.ShapeDtypeStruct((ROLE, 256 + STAT_ROWS, 128), BF),
        ],
        scratch_shapes=all_scratch(blocks, rows, 256, 2),
        compiler_params=params(58),
        cost_estimate=pl.CostEstimate(
            flops=6 * 10**9, bytes_accessed=20 * 2**20, transcendentals=2**20
        ),
        name="keys_and_fresh_pages",
    )(
        core, start, group, text, ssq, gain.reshape(TP, 1, 512), *weights, q, token_row
    )


def queries_kernel(
    blocks_ref, text, ssq, gain, weight, keys, values,
    out, xbuf, wbuf, scale, xsem, wsem, acc, q,
):
    row_factors(ssq, 0, scale)
    all_blocks(text, gain, (weight,), scale, xbuf, wbuf, xsem, wsem, acc)
    for n in range(acc.shape[0] // 256):
        at = slice(n * 256, (n + 1) * 256)
        q[at, :] = acc[at, :].astype(BF)
    position = lax.broadcasted_iota(jnp.int32, (1, q.shape[0]), 1)
    segment = jnp.zeros((1, q.shape[0]), F32)
    end = 0
    for n in range(blocks_ref.shape[1]):
        end = end + blocks_ref[0, n] * PAGE_TOKENS
        segment = segment + jnp.where(position >= end, 1.0, 0.0)
    prefill_kernel(q, keys, values, segment, out)


def finish_queries(request_blocks, text, ssq, gain, weight, keys, values):
    blocks, rows, _ = text.shape
    return pl.pallas_call(
        queries_kernel,
        in_specs=[smem(), hbm()] + [vmem()] * 2 + [hbm()] + [vmem()] * 2,
        out_specs=vmem(),
        out_shape=jax.ShapeDtypeStruct((rows, 512), BF),
        scratch_shapes=all_scratch(blocks, rows, 512, 1) + [pltpu.VMEM((rows, 512), BF)],
        compiler_params=params(58),
        cost_estimate=pl.CostEstimate(
            flops=12 * 10**9, bytes_accessed=25 * 2**20, transcendentals=3 * 2**20
        ),
        name="queries_and_prefill",
    )(request_blocks, text, ssq, gain.reshape(TP, 1, 512), weight, keys, values)


def paged_kernel(
    first_chunk, slot_page, slot_live, where, q, cache, out, kv, top, total, acc, lse, sem
):
    def fetch(i, carry):
        for j in range(8):
            pltpu.make_async_copy(
                cache.at[slot_page[i * 8 + j]],
                kv.at[i, pl.ds(j * PAGE_TOKENS, PAGE_TOKENS), :],
                sem.at[i],
            ).start()
        return carry

    lax.fori_loop(0, first_chunk[16], fetch, 0)
    lane = lax.broadcasted_iota(jnp.int32, (1, 128), 1)
    heads = range(KV_HEADS)

    def one_row(r, carry):
        top[...] = jnp.full_like(top, LOW)
        total[...] = jnp.zeros_like(total)
        acc[...] = jnp.zeros_like(acc)
        at = pl.multiple_of(r * 16, 16)
        queries = [
            jnp.concatenate(
                [q[where[2 * k], pl.ds(at, 16), :], q[where[2 * k + 1], pl.ds(at, 16), :]], axis=0
            )
            for k in heads
        ]

        def one_chunk(i, inner):
            live = jnp.zeros((1, 128), jnp.int32)
            for j in range(8):
                live = jnp.where(lane // PAGE_TOKENS == j, slot_live[i * 8 + j], live)
            valid = lane % PAGE_TOKENS < live
            pltpu.make_async_copy(kv.at[i], kv.at[i], sem.at[i]).wait()

            def part(column):
                return kv[i, :, column * 128 : (column + 1) * 128]

            scores = [jnp.where(valid, nt_dot(queries[k], part(2 * k)), LOW) for k in heads]
            old = [top[k * 32 : (k + 1) * 32, :] for k in heads]
            new = [jnp.maximum(old[k], jnp.max(scores[k], axis=1, keepdims=True)) for k in heads]
            weights = [
                jnp.where(valid, jnp.exp2((scores[k] - new[k]) * EXP2_SCALE), 0.0) for k in heads
            ]
            products = [nn_dot(weights[k].astype(BF), part(2 * k + 1)) for k in heads]
            for k in heads:
                rows = slice(k * 32, (k + 1) * 32)
                fade = jnp.exp2((old[k] - new[k]) * EXP2_SCALE)
                top[rows, :] = new[k]
                total[rows, :] = total[rows, :] * fade + jnp.sum(weights[k], axis=1, keepdims=True)
                acc[rows, :] = acc[rows, :] * fade + products[k]
            return inner

        lax.fori_loop(first_chunk[r], first_chunk[r + 1], one_chunk, 0)
        some = total[...] > 0.0
        divisor = jnp.where(some, total[...], 1.0)
        result = (acc[...] * (1.0 / divisor)).astype(BF)
        level = jnp.where(some, top[...] * SCALE + jnp.log(divisor), LOW)
        for t in range(TP):
            out[t, pl.ds(at, 16), :] = result[t * 16 : (t + 1) * 16]
            lse[t, pl.ds(at, 16), :] = level[t * 16 : (t + 1) * 16]
        return carry

    lax.fori_loop(0, 16, one_row, 0)

    def one_target(t, carry):
        out[t, 256:272, :] = stat_block(lse[t])
        return carry

    lax.fori_loop(0, TP, one_target, 0)


def paged_attention(first_chunk, slot_page, slot_live, where, q, cache):
    return pl.pallas_call(
        paged_kernel,
        in_specs=[smem()] * 4 + [vmem(), hbm()],
        out_specs=vmem(),
        out_shape=jax.ShapeDtypeStruct((TP, 256 + STAT_ROWS, 128), BF),
        scratch_shapes=[
            pltpu.VMEM((32, 128, 2048), BF),
            pltpu.VMEM((256, 128), F32),
            pltpu.VMEM((256, 128), F32),
            pltpu.VMEM((256, 128), F32),
            pltpu.VMEM((TP, 256, 128), F32),
            pltpu.SemaphoreType.DMA((32,)),
        ],
        compiler_params=params(58),
        cost_estimate=pl.CostEstimate(
            flops=2 * 10**9, bytes_accessed=12 * 2**20, transcendentals=2**20
        ),
        name="paged_attention",
    )(first_chunk, slot_page, slot_live, where, q, cache)


def fresh_groups(group, start, q, keys, values, token_row, out):
    span = token_row.shape[1]
    for i in range(ROLE):
        rows = pl.ds(pl.multiple_of(start[i] * PAGE_TOKENS, PAGE_TOKENS), span)
        row = lax.broadcasted_iota(jnp.int32, (256, 1), 0) // 16
        valid = token_row[i : i + 1, :] == row
        scores = jnp.where(valid, nt_dot(q[i], keys[rows, :]), LOW)
        top = jnp.maximum(jnp.max(scores, axis=1, keepdims=True), 0.5 * LOW)
        weights = jnp.exp2((scores - top) * EXP2_SCALE)
        total = jnp.sum(weights, axis=1, keepdims=True)
        acc = nn_dot(weights.astype(BF), values[rows, :])
        some = total > 0.0
        divisor = jnp.where(some, total, 1.0)
        target = group[i]
        out[target, :256, :] = (acc * (1.0 / divisor)).astype(BF)
        out[target, 256:272, :] = stat_block(
            jnp.where(some, top * SCALE + jnp.log(divisor), LOW)
        )


def prefill_kernel(q, keys, values, seg_row, out):
    rows = q.shape[0]
    for tile in range(rows // 256):
        high = (tile + 1) * 256
        low = max(0, (tile * 256 - 511) // 256 * 256)
        span = high - low
        seg_keys = seg_row[:, low:high]
        seg_queries = to_column(seg_row[:, tile * 256 : high])
        row = lax.broadcasted_iota(jnp.int32, (256, span), 0) + tile * 256
        column = lax.broadcasted_iota(jnp.int32, (256, span), 1) + low
        valid = (seg_keys == seg_queries) & (column <= row)
        for h in range(4):
            lanes = slice(h * 128, (h + 1) * 128)
            scores = nt_dot(q[tile * 256 : high, lanes], keys[low:high, :])
            scores = jnp.where(valid, scores, LOW)
            top = jnp.max(scores, axis=1, keepdims=True)
            weights = jnp.exp2((scores - top) * EXP2_SCALE)
            total = jnp.sum(weights, axis=1, keepdims=True)
            weights = (weights * (1.0 / total)).astype(BF)
            out[tile * 256 : high, lanes] = nn_dot(weights, values[low:high, :]).astype(BF)


def stat_columns(parts):
    rows = [stat_rows(parts[n, 256:272, :]) for n in range(parts.shape[0])]
    rows.append(jnp.zeros((128 - 2 * len(rows), 128), F32))
    columns = jnp.concatenate(rows, axis=0).T
    return [
        jnp.concatenate([columns[:, 2 * n : 2 * n + 1], columns[:, 2 * n + 1 : 2 * n + 2]], axis=0)
        for n in range(parts.shape[0])
    ]


def held_kernel(held, q, new_keys, new_values, out, top_out, total_out):
    row = lax.broadcasted_iota(jnp.int32, (256, 64), 0)
    key = lax.broadcasted_iota(jnp.int32, (256, 64), 1)
    valid = (row // 16 == key % 16) & (key // 16 <= row % 16 // 4)
    scores = jnp.where(valid, nt_dot(q[...], new_keys[...]) * SCALE, LOW)
    top = jnp.max(scores, axis=1, keepdims=True)
    levels = stat_columns(held)
    for level in levels:
        top = jnp.maximum(top, level)
    weights = jnp.where(valid, jnp.exp(scores - top), 0.0)
    total = jnp.sum(weights, axis=1, keepdims=True)
    acc = nn_dot(weights.astype(BF), new_values[...])
    for n, level in enumerate(levels):
        factor = jnp.exp(level - top)
        total = total + factor
        acc = acc + held[n, :256, :].astype(F32) * factor
    out[...] = acc
    top_out[...] = jnp.broadcast_to(top, top_out.shape)
    total_out[...] = jnp.broadcast_to(total, total_out.shape)


def merge_held(held, q, new_keys, new_values):
    state = jax.ShapeDtypeStruct((256, 128), F32)
    return pl.pallas_call(
        held_kernel,
        in_specs=[vmem()] * 4,
        out_specs=[vmem()] * 3,
        out_shape=[state] * 3,
        compiler_params=params(16),
        cost_estimate=pl.CostEstimate(
            flops=10**7, bytes_accessed=2 * 2**20, transcendentals=2**16
        ),
        name="merge_held_pages",
    )(held, q, new_keys, new_values)


def merge_kernel(fresh, held_acc, held_top, held_total, out):
    top = held_top[:, :1]
    levels = stat_columns(fresh)
    for level in levels:
        top = jnp.maximum(top, level)
    factor = jnp.exp(held_top[:, :1] - top)
    total = held_total[:, :1] * factor
    acc = held_acc[...] * factor
    for n, level in enumerate(levels):
        factor = jnp.exp(level - top)
        total = total + factor
        acc = acc + fresh[n, :256, :].astype(F32) * factor
    out[...] = (acc * (1.0 / total)).astype(BF)


def merge(fresh, state):
    return pl.pallas_call(
        merge_kernel,
        in_specs=[vmem()] * 4,
        out_specs=vmem(),
        out_shape=jax.ShapeDtypeStruct((256, 128), BF),
        compiler_params=params(16),
        cost_estimate=pl.CostEstimate(
            flops=10**7, bytes_accessed=2 * 2**20, transcendentals=2**16
        ),
        name="decode_merge",
    )(fresh, *state)


def page_tables(block_table, cache_len, ships, first_page):
    pages = 128
    page_ids = jnp.arange(pages, dtype=jnp.int32)
    rows, entries = block_table.shape
    code_of = (
        jnp.arange(rows, dtype=jnp.int32)[:, None] * entries
        + jnp.arange(entries, dtype=jnp.int32)[None, :]
    )
    match = block_table[None] == (first_page + page_ids)[:, None, None]
    code = jnp.max(jnp.where(match, code_of[None], -1), axis=(1, 2))
    replaced = jnp.any(ships.reshape(1, -1) == (first_page + page_ids)[:, None], axis=1)
    row = jnp.where(replaced | (code < 0), rows, code // entries)
    onehot = row[:, None] == jnp.arange(rows, dtype=jnp.int32)[None, :]
    length = jnp.sum(jnp.where(onehot, cache_len[None, :], 0), axis=1)
    live = jnp.clip(length - (code % entries) * PAGE_TOKENS, 0, PAGE_TOKENS)
    count = jnp.sum(onehot.astype(jnp.int32), axis=0)
    chunks = (count + 7) // 8
    ids17 = jnp.arange(rows + 1, dtype=jnp.int32)
    ids16 = jnp.arange(rows, dtype=jnp.int32)
    first_chunk = jnp.sum(
        jnp.where(ids16[None, :] < ids17[:, None], chunks[None, :], 0), axis=1
    )
    rank = jnp.sum(
        ((row[None, :] == row[:, None]) & (page_ids[None, :] < page_ids[:, None])).astype(jnp.int32),
        axis=1,
    )
    base = jnp.sum(jnp.where(onehot, first_chunk[None, :rows], 0), axis=1)
    slot = jnp.where(row < rows, base * 8 + rank, -1)
    hit = slot[None, :] == jnp.arange(256, dtype=jnp.int32)[:, None]
    slot_page = jnp.sum(jnp.where(hit, page_ids[None, :], 0), axis=1)
    slot_live = jnp.sum(jnp.where(hit, live[None, :], 0), axis=1)
    return first_chunk, slot_page, slot_live


def token_rows(tables, lengths, ship_page, group):
    rows, entries = tables.shape
    pages = ship_page.shape[0]
    window = pages // 2
    code_of = (
        jnp.arange(rows, dtype=jnp.int32)[:, None] * entries
        + jnp.arange(entries, dtype=jnp.int32)[None, :]
    )
    match = tables[None] == ship_page[:, None, None]
    code = jnp.max(jnp.where(match, code_of[None], -1), axis=(1, 2))
    row = jnp.where(code >= 0, code // entries, -1)
    onehot = row[:, None] == jnp.arange(rows, dtype=jnp.int32)[None, :]
    length = jnp.sum(jnp.where(onehot, lengths[None, :], 0), axis=1)
    live = jnp.clip(length - (code % entries) * PAGE_TOKENS, 0, PAGE_TOKENS)
    live = jnp.where(code >= 0, live, 0)
    page_ids = jnp.arange(pages, dtype=jnp.int32)
    ours = (ship_page // 2048)[None, :] == group[:, None]
    start = jnp.min(jnp.where(ours, page_ids[None, :], window), axis=1)
    start = jnp.minimum(start, window)
    packed = jnp.where(live > 0, row * 32 + live, 0)
    place = start[:, None] + jnp.arange(window, dtype=jnp.int32)[None, :]
    hit = place[:, :, None] == page_ids[None, None, :]
    here = jnp.sum(jnp.where(hit & ours[:, None, :], packed[None, None, :], 0), axis=2)
    token = jnp.arange(PAGE_TOKENS, dtype=jnp.int32)[None, None, :]
    token_row = jnp.where(token < (here % 32)[:, :, None], (here // 32 % 16)[:, :, None], -1)
    return start, token_row.reshape(ROLE, window * PAGE_TOKENS)


def phase(*arrays):
    return lax.optimization_barrier(arrays)


def per_device(
    text_embed,
    vision_rows,
    vision_group,
    vision_slot,
    request_blocks,
    ship_page,
    paged_cache,
    block_table,
    cache_len,
    step_embed,
    norm_gain,
    query_weight,
    keyvalue_weight,
):
    column = lax.axis_index("tp")
    role = lax.axis_index("role")
    core = column % 2
    group_rows, width = text_embed.shape
    steps, rows, _ = step_embed.shape

    role_id = role.reshape(1)

    def plus(a):
        return swap(a, "tp", CORE)

    other_weight = plus(keyvalue_weight)
    weights = (query_weight, keyvalue_weight, other_weight)
    (message,) = phase(pick_rows(vision_group, vision_slot, vision_rows))
    arrived = lax.all_to_all(message, "role", split_axis=0, concat_axis=0, tiled=True)
    merged, squares = land_rows(role_id, arrived, text_embed)
    text_all = lax.all_gather(merged, "tp")

    steps_all = jnp.stack(over_chips(step_embed.reshape(steps * rows, width)))
    meta = jnp.concatenate(
        [block_table.reshape(-1), cache_len, ship_page, jnp.zeros((48,), jnp.int32)]
    ).reshape(33, 128)
    metas = doubling(meta, "role", ROLE_MASKS[:1])
    steps_all, metas = phase(steps_all, metas)
    steps_all = more(steps_all, "tp", CORE)
    step_q, step_a, step_b = step_project(
        (column // 4) ^ jnp.arange(4, dtype=jnp.int32),
        (column % 4).reshape(1),
        steps_all,
        norm_gain,
        *weights,
    )
    new_keys = jnp.where(core == 0, step_a, step_b)
    new_values = jnp.where(core == 0, step_b, step_a)
    own_queries = (
        step_q.reshape(steps, rows, 4, HEAD_SIZE).transpose(1, 0, 2, 3).reshape(rows * 16, HEAD_SIZE)
    )
    metas = more(metas, "role", ROLE_MASKS[1])
    own_queries, metas, squares = phase(own_queries, metas, squares)

    queries = jnp.stack(over_chips(jnp.concatenate([own_queries, squares], axis=0)))
    queries_role = doubling(own_queries, "role", ROLE_MASKS[:1])
    metas = more(metas, "role", ROLE_MASKS[2])
    queries, queries_role, metas = phase(queries, queries_role, metas)

    query_all = more(queries, "tp", CORE)
    parts = jnp.sum(query_all[:, 256:280, :].astype(F32), axis=0)
    ssq = parts[0:8] + parts[8:16] + parts[16:24]
    queries_role = more(queries_role, "role", ROLE_MASKS[1])
    metas = metas.reshape(ROLE, -1)
    tables = metas[:, :4096].reshape(ROLE * rows, -1)
    lengths = metas[:, 4096 : 4096 + rows].reshape(-1)
    ships = metas[:, 4112 : 4112 + 64]
    role_order = role ^ jnp.array(ROLE_OFFSETS, jnp.int32)
    first_page = (role * TP + column) * 128
    first_chunk, slot_page, slot_live = page_tables(block_table, cache_len, ships, first_page)
    difference = column ^ jnp.arange(TP, dtype=jnp.int32)
    where = difference // 2 + 8 * (difference % 2)
    held = paged_attention(first_chunk, slot_page, slot_live, where, query_all, paged_cache)
    held, queries_role, tables = phase(held, queries_role, tables)

    held_parts = lax.all_to_all(held, "tp", split_axis=0, concat_axis=0, tiled=True)
    queries_role = more(queries_role, "role", ROLE_MASKS[2])
    start, token_row = token_rows(tables, lengths, ship_page, role_order)
    state = merge_held(held_parts, own_queries, new_keys, new_values)
    text_all, start, token_row, queries_role, ssq, *state = phase(
        text_all, start, token_row, queries_role, ssq, *state
    )

    keys, values, fresh = finish_keys(
        core.reshape(1),
        start,
        role_order,
        text_all,
        ssq,
        norm_gain,
        weights[1:],
        queries_role,
        token_row,
    )
    fresh_parts = lax.all_to_all(fresh, "role", split_axis=0, concat_axis=0, tiled=True)

    prefill_out = finish_queries(
        request_blocks, text_all, ssq, norm_gain, query_weight, keys, values
    )

    decode = merge(fresh_parts, state)
    decode_out = (
        decode.reshape(rows, steps, 4, HEAD_SIZE).transpose(1, 0, 2, 3).reshape(steps, rows, 512)
    )
    return (prefill_out, decode_out)


def solution(mesh):
    in_specs = (
        P("role", "tp"),
        P("role", "tp"),
        P("role"),
        P("role"),
        P("role", None),
        P("role"),
        P(("role", "tp"), None, None),
        P("role", None),
        P("role"),
        P(None, "role", "tp"),
        P(),
        P(None, "tp"),
        P(None, "tp"),
    )
    out_specs = (P("role", "tp"), P(None, "role", "tp"))
    return jax.shard_map(
        per_device, mesh=mesh, in_specs=in_specs, out_specs=out_specs, check_vma=False
    )
```

profile of v0, /device:TPU:10, one launch (start us, length us, event | category | flops | bytes accessed | tf_op | source)
XLA Modules:
  0.0 198.9 jit_solution(7226266850573929654)
XLA Ops:
  7.2 0.9 copy-done
  8.1 0.7 copy-done.1
  8.8 0.7 copy-done.2
  9.5 1.3 pick_rows.1
  10.8 8.1 %all-to-all-start = ((bf16[8,80,512]{2,1,0:T(8,128)(2,1)}), bf16[8,80,512]{2,1,0:T(8,128)(2,1)S(1)}, u32[]{:S(2)}, u32[]{:S(2)}) async-start(bf16[8,80,512]{2,1,0:T(8,128)(2,1)} %pick_rows.1), calls=%async_computation | async-start | bytes 1310720 | tf_op jit(solution)/shard_map/all_to_all | solution.py:710
  18.9 11.8 %all-to-all-done.arrived = bf16[8,80,512]{2,1,0:T(8,128)(2,1)S(1)} async-done(((bf16[8,80,512]{2,1,0:T(8,128)(2,1)}), bf16[8,80,512]{2,1,0:T(8,128)(2,1)S(1)}, u32[]{:S(2)}, u32[]{:S(2)}) %all-to-all-start) | async-done | bytes 655392 | tf_op jit(solution)/shard_map/all_to_all | solution.py:710
  30.8 1.9 land_rows.1
  32.7 1.1 collective-permute-start
  33.8 0.4 collective-permute-start.1
  34.3 2.0 %collective-permute-start.2 = (bf16[64,512]{1,0:T(8,128)(2,1)S(1)}, bf16[64,512]{1,0:T(8,128)(2,1)S(1)}, u32[]{:S(2)}, u32[]{:S(2)}) collective-permute-start(bf16[64,512]{1,0:T(8,128)(2,1)S(1)} %bitcast.66), channel_id=1, source_target_pairs={{0,6},{1,7},{2,4},{3,5},{4,2},{5,3},{6,0},{7,1},{8,14},{9,15},{10,... | collective-permute-start | bytes 196616 | tf_op jit(solution)/shard_map/ppermute | solution.py:43
  36.3 2.3 %collective-permute-start.3 = (bf16[64,512]{1,0:T(8,128)(2,1)S(1)}, bf16[64,512]{1,0:T(8,128)(2,1)S(1)}, u32[]{:S(2)}, u32[]{:S(2)}) collective-permute-start(bf16[64,512]{1,0:T(8,128)(2,1)S(1)} %bitcast.67), channel_id=1, source_target_pairs={{0,8},{1,9},{2,10},{3,11},{4,12},{5,13},{6,14},{7,15},{8,0},{9,1},... | collective-permute-start | bytes 196616 | tf_op jit(solution)/shard_map/ppermute | solution.py:43
  38.7 0.6 collective-permute-start.7
  39.7 2.6 %select_reduce_fusion.1 = s32[128]{0:T(128)S(1)} fusion(s32[16,256]{1,0:T(8,128)S(1)} %iota_add_fusion.1, s32[16,256]{1,0:T(8,128)S(1)} %copy-done.8, s32[128]{0:T(128)S(1)} %iota_add_fusion.3), kind=kLoop, calls=%fused_computation.1 | loop fusion | flops 1572736 | bytes 33792 | tf_op jit(solution)/shard_map/reduce_max | solution.py:624
  42.5 0.5 fusion.8.where
  43.0 1.1 collective-permute-done.7
  44.1 1.7 collective-permute-start.4
  45.9 1.8 collective-permute-start.5
  47.7 0.8 collective-permute-start.6
  48.6 3.5 %collective-permute-done.4 = bf16[64,512]{1,0:T(8,128)(2,1)S(1)} collective-permute-done((bf16[64,512]{1,0:T(8,128)(2,1)S(1)}, bf16[64,512]{1,0:T(8,128)(2,1)S(1)}, u32[]{:S(2)}, u32[]{:S(2)}) %collective-permute-start.4) | collective-permute-done | bytes 65568 | tf_op jit(solution)/shard_map/ppermute | solution.py:43
  52.1 0.9 collective-permute-done.5
  53.0 3.1 %collective-permute-done.6 = bf16[64,512]{1,0:T(8,128)(2,1)S(1)} collective-permute-done((bf16[64,512]{1,0:T(8,128)(2,1)S(1)}, bf16[64,512]{1,0:T(8,128)(2,1)S(1)}, u32[]{:S(2)}, u32[]{:S(2)}) %collective-permute-start.6) | collective-permute-done | bytes 65568 | tf_op jit(solution)/shard_map/ppermute | solution.py:43
  56.2 1.4 collective-permute-start.10
  57.6 0.6 iota_xor_fusion.order
  58.2 0.6 reshape.368.gain
  58.8 0.6 reshape.369.gain
  59.5 0.7 collective-permute-done.10
  60.3 1.1 pad_maximum_fusion.xs
  61.4 1.3 copy-done.5
  62.7 9.0 %step_project.1 = (bf16[64,512]{1,0:T(8,128)(2,1)}, bf16[64,128]{1,0:T(8,128)(2,1)}, bf16[64,128]{1,0:T(8,128)(2,1)}) custom-call(s32[4]{0:T(128)} %iota_xor_fusion.order, s32[1]{0:T(128)} %bitcast.4.low, bf16[16,64,512]{2,1,0:T(8,128)(2,1)} %pad_maximum_fusion.xs, bf16[4,4,1,512]{3,2,1,0:T(2,128)(2,1)} %reshape.368.gain, bf16[8192,512]{1,0:T(8,128)(2,1)} %weight.1, ...), custom_call_target="tpu_custom_call" | custom-call | flops 805306368 | bytes 14680064 | tf_op jit(solution)/shard_map/step_project/pallas_call | solution.py:244
  71.7 0.9 reshape.359
  72.7 1.1 collective-permute-start.11
  73.8 2.4 %collective-permute-start.13 = (bf16[288,128]{1,0:T(8,128)(2,1)S(1)}, bf16[288,128]{1,0:T(8,128)(2,1)S(1)}, u32[]{:S(2)}, u32[]{:S(2)}) collective-permute-start(bf16[288,128]{1,0:T(8,128)(2,1)S(1)} %constant_dynamic-update-slice_fusion), channel_id=1, source_target_pairs={{0,6},{1,7},{2,4},{3,5},{4,2},{5,3},{6,0},{7,1},{8,14},{9,15},{10,... | collective-permute-start | bytes 221192 | tf_op jit(solution)/shard_map/ppermute | solution.py:43
  76.2 0.5 collective-permute-start.14
  76.7 2.0 %collective-permute-start.18 = (bf16[1,256,128]{2,1,0:T(8,128)(2,1)S(1)}, bf16[1,256,128]{2,1,0:T(8,128)(2,1)S(1)}, u32[]{:S(2)}, u32[]{:S(2)}) collective-permute-start(bf16[1,256,128]{2,1,0:T(8,128)(2,1)S(1)} %bitcast.54), channel_id=1, source_target_pairs={{0,64},{16,80},{32,96},{48,112},{64,0},{80,16},{96,32},{112,48},{1... | collective-permute-start | bytes 196616 | tf_op jit(solution)/shard_map/ppermute | solution.py:43
  78.7 0.7 broadcast_select_fusion
  79.5 3.4 %collective-permute-done.18 = bf16[1,256,128]{2,1,0:T(8,128)(2,1)S(1)} collective-permute-done((bf16[1,256,128]{2,1,0:T(8,128)(2,1)S(1)}, bf16[1,256,128]{2,1,0:T(8,128)(2,1)S(1)}, u32[]{:S(2)}, u32[]{:S(2)}) %collective-permute-start.18) | collective-permute-done | bytes 65568 | tf_op jit(solution)/shard_map/ppermute | solution.py:43
  82.9 4.3 %collective-permute-done.19 = s32[4,33,128]{2,0,1:T(4,128)S(1)} collective-permute-done((s32[4,33,128]{2,0,1:T(4,128)S(1)}, s32[4,33,128]{2,0,1:T(4,128)S(1)}, u32[]{:S(2)}, u32[]{:S(2)}) %collective-permute-start.19) | collective-permute-done | bytes 67616 | tf_op jit(solution)/shard_map/ppermute | solution.py:43
  87.1 4.7 %collective-permute-start.15 = (bf16[288,128]{1,0:T(8,128)(2,1)S(1)}, bf16[288,128]{1,0:T(8,128)(2,1)S(1)}, u32[]{:S(2)}, u32[]{:S(2)}) collective-permute-start(bf16[288,128]{1,0:T(8,128)(2,1)S(1)} %constant_dynamic-update-slice_fusion), channel_id=1, source_target_pairs={{0,10},{1,11},{2,8},{3,9},{4,14},{5,15},{6,12},{7,13},{8,2},{9,3},... | collective-permute-start | bytes 221192 | tf_op jit(solution)/shard_map/ppermute | solution.py:43
  91.9 1.3 collective-permute-start.16
  93.2 1.7 collective-permute-start.17
  95.0 0.8 collective-permute-done.15
  95.7 2.9 %collective-permute-done.16 = bf16[288,128]{1,0:T(8,128)(2,1)S(1)} collective-permute-done((bf16[288,128]{1,0:T(8,128)(2,1)S(1)}, bf16[288,128]{1,0:T(8,128)(2,1)S(1)}, u32[]{:S(2)}, u32[]{:S(2)}) %collective-permute-start.16) | collective-permute-done | bytes 73760 | tf_op jit(solution)/shard_map/ppermute | solution.py:43
  98.7 3.1 %collective-permute-done.17 = bf16[288,128]{1,0:T(8,128)(2,1)S(1)} collective-permute-done((bf16[288,128]{1,0:T(8,128)(2,1)S(1)}, bf16[288,128]{1,0:T(8,128)(2,1)S(1)}, u32[]{:S(2)}, u32[]{:S(2)}) %collective-permute-start.17) | collective-permute-done | bytes 73760 | tf_op jit(solution)/shard_map/ppermute | solution.py:43
  101.8 2.5 %collective-permute-start.21 = (bf16[2,256,128]{2,1,0:T(8,128)(2,1)S(1)}, bf16[2,256,128]{2,1,0:T(8,128)(2,1)S(1)}, u32[]{:S(2)}, u32[]{:S(2)}) collective-permute-start(bf16[2,256,128]{2,1,0:T(8,128)(2,1)S(1)} %pad_maximum_fusion.3), channel_id=1, source_target_pairs={{0,16},{16,0},{32,48},{48,32},{64,80},{80,64},{96,112},{112,96},{1... | collective-permute-start | bytes 393224 | tf_op jit(solution)/shard_map/ppermute | solution.py:43
  105.1 0.7 select_reduce_fusion.3
  106.0 1.2 collective-permute-done.21
  107.4 1.0 copy-done.4
  108.4 16.3 %paged_attention.1 = bf16[16,272,128]{2,1,0:T(8,128)(2,1)} custom-call(s32[17]{0:T(128)} %copy-done.11, s32[256]{0:T(256)} %get-tuple-element.63.slot_page, s32[256]{0:T(256)} %get-tuple-element.62.slot_live, s32[16]{0:T(128)} %fusion.8.where, bf16[16,288,128]{2,1,0:T(8,128)(2,1)} %copy-done.4, bf16[128,16,2048]{2,1,0:T(8,128)(2,1)} %cache.1), custom_call_target="tpu_custom_call" | custom-call | flops 2000000000 | bytes 12582912 | tf_op jit(solution)/shard_map/paged_attention/pallas_call | solution.py:477
  124.6 4.7 %all-to-all-start.1 = ((bf16[16,272,128]{2,1,0:T(8,128)(2,1)}), bf16[16,272,128]{2,1,0:T(8,128)(2,1)S(1)}, u32[]{:S(2)}, u32[]{:S(2)}) async-start(bf16[16,272,128]{2,1,0:T(8,128)(2,1)} %paged_attention.1), calls=%async_computation.1 | async-start | bytes 2228224 | tf_op jit(solution)/shard_map/all_to_all | solution.py:757
  129.3 0.9 collective-permute-start.22
  130.1 1.8 select_reduce_fusion
  132.1 0.3 select_reduce_fusion.2
  132.4 0.9 convert_reduce_fusion
  133.4 0.6 slice_add_fusion.ssq
  134.4 0.6 compare_select_fusion.token_row
  135.0 2.7 %collective-permute-done.22 = bf16[4,256,128]{2,1,0:T(8,128)(2,1)S(1)} collective-permute-done((bf16[4,256,128]{2,1,0:T(8,128)(2,1)S(1)}, bf16[4,256,128]{2,1,0:T(8,128)(2,1)S(1)}, u32[]{:S(2)}, u32[]{:S(2)}) %collective-permute-start.22) | collective-permute-done | bytes 262176 | tf_op jit(solution)/shard_map/ppermute | solution.py:43
  137.6 0.9 pad_maximum_fusion.1.q
  138.5 5.9 %all-to-all-done.1.held = bf16[16,272,128]{2,1,0:T(8,128)(2,1)S(1)} async-done(((bf16[16,272,128]{2,1,0:T(8,128)(2,1)}), bf16[16,272,128]{2,1,0:T(8,128)(2,1)S(1)}, u32[]{:S(2)}, u32[]{:S(2)}) %all-to-all-start.1) | async-done | bytes 1114144 | tf_op jit(solution)/shard_map/all_to_all | solution.py:757
  144.4 3.4 %merge_held_pages.1 = (f32[256,128]{1,0:T(8,128)S(1)}, f32[256,128]{1,0:T(8,128)S(1)}, f32[256,128]{1,0:T(8,128)S(1)}) custom-call(bf16[16,272,128]{2,1,0:T(8,128)(2,1)S(1)} %all-to-all-done.1.held, bf16[256,128]{1,0:T(8,128)(2,1)S(1)} %bitcast.56, bf16[64,128]{1,0:T(8,128)(2,1)S(1)} %get-tuple-element.67.new_keys, ...), custom_call_target="tpu_custom_call" | custom-call | flops 10000000 | bytes 2097152 | tf_op jit(solution)/shard_map/merge_held_pages/pallas_call | solution.py:573
  147.8 13.7 %keys_and_fresh_pages.1 = (bf16[1024,128]{1,0:T(8,128)(2,1)}, bf16[1024,128]{1,0:T(8,128)(2,1)}, bf16[8,272,128]{2,1,0:T(8,128)(2,1)}) custom-call(s32[1]{0:T(128)} %bitcast.26.core, s32[8]{0:T(128)} %copy-done.12, s32[8]{0:T(128)} %copy-done.13, bf16[16,1024,512]{2,1,0:T(8,128)(2,1)} %bitcast.74, f32[8,128]{1,0:T(8,128)} %slice_add_fusion.ssq, ...), custom_call_target="tpu_custom_call" | custom-call | flops 6000000000 | bytes 20971520 | tf_op jit(solution)/shard_map/keys_and_fresh_pages/pallas_call | solution.py:350
  161.5 6.5 %all-to-all-start.2 = ((bf16[8,272,128]{2,1,0:T(8,128)(2,1)}), bf16[8,272,128]{2,1,0:T(8,128)(2,1)S(1)}, u32[]{:S(2)}, u32[]{:S(2)}) async-start(bf16[8,272,128]{2,1,0:T(8,128)(2,1)} %get-tuple-element.58), calls=%async_computation.2 | async-start | bytes 1114112 | tf_op jit(solution)/shard_map/all_to_all | solution.py:776
  168.0 21.7 %queries_and_prefill.1 = bf16[1024,512]{1,0:T(8,128)(2,1)} custom-call(s32[1,8]{1,0:T(1,128)} %blocks_ref.1, bf16[16,1024,512]{2,1,0:T(8,128)(2,1)} %bitcast.75, f32[8,128]{1,0:T(8,128)} %slice_add_fusion.ssq, bf16[16,1,512]{2,1,0:T(2,128)(2,1)} %reshape.369.gain, bf16[8192,512]{1,0:T(8,128)(2,1)} %weight.1, bf16[1024,128]{1,0:T(8,128)(2,1)} %get-tuple-element.56.keys, ...), custom_call_target="tpu_custom_call" | custom-call | flops 12000000000 | bytes 26214400 | tf_op jit(solution)/shard_map/queries_and_prefill/pallas_call | solution.py:390
  189.7 1.7 decode_merge.1
  191.4 0.6 copy.28
  (111 shorter events, 3.0 us)
Async XLA Ops:
  7.2 1.0 copy-start
  8.1 0.7 copy-start.1
  8.8 0.7 copy-start.2
  9.5 21.3 %copy-start.3 = (bf16[1024,512]{1,0:T(8,128)(2,1)S(1)}, bf16[1024,512]{1,0:T(8,128)(2,1)}, u32[]{:S(2)}) copy-start(bf16[1024,512]{1,0:T(8,128)(2,1)} %text.1) | copy-start | bytes 3145732
  10.8 20.0 %all-to-all-start = ((bf16[8,80,512]{2,1,0:T(8,128)(2,1)}), bf16[8,80,512]{2,1,0:T(8,128)(2,1)S(1)}, u32[]{:S(2)}, u32[]{:S(2)}) async-start(bf16[8,80,512]{2,1,0:T(8,128)(2,1)} %pick_rows.1), calls=%async_computation | async-start | bytes 1310720 | tf_op jit(solution)/shard_map/all_to_all | solution.py:710
  18.9 128.9 %all-gather.3.cloned.1.call-start = ((), (), s32[]{:S(2)}) async-start(), calls=%async_computation.3 | async-start | bytes 17825792 | tf_op jit(solution)/shard_map/all_gather | solution.py:712
  30.7 2.0 copy-start.7
  30.7 7.8 %copy-start.8 = (s32[16,256]{1,0:T(8,128)S(1)}, s32[16,256]{1,0:T(8,128)}, u32[]{:S(2)}) copy-start(s32[16,256]{1,0:T(8,128)} %param.21) | copy-start | bytes 49156
  30.7 7.9 %copy-start.9 = (s32[64]{0:T(128)S(1)}, s32[64]{0:T(128)}, u32[]{:S(2)}) copy-start(s32[64]{0:T(128)} %param.19) | copy-start | bytes 772
  30.7 7.9 %copy-start.10 = (s32[16]{0:T(128)S(1)}, s32[16]{0:T(128)}, u32[]{:S(2)}) copy-start(s32[16]{0:T(128)} %param.22) | copy-start | bytes 196
  30.8 8.6 %copy-start.14 = (s32[8]{0:T(128)S(1)}, s32[8]{0:T(128)}, u32[]{:S(2)}) copy-start(s32[8]{0:T(128)} %constant.186.clone) | copy-start | bytes 100
  32.7 25.5 %copy-start.6 = (bf16[8192]{0:T(1024)(128)(2,1)S(1)}, bf16[8192]{0:T(1024)(128)(2,1)}, u32[]{:S(2)}) copy-start(bf16[8192]{0:T(1024)(128)(2,1)} %param.24) | copy-start | bytes 49156
  32.7 13.1 %collective-permute-start = (bf16[64,512]{1,0:T(8,128)(2,1)S(1)}, bf16[64,512]{1,0:T(8,128)(2,1)S(1)}, u32[]{:S(2)}, u32[]{:S(2)}) collective-permute-start(bf16[64,512]{1,0:T(8,128)(2,1)S(1)} %bitcast.64), channel_id=1, source_target_pairs={{0,2},{1,3},{2,0},{3,1},{4,6},{5,7},{6,4},{7,5},{8,10},{9,11},{10,... | collective-permute-start | bytes 196616 | tf_op jit(solution)/shard_map/ppermute | solution.py:43
  33.8 12.1 %collective-permute-start.1 = (bf16[64,512]{1,0:T(8,128)(2,1)S(1)}, bf16[64,512]{1,0:T(8,128)(2,1)S(1)}, u32[]{:S(2)}, u32[]{:S(2)}) collective-permute-start(bf16[64,512]{1,0:T(8,128)(2,1)S(1)} %bitcast.65), channel_id=1, source_target_pairs={{0,4},{1,5},{2,6},{3,7},{4,0},{5,1},{6,2},{7,3},{8,12},{9,13},{10,... | collective-permute-start | bytes 196616 | tf_op jit(solution)/shard_map/ppermute | solution.py:43
  34.3 13.5 %collective-permute-start.2 = (bf16[64,512]{1,0:T(8,128)(2,1)S(1)}, bf16[64,512]{1,0:T(8,128)(2,1)S(1)}, u32[]{:S(2)}, u32[]{:S(2)}) collective-permute-start(bf16[64,512]{1,0:T(8,128)(2,1)S(1)} %bitcast.66), channel_id=1, source_target_pairs={{0,6},{1,7},{2,4},{3,5},{4,2},{5,3},{6,0},{7,1},{8,14},{9,15},{10,... | collective-permute-start | bytes 196616 | tf_op jit(solution)/shard_map/ppermute | solution.py:43
  36.3 12.3 %collective-permute-start.3 = (bf16[64,512]{1,0:T(8,128)(2,1)S(1)}, bf16[64,512]{1,0:T(8,128)(2,1)S(1)}, u32[]{:S(2)}, u32[]{:S(2)}) collective-permute-start(bf16[64,512]{1,0:T(8,128)(2,1)S(1)} %bitcast.67), channel_id=1, source_target_pairs={{0,8},{1,9},{2,10},{3,11},{4,12},{5,13},{6,14},{7,15},{8,0},{9,1},... | collective-permute-start | bytes 196616 | tf_op jit(solution)/shard_map/ppermute | solution.py:43
  38.7 5.3 %collective-permute-start.7 = (s32[1,33,128]{2,0,1:T(1,128)S(1)}, s32[1,33,128]{2,0,1:T(1,128)S(1)}, u32[]{:S(2)}, u32[]{:S(2)}) collective-permute-start(s32[1,33,128]{2,0,1:T(1,128)S(1)} %broadcast_in_dim_reshape.4), channel_id=1, source_target_pairs={{0,64},{16,80},{32,96},{48,112},{64,0},{80,16},{96,32},{112,48},{1... | collective-permute-start | bytes 50696 | tf_op jit(solution)/shard_map/ppermute | solution.py:43
  39.4 32.3 %copy-start.13 = (s32[8]{0:T(128)}, s32[8]{0:T(128)S(1)}, u32[]{:S(2)}) copy-start(s32[8]{0:T(128)S(1)} %broadcast_xor_fusion.group) | copy-start | bytes 100
  42.3 29.4 %copy-start.12 = (s32[8]{0:T(128)}, s32[8]{0:T(128)S(1)}, u32[]{:S(2)}) copy-start(s32[8]{0:T(128)S(1)} %broadcast_minimum_fusion.start) | copy-start | bytes 100
  44.1 8.0 %collective-permute-start.4 = (bf16[64,512]{1,0:T(8,128)(2,1)S(1)}, bf16[64,512]{1,0:T(8,128)(2,1)S(1)}, u32[]{:S(2)}, u32[]{:S(2)}) collective-permute-start(bf16[64,512]{1,0:T(8,128)(2,1)S(1)} %bitcast.69), channel_id=1, source_target_pairs={{0,10},{1,11},{2,8},{3,9},{4,14},{5,15},{6,12},{7,13},{8,2},{9,3},... | collective-permute-start | bytes 196616 | tf_op jit(solution)/shard_map/ppermute | solution.py:43
  45.8 15.5 %collective-permute-start.9 = (bf16[8192,128]{1,0:T(8,128)(2,1)}, bf16[8192,128]{1,0:T(8,128)(2,1)S(1)}, u32[]{:S(2)}, u32[]{:S(2)}) collective-permute-start(bf16[8192,128]{1,0:T(8,128)(2,1)} %wa.3), channel_id=1, source_target_pairs={{0,1},{1,0},{2,3},{3,2},{4,5},{5,4},{6,7},{7,6},{8,9},{9,8},{10,11... | collective-permute-start | bytes 6291464 | tf_op jit(solution)/shard_map/ppermute | solution.py:43
  45.9 7.1 %collective-permute-start.5 = (bf16[64,512]{1,0:T(8,128)(2,1)S(1)}, bf16[64,512]{1,0:T(8,128)(2,1)S(1)}, u32[]{:S(2)}, u32[]{:S(2)}) collective-permute-start(bf16[64,512]{1,0:T(8,128)(2,1)S(1)} %bitcast.70), channel_id=1, source_target_pairs={{0,12},{1,13},{2,14},{3,15},{4,8},{5,9},{6,10},{7,11},{8,4},{9,5},... | collective-permute-start | bytes 196616 | tf_op jit(solution)/shard_map/ppermute | solution.py:43
  47.7 8.4 %collective-permute-start.6 = (bf16[64,512]{1,0:T(8,128)(2,1)S(1)}, bf16[64,512]{1,0:T(8,128)(2,1)S(1)}, u32[]{:S(2)}, u32[]{:S(2)}) collective-permute-start(bf16[64,512]{1,0:T(8,128)(2,1)S(1)} %bitcast.71), channel_id=1, source_target_pairs={{0,14},{1,15},{2,12},{3,13},{4,10},{5,11},{6,8},{7,9},{8,6},{9,7},... | collective-permute-start | bytes 196616 | tf_op jit(solution)/shard_map/ppermute | solution.py:43
  56.1 4.1 %collective-permute-start.8 = (bf16[8,64,512]{2,1,0:T(8,128)(2,1)S(1)}, bf16[8,64,512]{2,1,0:T(8,128)(2,1)S(1)}, u32[]{:S(2)}, u32[]{:S(2)}) collective-permute-start(bf16[8,64,512]{2,1,0:T(8,128)(2,1)S(1)} %bitcast_dynamic-update-slice_fusion.8), channel_id=1, source_target_pairs={{0,1},{1,0},{2,3},{3,2},{4,5},{5,4},{6,7},{7,6},{8,9},{9,8},{10,11... | collective-permute-start | bytes 1572872 | tf_op jit(solution)/shard_map/ppermute | solution.py:43
  56.2 4.0 %collective-permute-start.10 = (s32[2,33,128]{2,0,1:T(2,128)S(1)}, s32[2,33,128]{2,0,1:T(2,128)S(1)}, u32[]{:S(2)}, u32[]{:S(2)}) collective-permute-start(s32[2,33,128]{2,0,1:T(2,128)S(1)} %pad_add_fusion.2), channel_id=1, source_target_pairs={{0,16},{16,0},{32,48},{48,32},{64,80},{80,64},{96,112},{112,96},{1... | collective-permute-start | bytes 101384 | tf_op jit(solution)/shard_map/ppermute | solution.py:43
  61.4 1.3 copy-start.5
  72.7 19.2 %collective-permute-start.11 = (bf16[288,128]{1,0:T(8,128)(2,1)S(1)}, bf16[288,128]{1,0:T(8,128)(2,1)S(1)}, u32[]{:S(2)}, u32[]{:S(2)}) collective-permute-start(bf16[288,128]{1,0:T(8,128)(2,1)S(1)} %constant_dynamic-update-slice_fusion), channel_id=1, source_target_pairs={{0,2},{1,3},{2,0},{3,1},{4,6},{5,7},{6,4},{7,5},{8,10},{9,11},{10,... | collective-permute-start | bytes 221192 | tf_op jit(solution)/shard_map/ppermute | solution.py:43
  73.8 19.4 %collective-permute-start.12 = (bf16[288,128]{1,0:T(8,128)(2,1)S(1)}, bf16[288,128]{1,0:T(8,128)(2,1)S(1)}, u32[]{:S(2)}, u32[]{:S(2)}) collective-permute-start(bf16[288,128]{1,0:T(8,128)(2,1)S(1)} %constant_dynamic-update-slice_fusion), channel_id=1, source_target_pairs={{0,4},{1,5},{2,6},{3,7},{4,0},{5,1},{6,2},{7,3},{8,12},{9,13},{10,... | collective-permute-start | bytes 221192 | tf_op jit(solution)/shard_map/ppermute | solution.py:43
  73.8 21.1 %collective-permute-start.13 = (bf16[288,128]{1,0:T(8,128)(2,1)S(1)}, bf16[288,128]{1,0:T(8,128)(2,1)S(1)}, u32[]{:S(2)}, u32[]{:S(2)}) collective-permute-start(bf16[288,128]{1,0:T(8,128)(2,1)S(1)} %constant_dynamic-update-slice_fusion), channel_id=1, source_target_pairs={{0,6},{1,7},{2,4},{3,5},{4,2},{5,3},{6,0},{7,1},{8,14},{9,15},{10,... | collective-permute-start | bytes 221192 | tf_op jit(solution)/shard_map/ppermute | solution.py:43
  76.2 18.7 %collective-permute-start.14 = (bf16[288,128]{1,0:T(8,128)(2,1)S(1)}, bf16[288,128]{1,0:T(8,128)(2,1)S(1)}, u32[]{:S(2)}, u32[]{:S(2)}) collective-permute-start(bf16[288,128]{1,0:T(8,128)(2,1)S(1)} %constant_dynamic-update-slice_fusion), channel_id=1, source_target_pairs={{0,8},{1,9},{2,10},{3,11},{4,12},{5,13},{6,14},{7,15},{8,0},{9,1},... | collective-permute-start | bytes 221192 | tf_op jit(solution)/shard_map/ppermute | solution.py:43
  76.7 6.1 %collective-permute-start.18 = (bf16[1,256,128]{2,1,0:T(8,128)(2,1)S(1)}, bf16[1,256,128]{2,1,0:T(8,128)(2,1)S(1)}, u32[]{:S(2)}, u32[]{:S(2)}) collective-permute-start(bf16[1,256,128]{2,1,0:T(8,128)(2,1)S(1)} %bitcast.54), channel_id=1, source_target_pairs={{0,64},{16,80},{32,96},{48,112},{64,0},{80,16},{96,32},{112,48},{1... | collective-permute-start | bytes 196616 | tf_op jit(solution)/shard_map/ppermute | solution.py:43
  82.8 4.3 %collective-permute-start.19 = (s32[4,33,128]{2,0,1:T(4,128)S(1)}, s32[4,33,128]{2,0,1:T(4,128)S(1)}, u32[]{:S(2)}, u32[]{:S(2)}) collective-permute-start(s32[4,33,128]{2,0,1:T(4,128)S(1)} %pad_add_fusion.1), channel_id=1, source_target_pairs={{0,48},{16,32},{32,16},{48,0},{64,112},{80,96},{96,80},{112,64},{1... | collective-permute-start | bytes 202760 | tf_op jit(solution)/shard_map/ppermute | solution.py:43
  87.1 8.6 %collective-permute-start.15 = (bf16[288,128]{1,0:T(8,128)(2,1)S(1)}, bf16[288,128]{1,0:T(8,128)(2,1)S(1)}, u32[]{:S(2)}, u32[]{:S(2)}) collective-permute-start(bf16[288,128]{1,0:T(8,128)(2,1)S(1)} %constant_dynamic-update-slice_fusion), channel_id=1, source_target_pairs={{0,10},{1,11},{2,8},{3,9},{4,14},{5,15},{6,12},{7,13},{8,2},{9,3},... | collective-permute-start | bytes 221192 | tf_op jit(solution)/shard_map/ppermute | solution.py:43
  91.9 6.8 %collective-permute-start.16 = (bf16[288,128]{1,0:T(8,128)(2,1)S(1)}, bf16[288,128]{1,0:T(8,128)(2,1)S(1)}, u32[]{:S(2)}, u32[]{:S(2)}) collective-permute-start(bf16[288,128]{1,0:T(8,128)(2,1)S(1)} %constant_dynamic-update-slice_fusion), channel_id=1, source_target_pairs={{0,12},{1,13},{2,14},{3,15},{4,8},{5,9},{6,10},{7,11},{8,4},{9,5},... | collective-permute-start | bytes 221192 | tf_op jit(solution)/shard_map/ppermute | solution.py:43
  93.2 8.6 %collective-permute-start.17 = (bf16[288,128]{1,0:T(8,128)(2,1)S(1)}, bf16[288,128]{1,0:T(8,128)(2,1)S(1)}, u32[]{:S(2)}, u32[]{:S(2)}) collective-permute-start(bf16[288,128]{1,0:T(8,128)(2,1)S(1)} %constant_dynamic-update-slice_fusion), channel_id=1, source_target_pairs={{0,14},{1,15},{2,12},{3,13},{4,10},{5,11},{6,8},{7,9},{8,6},{9,7},... | collective-permute-start | bytes 221192 | tf_op jit(solution)/shard_map/ppermute | solution.py:43
  101.8 5.4 %collective-permute-start.21 = (bf16[2,256,128]{2,1,0:T(8,128)(2,1)S(1)}, bf16[2,256,128]{2,1,0:T(8,128)(2,1)S(1)}, u32[]{:S(2)}, u32[]{:S(2)}) collective-permute-start(bf16[2,256,128]{2,1,0:T(8,128)(2,1)S(1)} %pad_maximum_fusion.3), channel_id=1, source_target_pairs={{0,16},{16,0},{32,48},{48,32},{64,80},{80,64},{96,112},{112,96},{1... | collective-permute-start | bytes 393224 | tf_op jit(solution)/shard_map/ppermute | solution.py:43
  104.3 3.0 %collective-permute-start.20 = (bf16[8,288,128]{2,1,0:T(8,128)(2,1)S(1)}, bf16[8,288,128]{2,1,0:T(8,128)(2,1)S(1)}, u32[]{:S(2)}, u32[]{:S(2)}) collective-permute-start(bf16[8,288,128]{2,1,0:T(8,128)(2,1)S(1)} %bitcast_dynamic-update-slice_fusion), channel_id=1, source_target_pairs={{0,1},{1,0},{2,3},{3,2},{4,5},{5,4},{6,7},{7,6},{8,9},{9,8},{10,11... | collective-permute-start | bytes 1769480 | tf_op jit(solution)/shard_map/ppermute | solution.py:43
  104.8 2.5 %copy-start.11 = (s32[17]{0:T(128)}, s32[17]{0:T(128)S(1)}, u32[]{:S(2)}) copy-start(s32[17]{0:T(128)S(1)} %select_reduce_fusion.8.first_chunk) | copy-start | bytes 208
  107.3 1.0 copy-start.4
  124.6 19.7 %all-to-all-start.1 = ((bf16[16,272,128]{2,1,0:T(8,128)(2,1)}), bf16[16,272,128]{2,1,0:T(8,128)(2,1)S(1)}, u32[]{:S(2)}, u32[]{:S(2)}) async-start(bf16[16,272,128]{2,1,0:T(8,128)(2,1)} %paged_attention.1), calls=%async_computation.1 | async-start | bytes 2228224 | tf_op jit(solution)/shard_map/all_to_all | solution.py:757
  129.3 8.4 %collective-permute-start.22 = (bf16[4,256,128]{2,1,0:T(8,128)(2,1)S(1)}, bf16[4,256,128]{2,1,0:T(8,128)(2,1)S(1)}, u32[]{:S(2)}, u32[]{:S(2)}) collective-permute-start(bf16[4,256,128]{2,1,0:T(8,128)(2,1)S(1)} %pad_maximum_fusion.2), channel_id=1, source_target_pairs={{0,48},{16,32},{32,16},{48,0},{64,112},{80,96},{96,80},{112,64},{1... | collective-permute-start | bytes 786440 | tf_op jit(solution)/shard_map/ppermute | solution.py:43
  161.5 28.2 %all-to-all-start.2 = ((bf16[8,272,128]{2,1,0:T(8,128)(2,1)}), bf16[8,272,128]{2,1,0:T(8,128)(2,1)S(1)}, u32[]{:S(2)}, u32[]{:S(2)}) async-start(bf16[8,272,128]{2,1,0:T(8,128)(2,1)} %get-tuple-element.58), calls=%async_computation.2 | async-start | bytes 1114112 | tf_op jit(solution)/shard_map/all_to_all | solution.py:776
Sparse Core Ops, SparseCore 0:
  32.8 100.0 all-gather.2
where the time goes:
time: 201 us; the launch traced here: 199 us
  Pallas kernels  69 us (34%)
  starting transfers between devices  48.6 us (24%)
  waiting for transfers between devices  45.3 us (23%)
  between operations  14.5 us (7%)
  other arithmetic  12.8 us (6%)
  local copies, waits for them, and re-layouts  8.65 us (4%)
    ppermute x23, starting transfers between devices, swap(): return lax.ppermute(x, axis, [(i, i ^ mask) for i in range(size)])  29.4 us
    ppermute x23, waiting for transfers between devices, swap(): return lax.ppermute(x, axis, [(i, i ^ mask) for i in range(size)])  27.6 us
    pallas_call x1, Pallas kernels, finish_queries(): pl.pallas_call(queries_kernel, in_specs=[smem(), hbm()] + [vmem()] * 2 +...  21.7 us
    pallas_call x1, Pallas kernels, paged_attention(): pl.pallas_call(paged_kernel, in_specs=[smem()] * 4 + [vmem(), hbm()], out...  16.3 us
    pallas_call x1, Pallas kernels, finish_keys(): pl.pallas_call(keys_kernel, in_specs=[smem()] * 3 + [hbm()] + [vmem()] *...  13.7 us
    all_to_all x1, waiting for transfers between devices, per_device(): lax.all_to_all(message, 'role', split_axis=0, concat_axis=0, tiled=True)  11.8 us
    pallas_call x1, Pallas kernels, step_project(): pl.pallas_call(step_kernel, grid_spec=pltpu.PrefetchScalarGridSpec(num_sc...  9.04 us
    all_to_all x1, starting transfers between devices, per_device(): lax.all_to_all(message, 'role', split_axis=0, concat_axis=0, tiled=True)  8.14 us
  transfers between devices with their start and end apart: 27, of which 14 were waited for; matrix products, arithmetic and copies ran while one was open for 8% of the time, Pallas kernels for 25%

commit v1 on v0

--- a/solution.py
+++ b/solution.py
@@ -20,6 +20,8 @@
 STAT_ROWS = 16
 
 CORE = 1
+TP_MASKS = (2, 4, 12, CORE)
+ROLE_MASKS = (4, 1, 3)
 
 
 def params(mebibytes):
@@ -41,10 +43,6 @@
 def swap(x, axis, mask):
     size = TP if axis == "tp" else ROLE
     return lax.ppermute(x, axis, [(i, i ^ mask) for i in range(size)])
-
-
-def over_chips(x):
-    return [x] + [swap(x, "tp", 2 * i) for i in range(1, 8)]
 
 
 def more(held, axis, mask):
@@ -65,7 +63,6 @@
     return table
 
 
-ROLE_MASKS = (4, 1, 3)
 ROLE_OFFSETS = offsets(ROLE_MASKS)
 
 
@@ -122,7 +119,7 @@
     return wide[0:2] + wide[2:4] + wide[4:6]
 
 
-def pick_kernel(group, slot, rows, out):
+def pick_kernel(group, slot, ships, rows, out):
     count = group.shape[1]
     capacity = 2 * count // ROLE
     onehot = group[...] == lax.broadcasted_iota(jnp.int32, (ROLE, 1), 0)
@@ -138,24 +135,29 @@
     code = slot[...] + 1
     line = lax.broadcasted_iota(jnp.int32, (16, 1), 0)
     codes = jnp.where(line == 0, code // 32, jnp.where(line == 1, code % 32, 0))
-    codes = nt_dot(codes.astype(F32).astype(BF), picked).astype(BF)
+    codes = nt_dot(codes.astype(F32).astype(BF), picked)
+    page = jnp.concatenate(
+        [ships[...], jnp.zeros((1, ROLE * capacity - ships.shape[1]), jnp.int32)], axis=1
+    )
+    pages = jnp.where(line == 2, page // 128, jnp.where(line == 3, page % 128, 0))
+    codes = (codes + pages.astype(F32)).astype(BF)
     for g in range(ROLE):
         out[g, :capacity, :] = chosen[g * capacity : (g + 1) * capacity]
         out[g, capacity:, :] = codes
 
 
-def pick_rows(group, slot, rows):
+def pick_rows(group, slot, ships, rows):
     count, width = rows.shape
     capacity = 2 * count // ROLE
     return pl.pallas_call(
         pick_kernel,
-        in_specs=[vmem()] * 3,
+        in_specs=[vmem()] * 4,
         out_specs=vmem(),
         out_shape=jax.ShapeDtypeStruct((ROLE, capacity + 16, width), BF),
         compiler_params=params(16),
         cost_estimate=pl.CostEstimate(flops=2 * 10**8, bytes_accessed=2**20, transcendentals=0),
         name="pick_rows",
-    )(group.reshape(1, count), slot.reshape(1, count), rows)
+    )(group.reshape(1, count), slot.reshape(1, count), ships.reshape(1, -1), rows)
 
 
 def land_kernel(role, arrived, text, merged, squares):
@@ -283,47 +285,43 @@
 
 def all_blocks(text, gain, weights, scale, xbuf, wbuf, xsem, wsem, acc):
     blocks, rows = text.shape[0], text.shape[1]
+    widths = [weight.shape[1] for weight in weights]
+
+    def part(n, k):
+        return wbuf.at[n // 4, pl.ds(n % 4 * 512, 512), pl.ds(sum(widths[:k]), widths[k])]
+
     for n in range(blocks):
         pltpu.make_async_copy(text.at[n], xbuf.at[n], xsem.at[n]).start()
-        at = 0
         for k, weight in enumerate(weights):
-            width = weight.shape[1]
-            pltpu.make_async_copy(
-                weight.at[pl.ds(n * 512, 512)], wbuf.at[n, :, pl.ds(at, width)], wsem.at[n, k]
-            ).start()
-            at += width
-
-    def wait(n):
-        pltpu.make_async_copy(xbuf.at[n], xbuf.at[n], xsem.at[n]).wait()
-        at = 0
-        for k, weight in enumerate(weights):
-            part = wbuf.at[n, :, pl.ds(at, weight.shape[1])]
-            pltpu.make_async_copy(part, part, wsem.at[n, k]).wait()
-            at += weight.shape[1]
-
-    def pair(i, carry):
-        for n in (2 * i, 2 * i + 1):
-            wait(n)
-        gains = [gain[2 * i].astype(F32), gain[2 * i + 1].astype(F32)]
+            pltpu.make_async_copy(weight.at[pl.ds(n * 512, 512)], part(n, k), wsem.at[n, k]).start()
+
+    for i in range(blocks // 4):
+        for n in range(4 * i, 4 * i + 4):
+            pltpu.make_async_copy(xbuf.at[n], xbuf.at[n], xsem.at[n]).wait()
+            for k in range(len(weights)):
+                pltpu.make_async_copy(part(n, k), part(n, k), wsem.at[n, k]).wait()
+        gains = [gain[4 * i + k].astype(F32) for k in range(4)]
         for r in range(rows // 256):
             at = slice(r * 256, (r + 1) * 256)
             factor = scale[at, :1]
-            product = None
-            for k in range(2):
-                normed = (xbuf[2 * i + k, at, :].astype(F32) * factor * gains[k]).astype(BF)
-                term = nn_dot(normed, wbuf[2 * i + k])
-                product = term if product is None else product + term
-            acc[at, :] += product
-        return carry
-
-    acc[...] = jnp.zeros_like(acc)
-    lax.fori_loop(0, blocks // 2, pair, 0)
+            normed = jnp.concatenate(
+                [
+                    (xbuf[4 * i + k, at, :].astype(F32) * factor * gains[k]).astype(BF)
+                    for k in range(4)
+                ],
+                axis=1,
+            )
+            product = nn_dot(normed, wbuf[i])
+            if i == 0:
+                acc[at, :] = product
+            else:
+                acc[at, :] += product
 
 
 def all_scratch(blocks, rows, width, kinds):
     return [
         pltpu.VMEM((blocks, rows, 512), BF),
-        pltpu.VMEM((blocks, 512, width), BF),
+        pltpu.VMEM((blocks // 4, 2048, width), BF),
         pltpu.VMEM((rows, 128), F32),
         pltpu.SemaphoreType.DMA((blocks,)),
         pltpu.SemaphoreType.DMA((blocks, kinds)),
@@ -332,14 +330,15 @@
 
 
 def keys_kernel(
-    core, start, group, text, ssq, gain, wa, wb, q, token_row,
-    keys, values, out, xbuf, wbuf, scale, xsem, wsem, acc,
+    core, start, group, text, ssq, gain, wq, wa, wb, q, token_row,
+    queries, keys, values, out, xbuf, wbuf, scale, xsem, wsem, acc,
 ):
     row_factors(ssq, 0, scale)
-    all_blocks(text, gain, (wa, wb), scale, xbuf, wbuf, xsem, wsem, acc)
+    all_blocks(text, gain, (wq, wa, wb), scale, xbuf, wbuf, xsem, wsem, acc)
     for n in range(acc.shape[0] // 256):
         at = slice(n * 256, (n + 1) * 256)
-        own, other = acc[at, :128], acc[at, 128:]
+        queries[at, :] = acc[at, :512].astype(BF)
+        own, other = acc[at, 512:640], acc[at, 640:]
         keys[at, :] = jnp.where(core[0] == 0, own, other).astype(BF)
         values[at, :] = jnp.where(core[0] == 0, other, own).astype(BF)
     fresh_groups(group, start, q, keys, values, token_row, out)
@@ -349,14 +348,15 @@
     blocks, rows, _ = text.shape
     return pl.pallas_call(
         keys_kernel,
-        in_specs=[smem()] * 3 + [hbm()] + [vmem()] * 2 + [hbm()] * 2 + [vmem()] * 2,
-        out_specs=[vmem()] * 3,
+        in_specs=[smem()] * 3 + [hbm()] + [vmem()] * 2 + [hbm()] * 3 + [vmem()] * 2,
+        out_specs=[vmem()] * 4,
         out_shape=[
+            jax.ShapeDtypeStruct((rows, 512), BF),
             jax.ShapeDtypeStruct((rows, 128), BF),
             jax.ShapeDtypeStruct((rows, 128), BF),
             jax.ShapeDtypeStruct((ROLE, 256 + STAT_ROWS, 128), BF),
         ],
-        scratch_shapes=all_scratch(blocks, rows, 256, 2),
+        scratch_shapes=all_scratch(blocks, rows, 768, 3),
         compiler_params=params(58),
         cost_estimate=pl.CostEstimate(
             flops=6 * 10**9, bytes_accessed=20 * 2**20, transcendentals=2**20
@@ -367,15 +367,7 @@
     )
 
 
-def queries_kernel(
-    blocks_ref, text, ssq, gain, weight, keys, values,
-    out, xbuf, wbuf, scale, xsem, wsem, acc, q,
-):
-    row_factors(ssq, 0, scale)
-    all_blocks(text, gain, (weight,), scale, xbuf, wbuf, xsem, wsem, acc)
-    for n in range(acc.shape[0] // 256):
-        at = slice(n * 256, (n + 1) * 256)
-        q[at, :] = acc[at, :].astype(BF)
+def attend_kernel(blocks_ref, q, keys, values, out):
     position = lax.broadcasted_iota(jnp.int32, (1, q.shape[0]), 1)
     segment = jnp.zeros((1, q.shape[0]), F32)
     end = 0
@@ -385,20 +377,18 @@
     prefill_kernel(q, keys, values, segment, out)
 
 
-def finish_queries(request_blocks, text, ssq, gain, weight, keys, values):
-    blocks, rows, _ = text.shape
+def prefill_attention(request_blocks, q, keys, values):
     return pl.pallas_call(
-        queries_kernel,
-        in_specs=[smem(), hbm()] + [vmem()] * 2 + [hbm()] + [vmem()] * 2,
+        attend_kernel,
+        in_specs=[smem()] + [vmem()] * 3,
         out_specs=vmem(),
-        out_shape=jax.ShapeDtypeStruct((rows, 512), BF),
-        scratch_shapes=all_scratch(blocks, rows, 512, 1) + [pltpu.VMEM((rows, 512), BF)],
-        compiler_params=params(58),
+        out_shape=jax.ShapeDtypeStruct(q.shape, BF),
+        compiler_params=params(24),
         cost_estimate=pl.CostEstimate(
-            flops=12 * 10**9, bytes_accessed=25 * 2**20, transcendentals=3 * 2**20
+            flops=3 * 10**9, bytes_accessed=3 * 2**20, transcendentals=3 * 2**20
         ),
-        name="queries_and_prefill",
-    )(request_blocks, text, ssq, gain.reshape(TP, 1, 512), weight, keys, values)
+        name="prefill_attention",
+    )(request_blocks, q, keys, values)
 
 
 def paged_kernel(
@@ -501,7 +491,7 @@
         rows = pl.ds(pl.multiple_of(start[i] * PAGE_TOKENS, PAGE_TOKENS), span)
         row = lax.broadcasted_iota(jnp.int32, (256, 1), 0) // 16
         valid = token_row[i : i + 1, :] == row
-        scores = jnp.where(valid, nt_dot(q[i], keys[rows, :]), LOW)
+        scores = jnp.where(valid, nt_dot(q[i, :256, :], keys[rows, :]), LOW)
         top = jnp.maximum(jnp.max(scores, axis=1, keepdims=True), 0.5 * LOW)
         weights = jnp.exp2((scores - top) * EXP2_SCALE)
         total = jnp.sum(weights, axis=1, keepdims=True)
@@ -612,21 +602,42 @@
     )(fresh, *state)
 
 
-def page_tables(block_table, cache_len, ships, first_page):
-    pages = 128
-    page_ids = jnp.arange(pages, dtype=jnp.int32)
-    rows, entries = block_table.shape
-    code_of = (
-        jnp.arange(rows, dtype=jnp.int32)[:, None] * entries
-        + jnp.arange(entries, dtype=jnp.int32)[None, :]
-    )
-    match = block_table[None] == (first_page + page_ids)[:, None, None]
-    code = jnp.max(jnp.where(match, code_of[None], -1), axis=(1, 2))
-    replaced = jnp.any(ships.reshape(1, -1) == (first_page + page_ids)[:, None], axis=1)
-    row = jnp.where(replaced | (code < 0), rows, code // entries)
+def find_kernel(table, length, pages, row_out, live_out):
+    code = jnp.full(pages.shape, -1.0, F32)
+    entry = lax.broadcasted_iota(jnp.int32, (128, 1), 0).astype(F32)
+    for r in range(table.shape[0]):
+        for n in range(table.shape[1] // 128):
+            column = to_column(table[r : r + 1, n * 128 : (n + 1) * 128].astype(F32))
+            found = jnp.where(column == pages[...], entry + (r * 256 + n * 128), -1.0)
+            code = jnp.maximum(code, jnp.max(found, axis=0, keepdims=True))
+    code = code.astype(jnp.int32)
+    row = jnp.where(code >= 0, code // 256, -1)
+    tokens = jnp.zeros(row.shape, jnp.int32)
+    for r in range(table.shape[0]):
+        tokens = jnp.where(row == r, length[r], tokens)
+    row_out[...] = row
+    live_out[...] = jnp.where(row >= 0, jnp.clip(tokens - code % 256 * PAGE_TOKENS, 0, PAGE_TOKENS), 0)
+
+
+def find_pages(block_table, cache_len, pages):
+    count = pages.shape[0]
+    line = jax.ShapeDtypeStruct((1, count), jnp.int32)
+    row, live = pl.pallas_call(
+        find_kernel,
+        in_specs=[vmem(), smem(), vmem()],
+        out_specs=[vmem()] * 2,
+        out_shape=[line] * 2,
+        compiler_params=params(16),
+        cost_estimate=pl.CostEstimate(flops=10**7, bytes_accessed=2**16, transcendentals=0),
+        name="find_pages",
+    )(block_table, cache_len, pages.astype(F32).reshape(1, count))
+    return row[0], live[0]
+
+
+def page_tables(row, live, replaced, rows):
+    page_ids = jnp.arange(row.shape[0], dtype=jnp.int32)
+    row = jnp.where(replaced | (row < 0), rows, row)
     onehot = row[:, None] == jnp.arange(rows, dtype=jnp.int32)[None, :]
-    length = jnp.sum(jnp.where(onehot, cache_len[None, :], 0), axis=1)
-    live = jnp.clip(length - (code % entries) * PAGE_TOKENS, 0, PAGE_TOKENS)
     count = jnp.sum(onehot.astype(jnp.int32), axis=0)
     chunks = (count + 7) // 8
     ids17 = jnp.arange(rows + 1, dtype=jnp.int32)
@@ -646,31 +657,19 @@
     return first_chunk, slot_page, slot_live
 
 
-def token_rows(tables, lengths, ship_page, group):
-    rows, entries = tables.shape
+def token_rows(row, live, ship_page, group):
     pages = ship_page.shape[0]
     window = pages // 2
-    code_of = (
-        jnp.arange(rows, dtype=jnp.int32)[:, None] * entries
-        + jnp.arange(entries, dtype=jnp.int32)[None, :]
-    )
-    match = tables[None] == ship_page[:, None, None]
-    code = jnp.max(jnp.where(match, code_of[None], -1), axis=(1, 2))
-    row = jnp.where(code >= 0, code // entries, -1)
-    onehot = row[:, None] == jnp.arange(rows, dtype=jnp.int32)[None, :]
-    length = jnp.sum(jnp.where(onehot, lengths[None, :], 0), axis=1)
-    live = jnp.clip(length - (code % entries) * PAGE_TOKENS, 0, PAGE_TOKENS)
-    live = jnp.where(code >= 0, live, 0)
     page_ids = jnp.arange(pages, dtype=jnp.int32)
     ours = (ship_page // 2048)[None, :] == group[:, None]
     start = jnp.min(jnp.where(ours, page_ids[None, :], window), axis=1)
     start = jnp.minimum(start, window)
-    packed = jnp.where(live > 0, row * 32 + live, 0)
+    packed = jnp.where(ours & (live > 0), row * 32 + live, 0)
     place = start[:, None] + jnp.arange(window, dtype=jnp.int32)[None, :]
     hit = place[:, :, None] == page_ids[None, None, :]
-    here = jnp.sum(jnp.where(hit & ours[:, None, :], packed[None, None, :], 0), axis=2)
+    here = jnp.sum(jnp.where(hit, packed[:, None, :], 0), axis=2)
     token = jnp.arange(PAGE_TOKENS, dtype=jnp.int32)[None, None, :]
-    token_row = jnp.where(token < (here % 32)[:, :, None], (here // 32 % 16)[:, :, None], -1)
+    token_row = jnp.where(token < (here % 32)[:, :, None], (here // 32)[:, :, None], -1)
     return start, token_row.reshape(ROLE, window * PAGE_TOKENS)
 
 
@@ -706,20 +705,32 @@
 
     other_weight = plus(keyvalue_weight)
     weights = (query_weight, keyvalue_weight, other_weight)
-    (message,) = phase(pick_rows(vision_group, vision_slot, vision_rows))
+    (message,) = phase(pick_rows(vision_group, vision_slot, ship_page, vision_rows))
     arrived = lax.all_to_all(message, "role", split_axis=0, concat_axis=0, tiled=True)
+    steps_y = doubling(step_embed.reshape(steps * rows, width), "tp", TP_MASKS[:2])
+    arrived, steps_y = phase(arrived, steps_y)
     merged, squares = land_rows(role_id, arrived, text_embed)
     text_all = lax.all_gather(merged, "tp")
 
-    steps_all = jnp.stack(over_chips(step_embed.reshape(steps * rows, width)))
-    meta = jnp.concatenate(
-        [block_table.reshape(-1), cache_len, ship_page, jnp.zeros((48,), jnp.int32)]
-    ).reshape(33, 128)
-    metas = doubling(meta, "role", ROLE_MASKS[:1])
-    steps_all, metas = phase(steps_all, metas)
-    steps_all = more(steps_all, "tp", CORE)
+    first_page = (role * TP + column) * 128
+    parts = arrived[:, 64 + 2 : 64 + 4, : ship_page.shape[0]].astype(jnp.int32)
+    ships = parts[:, 0] * 128 + parts[:, 1]
+    page_ids = first_page + jnp.arange(paged_cache.shape[0], dtype=jnp.int32)
+    held_count = page_ids.shape[0]
+    row_of, live_of = find_pages(
+        block_table, cache_len, jnp.concatenate([page_ids, ships.reshape(-1)])
+    )
+    codes = jnp.concatenate(
+        [
+            row_of[held_count:].reshape(4, 128),
+            live_of[held_count:].reshape(4, 128),
+            jnp.zeros((8, 128), jnp.int32),
+        ],
+        axis=0,
+    ).astype(BF)
+    steps_all = more(more(steps_y, "tp", TP_MASKS[2]), "tp", CORE)
     step_q, step_a, step_b = step_project(
-        (column // 4) ^ jnp.arange(4, dtype=jnp.int32),
+        (column // 4) ^ jnp.array([0, 1, 3, 2], jnp.int32),
         (column % 4).reshape(1),
         steps_all,
         norm_gain,
@@ -730,54 +741,51 @@
     own_queries = (
         step_q.reshape(steps, rows, 4, HEAD_SIZE).transpose(1, 0, 2, 3).reshape(rows * 16, HEAD_SIZE)
     )
-    metas = more(metas, "role", ROLE_MASKS[1])
-    own_queries, metas, squares = phase(own_queries, metas, squares)
-
-    queries = jnp.stack(over_chips(jnp.concatenate([own_queries, squares], axis=0)))
-    queries_role = doubling(own_queries, "role", ROLE_MASKS[:1])
-    metas = more(metas, "role", ROLE_MASKS[2])
-    queries, queries_role, metas = phase(queries, queries_role, metas)
-
-    query_all = more(queries, "tp", CORE)
-    parts = jnp.sum(query_all[:, 256:280, :].astype(F32), axis=0)
-    ssq = parts[0:8] + parts[8:16] + parts[16:24]
-    queries_role = more(queries_role, "role", ROLE_MASKS[1])
-    metas = metas.reshape(ROLE, -1)
-    tables = metas[:, :4096].reshape(ROLE * rows, -1)
-    lengths = metas[:, 4096 : 4096 + rows].reshape(-1)
-    ships = metas[:, 4112 : 4112 + 64]
+    own_queries, squares, codes = phase(own_queries, squares, codes)
+
+    query_all = doubling(jnp.concatenate([own_queries, squares], axis=0), "tp", TP_MASKS)
+    replaced = jnp.any(ships.reshape(1, -1) == page_ids[:, None], axis=1)
+    first_chunk, slot_page, slot_live = page_tables(
+        row_of[:held_count], live_of[:held_count], replaced, rows
+    )
+    role_message = jnp.concatenate([own_queries, codes], axis=0)
+    queries_role = doubling(role_message, "role", ROLE_MASKS[:1])
+    difference = column ^ jnp.arange(TP, dtype=jnp.int32)
+    far_bit = difference // 8
+    near_bit = (difference // 4) % 2 ^ far_bit
+    where = difference // 2 % 2 + 2 * near_bit + 4 * far_bit + 8 * (difference % 2)
+    held = paged_attention(first_chunk, slot_page, slot_live, where, query_all, paged_cache)
+    held, queries_role = phase(held, queries_role)
+
+    held_parts = lax.all_to_all(held, "tp", split_axis=0, concat_axis=0, tiled=True)
+    sums = jnp.sum(query_all[:, 256:280, :].astype(F32), axis=0)
+    ssq = sums[0:8] + sums[8:16] + sums[16:24]
+    queries_role = more(more(queries_role, "role", ROLE_MASKS[1]), "role", ROLE_MASKS[2])
     role_order = role ^ jnp.array(ROLE_OFFSETS, jnp.int32)
-    first_page = (role * TP + column) * 128
-    first_chunk, slot_page, slot_live = page_tables(block_table, cache_len, ships, first_page)
-    difference = column ^ jnp.arange(TP, dtype=jnp.int32)
-    where = difference // 2 + 8 * (difference % 2)
-    held = paged_attention(first_chunk, slot_page, slot_live, where, query_all, paged_cache)
-    held, queries_role, tables = phase(held, queries_role, tables)
-
-    held_parts = lax.all_to_all(held, "tp", split_axis=0, concat_axis=0, tiled=True)
-    queries_role = more(queries_role, "role", ROLE_MASKS[2])
-    start, token_row = token_rows(tables, lengths, ship_page, role_order)
-    state = merge_held(held_parts, own_queries, new_keys, new_values)
-    text_all, start, token_row, queries_role, ssq, *state = phase(
-        text_all, start, token_row, queries_role, ssq, *state
-    )
-
-    keys, values, fresh = finish_keys(
+    info = queries_role[:, 256:264, :].reshape(ROLE, 2, ROLE * ship_page.shape[0])
+    info = lax.dynamic_slice_in_dim(info, role * ship_page.shape[0], ship_page.shape[0], 2)
+    info = info.astype(jnp.int32)
+    start, token_row = token_rows(info[:, 0], info[:, 1], ship_page, role_order)
+    text_all, start, token_row, queries_role, ssq = phase(
+        text_all, start, token_row, queries_role, ssq
+    )
+
+    prefill_queries, keys, values, fresh = finish_keys(
         core.reshape(1),
         start,
         role_order,
         text_all,
         ssq,
         norm_gain,
-        weights[1:],
+        weights,
         queries_role,
         token_row,
     )
+    fresh, held_parts = phase(fresh, held_parts)
     fresh_parts = lax.all_to_all(fresh, "role", split_axis=0, concat_axis=0, tiled=True)
 
-    prefill_out = finish_queries(
-        request_blocks, text_all, ssq, norm_gain, query_weight, keys, values
-    )
+    prefill_out = prefill_attention(request_blocks, prefill_queries, keys, values)
+    state = merge_held(held_parts, own_queries, new_keys, new_values)
 
     decode = merge(fresh_parts, state)
     decode_out = (

time: 201 us -> 193 us (0.960)
  starting transfers between devices: 48.6 us -> 41.9 us
  waiting for transfers between devices: 45.3 us -> 50.8 us
  other arithmetic: 12.8 us -> 7.42 us
    ppermute x23 -> x12, waiting for transfers between devices: 27.6 us -> 49.5 us  [swap(): return lax.ppermute(x, axis, [(i, i ^ mask) for i in range(size)])]
    ppermute x23 -> x12, starting transfers between devices: 29.4 us -> 17.5 us  [swap(): return lax.ppermute(x, axis, [(i, i ^ mask) for i in range(size)])]
    all_to_all x1, waiting for transfers between devices: 11.8 us -> 0.01 us  [per_device(): lax.all_to_all(message, 'role', split_axis=0, concat_axis=0, tiled=True)]
    pallas_call x2 -> x3, Pallas kernels: 23 us -> 11.9 us  [the longest x1 8.61 us: prefill_attention(): pl.pallas_call(attend_kernel, in_specs=[smem()] + [vmem()] * 3, out_specs...]
    pallas_call x1, Pallas kernels: 13.7 us -> 24.3 us  [finish_keys(): pl.pallas_call(keys_kernel, in_specs=[smem()] * 3 + [hbm()] + [vmem()] *...]
    all_to_all x1, waiting for transfers between devices: 5.86 us -> 0.01 us  [per_device(): lax.all_to_all(held, 'tp', split_axis=0, concat_axis=0, tiled=True)]
    all_to_all x1, starting transfers between devices: 6.45 us -> 10.9 us  [per_device(): lax.all_to_all(fresh, 'role', split_axis=0, concat_axis=0, tiled=True)]
    reduce_max x2 -> x0, other arithmetic: 4.37 us -> none  [the longest x1 2.62 us: page_tables(): code = jnp.max(jnp.where(match, code_of[None], -1), axis=(1, 2))]
  transfers between devices with their start and end apart: 27 -> 16, of which waited for: 14 -> 11; matrix products, arithmetic and copies ran while one was open for 8% -> 6% of each run, Pallas kernels for 25% -> 33%
where the time goes in v1:
time: 193 us
  Pallas kernels  68.4 us (35%)
  waiting for transfers between devices  50.8 us (26%)
  starting transfers between devices  41.9 us (22%)
  between operations  14.5 us (8%)
  local copies, waits for them, and re-layouts  9.67 us (5%)
  other arithmetic  7.42 us (4%)
    ppermute x12, waiting for transfers between devices, swap(): return lax.ppermute(x, axis, [(i, i ^ mask) for i in range(size)])  49.5 us
    pallas_call x1, Pallas kernels, finish_keys(): pl.pallas_call(keys_kernel, in_specs=[smem()] * 3 + [hbm()] + [vmem()] *...  24.3 us
    ppermute x12, starting transfers between devices, swap(): return lax.ppermute(x, axis, [(i, i ^ mask) for i in range(size)])  17.5 us
    pallas_call x1, Pallas kernels, paged_attention(): pl.pallas_call(paged_kernel, in_specs=[smem()] * 4 + [vmem(), hbm()], out...  16.3 us
    all_to_all x1, starting transfers between devices, per_device(): lax.all_to_all(fresh, 'role', split_axis=0, concat_axis=0, tiled=True)  10.9 us
    pallas_call x1, Pallas kernels, step_project(): pl.pallas_call(step_kernel, grid_spec=pltpu.PrefetchScalarGridSpec(num_sc...  9.08 us
    pallas_call x1, Pallas kernels, prefill_attention(): pl.pallas_call(attend_kernel, in_specs=[smem()] + [vmem()] * 3, out_specs...  8.61 us
    all_to_all x1, starting transfers between devices, per_device(): lax.all_to_all(message, 'role', split_axis=0, concat_axis=0, tiled=True)  8.27 us
  transfers between devices with their start and end apart: 16, of which 11 were waited for; matrix products, arithmetic and copies ran while one was open for 6% of the time, Pallas kernels for 33%

profile of v1, /device:TPU:10, one launch (start us, length us, event | category | flops | bytes accessed | tf_op | source)
XLA Modules:
  0.0 192.8 jit_solution(5133477122646357980)
XLA Ops:
  7.2 0.9 copy-done
  8.1 0.7 copy-done.1
  8.8 0.7 copy-done.2
  9.5 0.7 copy-done.3
  10.1 1.3 pick_rows.1
  11.4 8.3 %all-to-all-start = ((bf16[8,80,512]{2,1,0:T(8,128)(2,1)}), bf16[8,80,512]{2,1,0:T(8,128)(2,1)S(1)}, u32[]{:S(2)}, u32[]{:S(2)}) async-start(bf16[8,80,512]{2,1,0:T(8,128)(2,1)} %pick_rows.1), calls=%async_computation | async-start | bytes 1310720 | tf_op jit(solution)/shard_map/all_to_all | solution.py:709
  19.7 1.1 collective-permute-start
  20.8 7.8 %collective-permute-done = bf16[1,64,512]{2,1,0:T(8,128)(2,1)S(1)} collective-permute-done((bf16[1,64,512]{2,1,0:T(8,128)(2,1)S(1)}, bf16[1,64,512]{2,1,0:T(8,128)(2,1)S(1)}, u32[]{:S(2)}, u32[]{:S(2)}) %collective-permute-start) | collective-permute-done | bytes 65568 | tf_op jit(solution)/shard_map/ppermute | solution.py:45
  28.6 0.5 collective-permute-start.1
  29.1 4.5 %collective-permute-done.1 = bf16[2,64,512]{2,1,0:T(8,128)(2,1)S(1)} collective-permute-done((bf16[2,64,512]{2,1,0:T(8,128)(2,1)S(1)}, bf16[2,64,512]{2,1,0:T(8,128)(2,1)S(1)}, u32[]{:S(2)}, u32[]{:S(2)}) %collective-permute-start.1) | collective-permute-done | bytes 131104 | tf_op jit(solution)/shard_map/ppermute | solution.py:45
  33.8 1.9 land_rows.1
  35.7 0.1 collective-permute-start.4
  35.8 0.5 fusion.12.where
  36.4 0.2 select_reduce_fusion.5
  36.6 0.5 broadcast_xor_fusion.order
  37.1 0.6 reshape.273.gain
  37.8 0.5 broadcast.273
  38.3 0.7 fusion.18
  39.2 1.6 collective-permute-start.2
  40.7 2.0 %find_pages.1 = (s32[1,640]{1,0:T(1,128)S(1)}, s32[1,640]{1,0:T(1,128)S(1)}) custom-call(s32[16,256]{1,0:T(8,128)S(1)} %copy-done.9, s32[16]{0:T(128)S(1)} %copy-done.10, f32[1,640]{1,0:T(1,128)S(1)} %add_convert_fusion.pages), custom_call_target="tpu_custom_call" | custom-call | flops 10000000 | bytes 65536 | tf_op jit(solution)/shard_map/find_pages/pallas_call | solution.py:625
  42.7 0.2 compare_reduce_fusion
  42.9 0.1 convert_reduce_fusion.2
  43.1 4.8 %collective-permute-done.2 = bf16[4,64,512]{2,1,0:T(8,128)(2,1)S(1)} collective-permute-done((bf16[4,64,512]{2,1,0:T(8,128)(2,1)S(1)}, bf16[4,64,512]{2,1,0:T(8,128)(2,1)S(1)}, u32[]{:S(2)}, u32[]{:S(2)}) %collective-permute-start.2) | collective-permute-done | bytes 262176 | tf_op jit(solution)/shard_map/ppermute | solution.py:45
  48.1 2.1 %collective-permute-done.3 = bf16[8,64,512]{2,1,0:T(8,128)(2,1)S(1)} collective-permute-done((bf16[8,64,512]{2,1,0:T(8,128)(2,1)S(1)}, bf16[8,64,512]{2,1,0:T(8,128)(2,1)S(1)}, u32[]{:S(2)}, u32[]{:S(2)}) %collective-permute-start.3) | collective-permute-done | bytes 524320 | tf_op jit(solution)/shard_map/ppermute | solution.py:45
  50.2 1.1 pad_maximum_fusion.xs
  51.3 1.3 copy-done.12
  52.6 9.1 %step_project.1 = (bf16[64,512]{1,0:T(8,128)(2,1)}, bf16[64,128]{1,0:T(8,128)(2,1)}, bf16[64,128]{1,0:T(8,128)(2,1)}) custom-call(s32[4]{0:T(128)} %broadcast_xor_fusion.order, s32[1]{0:T(128)} %bitcast.14.low, bf16[16,64,512]{2,1,0:T(8,128)(2,1)} %pad_maximum_fusion.xs, bf16[4,4,1,512]{3,2,1,0:T(2,128)(2,1)} %reshape.273.gain, bf16[8192,512]{1,0:T(8,128)(2,1)} %wq.3, ...), custom_call_target="tpu_custom_call" | custom-call | flops 805306368 | bytes 14680064 | tf_op jit(solution)/shard_map/step_project/pallas_call | solution.py:246
  61.7 0.9 reshape.264
  62.6 1.6 collective-permute-start.5
  64.2 0.1 select_reduce_fusion.4.first_chunk
  64.2 2.9 %collective-permute-done.5 = bf16[1,288,128]{2,1,0:T(8,128)(2,1)S(1)} collective-permute-done((bf16[1,288,128]{2,1,0:T(8,128)(2,1)S(1)}, bf16[1,288,128]{2,1,0:T(8,128)(2,1)S(1)}, u32[]{:S(2)}, u32[]{:S(2)}) %collective-permute-start.5) | collective-permute-done | bytes 73760 | tf_op jit(solution)/shard_map/ppermute | solution.py:45
  67.2 3.5 %collective-permute-start.6 = (bf16[2,288,128]{2,1,0:T(8,128)(2,1)S(1)}, bf16[2,288,128]{2,1,0:T(8,128)(2,1)S(1)}, u32[]{:S(2)}, u32[]{:S(2)}) collective-permute-start(bf16[2,288,128]{2,1,0:T(8,128)(2,1)S(1)} %pad_maximum_fusion.6), channel_id=1, source_target_pairs={{0,4},{1,5},{2,6},{3,7},{4,0},{5,1},{6,2},{7,3},{8,12},{9,13},{10,... | collective-permute-start | bytes 442376 | tf_op jit(solution)/shard_map/ppermute | solution.py:45
  70.6 0.1 select_reduce_fusion.3
  70.7 0.2 convert_reduce_fusion.1
  70.9 7.1 %collective-permute-done.6 = bf16[2,288,128]{2,1,0:T(8,128)(2,1)S(1)} collective-permute-done((bf16[2,288,128]{2,1,0:T(8,128)(2,1)S(1)}, bf16[2,288,128]{2,1,0:T(8,128)(2,1)S(1)}, u32[]{:S(2)}, u32[]{:S(2)}) %collective-permute-start.6) | collective-permute-done | bytes 147488 | tf_op jit(solution)/shard_map/ppermute | solution.py:45
  78.1 2.4 %collective-permute-start.7 = (bf16[4,288,128]{2,1,0:T(8,128)(2,1)S(1)}, bf16[4,288,128]{2,1,0:T(8,128)(2,1)S(1)}, u32[]{:S(2)}, u32[]{:S(2)}) collective-permute-start(bf16[4,288,128]{2,1,0:T(8,128)(2,1)S(1)} %pad_maximum_fusion.3), channel_id=1, source_target_pairs={{0,12},{1,13},{2,14},{3,15},{4,8},{5,9},{6,10},{7,11},{8,4},{9,5},... | collective-permute-start | bytes 884744 | tf_op jit(solution)/shard_map/ppermute | solution.py:45
  80.5 0.7 select_reduce_fusion.1
  81.2 12.8 %collective-permute-done.7 = bf16[4,288,128]{2,1,0:T(8,128)(2,1)S(1)} collective-permute-done((bf16[4,288,128]{2,1,0:T(8,128)(2,1)S(1)}, bf16[4,288,128]{2,1,0:T(8,128)(2,1)S(1)}, u32[]{:S(2)}, u32[]{:S(2)}) %collective-permute-start.7) | collective-permute-done | bytes 294944 | tf_op jit(solution)/shard_map/ppermute | solution.py:45
  94.2 3.7 %collective-permute-start.9 = (bf16[1,272,128]{2,1,0:T(8,128)(2,1)S(1)}, bf16[1,272,128]{2,1,0:T(8,128)(2,1)S(1)}, u32[]{:S(2)}, u32[]{:S(2)}) collective-permute-start(bf16[1,272,128]{2,1,0:T(8,128)(2,1)S(1)} %maximum_bitcast_fusion.1), channel_id=1, source_target_pairs={{0,64},{16,80},{32,96},{48,112},{64,0},{80,16},{96,32},{112,48},{1... | collective-permute-start | bytes 208904 | tf_op jit(solution)/shard_map/ppermute | solution.py:45
  97.9 2.7 %collective-permute-done.9 = bf16[1,272,128]{2,1,0:T(8,128)(2,1)S(1)} collective-permute-done((bf16[1,272,128]{2,1,0:T(8,128)(2,1)S(1)}, bf16[1,272,128]{2,1,0:T(8,128)(2,1)S(1)}, u32[]{:S(2)}, u32[]{:S(2)}) %collective-permute-start.9) | collective-permute-done | bytes 69664 | tf_op jit(solution)/shard_map/ppermute | solution.py:45
  100.8 1.0 copy-done.13
  101.8 16.3 %paged_attention.1 = bf16[16,272,128]{2,1,0:T(8,128)(2,1)} custom-call(s32[17]{0:T(128)} %copy-done.21, s32[256]{0:T(256)} %get-tuple-element.59.slot_page, s32[256]{0:T(256)} %get-tuple-element.58.slot_live, s32[16]{0:T(128)} %fusion.12.where, bf16[16,288,128]{2,1,0:T(8,128)(2,1)} %copy-done.13, bf16[128,16,2048]{2,1,0:T(8,128)(2,1)} %cache.1), custom_call_target="tpu_custom_call" | custom-call | flops 2000000000 | bytes 12582912 | tf_op jit(solution)/shard_map/paged_attention/pallas_call | solution.py:467
  118.1 0.3 collective-permute-start.10
  118.5 0.6 reshape.274.gain
  119.2 0.9 convert_reduce_fusion
  120.1 3.5 %collective-permute-done.10 = bf16[2,272,128]{2,1,0:T(8,128)(2,1)S(1)} collective-permute-done((bf16[2,272,128]{2,1,0:T(8,128)(2,1)S(1)}, bf16[2,272,128]{2,1,0:T(8,128)(2,1)S(1)}, u32[]{:S(2)}, u32[]{:S(2)}) %collective-permute-start.10) | collective-permute-done | bytes 139296 | tf_op jit(solution)/shard_map/ppermute | solution.py:45
  123.6 2.7 %collective-permute-start.11 = (bf16[4,272,128]{2,1,0:T(8,128)(2,1)S(1)}, bf16[4,272,128]{2,1,0:T(8,128)(2,1)S(1)}, u32[]{:S(2)}, u32[]{:S(2)}) collective-permute-start(bf16[4,272,128]{2,1,0:T(8,128)(2,1)S(1)} %pad_maximum_fusion.4), channel_id=1, source_target_pairs={{0,48},{16,32},{32,16},{48,0},{64,112},{80,96},{96,80},{112,64},{1... | collective-permute-start | bytes 835592 | tf_op jit(solution)/shard_map/ppermute | solution.py:45
  126.3 0.6 slice_add_fusion.ssq
  126.9 5.2 %all-to-all-start.1 = ((bf16[16,272,128]{2,1,0:T(8,128)(2,1)}), bf16[16,272,128]{2,1,0:T(8,128)(2,1)S(1)}, u32[]{:S(2)}, u32[]{:S(2)}) async-start(bf16[16,272,128]{2,1,0:T(8,128)(2,1)} %paged_attention.1), calls=%async_computation.1 | async-start | bytes 2228224 | tf_op jit(solution)/shard_map/all_to_all | solution.py:760
  132.1 1.2 collective-permute-done.11
  133.4 0.1 dynamic-slice_convert_fusion
  133.6 0.3 select_reduce_fusion
  133.9 0.1 lt.121
  134.0 0.1 lt.122
  134.1 0.1 broadcast_in_dim.153
  134.2 0.1 broadcast_in_dim.154
  134.3 0.6 compare_select_fusion.token_row
  134.9 1.4 all-gather.3.cloned.1.call-done
  136.3 24.3 %keys_and_fresh_pages.1 = (bf16[1024,512]{1,0:T(8,128)(2,1)}, bf16[1024,128]{1,0:T(8,128)(2,1)}, bf16[1024,128]{1,0:T(8,128)(2,1)}, bf16[8,272,128]{2,1,0:T(8,128)(2,1)}) custom-call(s32[1]{0:T(128)} %bitcast.core, s32[8]{0:T(128)} %copy-done.19, s32[8]{0:T(128)} %copy-done.20, bf16[16,1024,512]{2,1,0:T(8,128)(2,1)} %bitcast.55, ...), custom_call_target="tpu_custom_call" | custom-call | flops 6000000000 | bytes 20971520 | tf_op jit(solution)/shard_map/keys_and_fresh_pages/pallas_call | solution.py:349
  160.6 10.9 %all-to-all-start.2 = ((bf16[8,272,128]{2,1,0:T(8,128)(2,1)}), bf16[8,272,128]{2,1,0:T(8,128)(2,1)S(1)}, u32[]{:S(2)}, u32[]{:S(2)}) async-start(bf16[8,272,128]{2,1,0:T(8,128)(2,1)} %get-tuple-element.51), calls=%async_computation.2 | async-start | bytes 1114112 | tf_op jit(solution)/shard_map/all_to_all | solution.py:785
  171.6 3.4 %merge_held_pages.1 = (f32[256,128]{1,0:T(8,128)S(1)}, f32[256,128]{1,0:T(8,128)S(1)}, f32[256,128]{1,0:T(8,128)S(1)}) custom-call(bf16[16,272,128]{2,1,0:T(8,128)(2,1)S(1)} %all-to-all-done.1.held, bf16[256,128]{1,0:T(8,128)(2,1)S(1)} %bitcast.50, bf16[64,128]{1,0:T(8,128)(2,1)S(1)} %get-tuple-element.63.new_keys, ...), custom_call_target="tpu_custom_call" | custom-call | flops 10000000 | bytes 2097152 | tf_op jit(solution)/shard_map/merge_held_pages/pallas_call | solution.py:563
  175.0 8.6 %prefill_attention.1 = bf16[1024,512]{1,0:T(8,128)(2,1)} custom-call(s32[1,8]{1,0:T(1,128)S(1)} %copy-done.11, bf16[1024,512]{1,0:T(8,128)(2,1)S(1)} %copy-done.6, bf16[1024,128]{1,0:T(8,128)(2,1)S(1)} %copy-done.7, bf16[1024,128]{1,0:T(8,128)(2,1)S(1)} %copy-done.8), custom_call_target="tpu_custom_call" | custom-call | flops 3000000000 | bytes 3145728 | tf_op jit(solution)/shard_map/prefill_attention/pallas_call | solution.py:381
  183.6 1.6 decode_merge.1
  185.3 0.6 copy.27
  (96 shorter events, 1.5 us)
Async XLA Ops:
  7.2 1.0 copy-start
  8.1 0.7 copy-start.1
  8.8 0.7 copy-start.2
  9.5 0.7 copy-start.3
  10.1 9.6 %copy-start.15 = (bf16[4,16,512]{2,1,0:T(8,128)(2,1)S(1)}, bf16[4,16,512]{2,1,0:T(8,128)(2,1)}, u32[]{:S(2)}) copy-start(bf16[4,16,512]{2,1,0:T(8,128)(2,1)} %param.24) | copy-start | bytes 196612
  11.4 22.3 %copy-start.5 = (bf16[1024,512]{1,0:T(8,128)(2,1)S(1)}, bf16[1024,512]{1,0:T(8,128)(2,1)}, u32[]{:S(2)}) copy-start(bf16[1024,512]{1,0:T(8,128)(2,1)} %text.1) | copy-start | bytes 3145732
  11.4 22.3 %all-to-all-start = ((bf16[8,80,512]{2,1,0:T(8,128)(2,1)}), bf16[8,80,512]{2,1,0:T(8,128)(2,1)S(1)}, u32[]{:S(2)}, u32[]{:S(2)}) async-start(bf16[8,80,512]{2,1,0:T(8,128)(2,1)} %pick_rows.1), calls=%async_computation | async-start | bytes 1310720 | tf_op jit(solution)/shard_map/all_to_all | solution.py:709
  19.7 116.6 %all-gather.3.cloned.1.call-start = ((), (), s32[]{:S(2)}) async-start(), calls=%async_computation.3 | async-start | bytes 17825792 | tf_op jit(solution)/shard_map/all_gather | solution.py:713
  19.7 8.9 %collective-permute-start = (bf16[1,64,512]{2,1,0:T(8,128)(2,1)S(1)}, bf16[1,64,512]{2,1,0:T(8,128)(2,1)S(1)}, u32[]{:S(2)}, u32[]{:S(2)}) collective-permute-start(bf16[1,64,512]{2,1,0:T(8,128)(2,1)S(1)} %bitcast.56), channel_id=1, source_target_pairs={{0,2},{1,3},{2,0},{3,1},{4,6},{5,7},{6,4},{7,5},{8,10},{9,11},{10,... | collective-permute-start | bytes 196616 | tf_op jit(solution)/shard_map/ppermute | solution.py:45
  28.6 5.0 %collective-permute-start.1 = (bf16[2,64,512]{2,1,0:T(8,128)(2,1)S(1)}, bf16[2,64,512]{2,1,0:T(8,128)(2,1)S(1)}, u32[]{:S(2)}, u32[]{:S(2)}) collective-permute-start(bf16[2,64,512]{2,1,0:T(8,128)(2,1)S(1)} %pad_maximum_fusion.8), channel_id=1, source_target_pairs={{0,4},{1,5},{2,6},{3,7},{4,0},{5,1},{6,2},{7,3},{8,12},{9,13},{10,... | collective-permute-start | bytes 393224 | tf_op jit(solution)/shard_map/ppermute | solution.py:45
  33.7 2.6 %copy-start.4 = (s32[64]{0:T(128)S(1)}, s32[64]{0:T(128)}, u32[]{:S(2)}) copy-start(s32[64]{0:T(128)} %param.20) | copy-start | bytes 772
  33.7 2.6 %copy-start.23 = (s32[8]{0:T(128)S(1)}, s32[8]{0:T(128)}, u32[]{:S(2)}) copy-start(s32[8]{0:T(128)} %constant.169.clone) | copy-start | bytes 100
  33.7 2.8 %copy-start.22 = (s32[4]{0:T(128)S(1)}, s32[4]{0:T(128)}, u32[]{:S(2)}) copy-start(s32[4]{0:T(128)} %constant.168.clone) | copy-start | bytes 52
  33.8 3.4 %copy-start.16 = (bf16[8192]{0:T(1024)(128)(2,1)S(1)}, bf16[8192]{0:T(1024)(128)(2,1)}, u32[]{:S(2)}) copy-start(bf16[8192]{0:T(1024)(128)(2,1)} %param.25) | copy-start | bytes 49156
  35.7 5.1 %copy-start.9 = (s32[16,256]{1,0:T(8,128)S(1)}, s32[16,256]{1,0:T(8,128)}, u32[]{:S(2)}) copy-start(s32[16,256]{1,0:T(8,128)} %table.1) | copy-start | bytes 49156
  35.7 5.1 %copy-start.10 = (s32[16]{0:T(128)S(1)}, s32[16]{0:T(128)}, u32[]{:S(2)}) copy-start(s32[16]{0:T(128)} %length.1) | copy-start | bytes 196
  35.7 15.6 %collective-permute-start.4 = (bf16[8192,128]{1,0:T(8,128)(2,1)}, bf16[8192,128]{1,0:T(8,128)(2,1)S(1)}, u32[]{:S(2)}, u32[]{:S(2)}) collective-permute-start(bf16[8192,128]{1,0:T(8,128)(2,1)} %wa.3), channel_id=1, source_target_pairs={{0,1},{1,0},{2,3},{3,2},{4,5},{5,4},{6,7},{7,6},{8,9},{9,8},{10,11... | collective-permute-start | bytes 6291464 | tf_op jit(solution)/shard_map/ppermute | solution.py:45
  36.4 97.1 %copy-start.20 = (s32[8]{0:T(128)}, s32[8]{0:T(128)S(1)}, u32[]{:S(2)}) copy-start(s32[8]{0:T(128)S(1)} %broadcast_xor_fusion.1.group) | copy-start | bytes 100
  36.6 81.8 %copy-start.19 = (s32[8]{0:T(128)}, s32[8]{0:T(128)S(1)}, u32[]{:S(2)}) copy-start(s32[8]{0:T(128)S(1)} %broadcast_minimum_fusion.start) | copy-start | bytes 100
  39.2 8.7 %collective-permute-start.2 = (bf16[4,64,512]{2,1,0:T(8,128)(2,1)S(1)}, bf16[4,64,512]{2,1,0:T(8,128)(2,1)S(1)}, u32[]{:S(2)}, u32[]{:S(2)}) collective-permute-start(bf16[4,64,512]{2,1,0:T(8,128)(2,1)S(1)} %pad_maximum_fusion.5), channel_id=1, source_target_pairs={{0,12},{1,13},{2,14},{3,15},{4,8},{5,9},{6,10},{7,11},{8,4},{9,5},... | collective-permute-start | bytes 786440 | tf_op jit(solution)/shard_map/ppermute | solution.py:45
  47.9 2.3 %collective-permute-start.3 = (bf16[8,64,512]{2,1,0:T(8,128)(2,1)S(1)}, bf16[8,64,512]{2,1,0:T(8,128)(2,1)S(1)}, u32[]{:S(2)}, u32[]{:S(2)}) collective-permute-start(bf16[8,64,512]{2,1,0:T(8,128)(2,1)S(1)} %pad_maximum_fusion.2), channel_id=1, source_target_pairs={{0,1},{1,0},{2,3},{3,2},{4,5},{5,4},{6,7},{7,6},{8,9},{9,8},{10,11... | collective-permute-start | bytes 1572872 | tf_op jit(solution)/shard_map/ppermute | solution.py:45
  51.3 1.3 copy-start.12
  62.6 4.6 %collective-permute-start.5 = (bf16[1,288,128]{2,1,0:T(8,128)(2,1)S(1)}, bf16[1,288,128]{2,1,0:T(8,128)(2,1)S(1)}, u32[]{:S(2)}, u32[]{:S(2)}) collective-permute-start(bf16[1,288,128]{2,1,0:T(8,128)(2,1)S(1)} %maximum_bitcast_fusion), channel_id=1, source_target_pairs={{0,2},{1,3},{2,0},{3,1},{4,6},{5,7},{6,4},{7,5},{8,10},{9,11},{10,... | collective-permute-start | bytes 221192 | tf_op jit(solution)/shard_map/ppermute | solution.py:45
  64.2 33.6 %copy-start.21 = (s32[17]{0:T(128)}, s32[17]{0:T(128)S(1)}, u32[]{:S(2)}) copy-start(s32[17]{0:T(128)S(1)} %select_reduce_fusion.4.first_chunk) | copy-start | bytes 208
  67.2 10.9 %collective-permute-start.6 = (bf16[2,288,128]{2,1,0:T(8,128)(2,1)S(1)}, bf16[2,288,128]{2,1,0:T(8,128)(2,1)S(1)}, u32[]{:S(2)}, u32[]{:S(2)}) collective-permute-start(bf16[2,288,128]{2,1,0:T(8,128)(2,1)S(1)} %pad_maximum_fusion.6), channel_id=1, source_target_pairs={{0,4},{1,5},{2,6},{3,7},{4,0},{5,1},{6,2},{7,3},{8,12},{9,13},{10,... | collective-permute-start | bytes 442376 | tf_op jit(solution)/shard_map/ppermute | solution.py:45
  78.1 15.9 %collective-permute-start.7 = (bf16[4,288,128]{2,1,0:T(8,128)(2,1)S(1)}, bf16[4,288,128]{2,1,0:T(8,128)(2,1)S(1)}, u32[]{:S(2)}, u32[]{:S(2)}) collective-permute-start(bf16[4,288,128]{2,1,0:T(8,128)(2,1)S(1)} %pad_maximum_fusion.3), channel_id=1, source_target_pairs={{0,12},{1,13},{2,14},{3,15},{4,8},{5,9},{6,10},{7,11},{8,4},{9,5},... | collective-permute-start | bytes 884744 | tf_op jit(solution)/shard_map/ppermute | solution.py:45
  94.1 6.6 %collective-permute-start.8 = (bf16[8,288,128]{2,1,0:T(8,128)(2,1)S(1)}, bf16[8,288,128]{2,1,0:T(8,128)(2,1)S(1)}, u32[]{:S(2)}, u32[]{:S(2)}) collective-permute-start(bf16[8,288,128]{2,1,0:T(8,128)(2,1)S(1)} %pad_maximum_fusion.1), channel_id=1, source_target_pairs={{0,1},{1,0},{2,3},{3,2},{4,5},{5,4},{6,7},{7,6},{8,9},{9,8},{10,11... | collective-permute-start | bytes 1769480 | tf_op jit(solution)/shard_map/ppermute | solution.py:45
  94.2 6.4 %collective-permute-start.9 = (bf16[1,272,128]{2,1,0:T(8,128)(2,1)S(1)}, bf16[1,272,128]{2,1,0:T(8,128)(2,1)S(1)}, u32[]{:S(2)}, u32[]{:S(2)}) collective-permute-start(bf16[1,272,128]{2,1,0:T(8,128)(2,1)S(1)} %maximum_bitcast_fusion.1), channel_id=1, source_target_pairs={{0,64},{16,80},{32,96},{48,112},{64,0},{80,16},{96,32},{112,48},{1... | collective-permute-start | bytes 208904 | tf_op jit(solution)/shard_map/ppermute | solution.py:45
  100.8 1.0 copy-start.13
  118.1 5.5 %collective-permute-start.10 = (bf16[2,272,128]{2,1,0:T(8,128)(2,1)S(1)}, bf16[2,272,128]{2,1,0:T(8,128)(2,1)S(1)}, u32[]{:S(2)}, u32[]{:S(2)}) collective-permute-start(bf16[2,272,128]{2,1,0:T(8,128)(2,1)S(1)} %pad_maximum_fusion.7), channel_id=1, source_target_pairs={{0,16},{16,0},{32,48},{48,32},{64,80},{80,64},{96,112},{112,96},{1... | collective-permute-start | bytes 417800 | tf_op jit(solution)/shard_map/ppermute | solution.py:45
  123.6 9.7 %collective-permute-start.11 = (bf16[4,272,128]{2,1,0:T(8,128)(2,1)S(1)}, bf16[4,272,128]{2,1,0:T(8,128)(2,1)S(1)}, u32[]{:S(2)}, u32[]{:S(2)}) collective-permute-start(bf16[4,272,128]{2,1,0:T(8,128)(2,1)S(1)} %pad_maximum_fusion.4), channel_id=1, source_target_pairs={{0,48},{16,32},{32,16},{48,0},{64,112},{80,96},{96,80},{112,64},{1... | collective-permute-start | bytes 835592 | tf_op jit(solution)/shard_map/ppermute | solution.py:45
  126.9 33.7 %all-to-all-start.1 = ((bf16[16,272,128]{2,1,0:T(8,128)(2,1)}), bf16[16,272,128]{2,1,0:T(8,128)(2,1)S(1)}, u32[]{:S(2)}, u32[]{:S(2)}) async-start(bf16[16,272,128]{2,1,0:T(8,128)(2,1)} %paged_attention.1), calls=%async_computation.1 | async-start | bytes 2228224 | tf_op jit(solution)/shard_map/all_to_all | solution.py:760
  133.4 2.9 %copy-start.14 = (bf16[8,272,128]{2,1,0:T(8,128)(2,1)}, bf16[8,272,128]{2,1,0:T(8,128)(2,1)S(1)}, u32[]{:S(2)}) copy-start(bf16[8,272,128]{2,1,0:T(8,128)(2,1)S(1)} %constant_dynamic-update-slice_fusion.5.q) | copy-start | bytes 1671172
  136.3 35.3 %copy-start.17 = (bf16[64,128]{1,0:T(8,128)(2,1)S(1)}, bf16[64,128]{1,0:T(8,128)(2,1)}, u32[]{:S(2)}) copy-start(bf16[64,128]{1,0:T(8,128)(2,1)} %get-tuple-element.53) | copy-start | bytes 49156
  136.3 35.3 %copy-start.18 = (bf16[64,128]{1,0:T(8,128)(2,1)S(1)}, bf16[64,128]{1,0:T(8,128)(2,1)}, u32[]{:S(2)}) copy-start(bf16[64,128]{1,0:T(8,128)(2,1)} %get-tuple-element.54) | copy-start | bytes 49156
  160.6 14.4 %copy-start.6 = (bf16[1024,512]{1,0:T(8,128)(2,1)S(1)}, bf16[1024,512]{1,0:T(8,128)(2,1)}, u32[]{:S(2)}) copy-start(bf16[1024,512]{1,0:T(8,128)(2,1)} %get-tuple-element.46.q) | copy-start | bytes 3145732
  160.6 14.4 %copy-start.7 = (bf16[1024,128]{1,0:T(8,128)(2,1)S(1)}, bf16[1024,128]{1,0:T(8,128)(2,1)}, u32[]{:S(2)}) copy-start(bf16[1024,128]{1,0:T(8,128)(2,1)} %get-tuple-element.47.keys) | copy-start | bytes 786436
  160.6 14.4 %copy-start.11 = (s32[1,8]{1,0:T(1,128)S(1)}, s32[1,8]{1,0:T(1,128)}, u32[]{:S(2)}) copy-start(s32[1,8]{1,0:T(1,128)} %blocks_ref.1) | copy-start | bytes 100
  160.6 23.0 %all-to-all-start.2 = ((bf16[8,272,128]{2,1,0:T(8,128)(2,1)}), bf16[8,272,128]{2,1,0:T(8,128)(2,1)S(1)}, u32[]{:S(2)}, u32[]{:S(2)}) async-start(bf16[8,272,128]{2,1,0:T(8,128)(2,1)} %get-tuple-element.51), calls=%async_computation.2 | async-start | bytes 1114112 | tf_op jit(solution)/shard_map/all_to_all | solution.py:785
  171.5 3.4 %copy-start.8 = (bf16[1024,128]{1,0:T(8,128)(2,1)S(1)}, bf16[1024,128]{1,0:T(8,128)(2,1)}, u32[]{:S(2)}) copy-start(bf16[1024,128]{1,0:T(8,128)(2,1)} %get-tuple-element.48.values) | copy-start | bytes 786436
Sparse Core Ops, SparseCore 0:
  35.8 100.4 all-gather.2

commit v2 on v1

--- a/solution.py
+++ b/solution.py
@@ -119,7 +119,13 @@
     return wide[0:2] + wide[2:4] + wide[4:6]
 
 
-def pick_kernel(group, slot, ships, rows, out):
+def pick_kernel(group_in, slot_in, ships_in, rows_in, out, group, slot, ships, rows, sem):
+    pairs = ((group_in, group), (slot_in, slot), (ships_in, ships), (rows_in, rows))
+    copies = [pltpu.make_async_copy(a, b, sem.at[n]) for n, (a, b) in enumerate(pairs)]
+    for copy in copies:
+        copy.start()
+    for copy in copies:
+        copy.wait()
     count = group.shape[1]
     capacity = 2 * count // ROLE
     onehot = group[...] == lax.broadcasted_iota(jnp.int32, (ROLE, 1), 0)
@@ -151,10 +157,17 @@
     capacity = 2 * count // ROLE
     return pl.pallas_call(
         pick_kernel,
-        in_specs=[vmem()] * 4,
+        in_specs=[hbm()] * 4,
         out_specs=vmem(),
+        scratch_shapes=[
+            pltpu.VMEM((1, count), jnp.int32),
+            pltpu.VMEM((1, count), jnp.int32),
+            pltpu.VMEM((1, ships.shape[0]), jnp.int32),
+            pltpu.VMEM(rows.shape, BF),
+            pltpu.SemaphoreType.DMA((4,)),
+        ],
         out_shape=jax.ShapeDtypeStruct((ROLE, capacity + 16, width), BF),
-        compiler_params=params(16),
+        compiler_params=params(58),
         cost_estimate=pl.CostEstimate(flops=2 * 10**8, bytes_accessed=2**20, transcendentals=0),
         name="pick_rows",
     )(group.reshape(1, count), slot.reshape(1, count), ships.reshape(1, -1), rows)
@@ -290,16 +303,21 @@
     def part(n, k):
         return wbuf.at[n // 4, pl.ds(n % 4 * 512, 512), pl.ds(sum(widths[:k]), widths[k])]
 
-    for n in range(blocks):
-        pltpu.make_async_copy(text.at[n], xbuf.at[n], xsem.at[n]).start()
-        for k, weight in enumerate(weights):
-            pltpu.make_async_copy(weight.at[pl.ds(n * 512, 512)], part(n, k), wsem.at[n, k]).start()
-
+    def fetch(i):
+        for n in range(4 * i, 4 * i + 4):
+            pltpu.make_async_copy(text.at[n], xbuf.at[n], xsem.at[n]).start()
+            for k, weight in enumerate(weights):
+                rows_of = weight.at[pl.ds(n * 512, 512)]
+                pltpu.make_async_copy(rows_of, part(n, k), wsem.at[n, k]).start()
+
+    fetch(0)
     for i in range(blocks // 4):
         for n in range(4 * i, 4 * i + 4):
             pltpu.make_async_copy(xbuf.at[n], xbuf.at[n], xsem.at[n]).wait()
             for k in range(len(weights)):
                 pltpu.make_async_copy(part(n, k), part(n, k), wsem.at[n, k]).wait()
+        if i + 1 < blocks // 4:
+            fetch(i + 1)
         gains = [gain[4 * i + k].astype(F32) for k in range(4)]
         for r in range(rows // 256):
             at = slice(r * 256, (r + 1) * 256)

time: 193 us -> 189 us (0.979)
  local copies, waits for them, and re-layouts: 9.67 us -> 6.72 us
    unnamed x53 -> x45, local copies, waits for them, and re-layouts: 5.49 us -> 2.53 us
  transfers between devices with their start and end apart: 16 -> 16, of which waited for: 11 -> 10; matrix products, arithmetic and copies ran while one was open for 6% -> 6% of each run, Pallas kernels for 33% -> 33%
where the time goes in v2:
time: 189 us; the launch traced here: 190 us
  Pallas kernels  68.5 us (36%)
  waiting for transfers between devices  50.1 us (27%)
  starting transfers between devices  42.6 us (23%)
  between operations  14.6 us (8%)
  other arithmetic  7.49 us (4%)
  local copies, waits for them, and re-layouts  6.72 us (4%)
    ppermute x12, waiting for transfers between devices, swap(): return lax.ppermute(x, axis, [(i, i ^ mask) for i in range(size)])  48 us
    pallas_call x1, Pallas kernels, finish_keys(): pl.pallas_call(keys_kernel, in_specs=[smem()] * 3 + [hbm()] + [vmem()] *...  22.5 us
    pallas_call x1, Pallas kernels, paged_attention(): pl.pallas_call(paged_kernel, in_specs=[smem()] * 4 + [vmem(), hbm()], out...  17 us
    ppermute x12, starting transfers between devices, swap(): return lax.ppermute(x, axis, [(i, i ^ mask) for i in range(size)])  16.9 us
    all_to_all x1, starting transfers between devices, per_device(): lax.all_to_all(fresh, 'role', split_axis=0, concat_axis=0, tiled=True)  11.7 us
    pallas_call x1, Pallas kernels, step_project(): pl.pallas_call(step_kernel, grid_spec=pltpu.PrefetchScalarGridSpec(num_sc...  9.08 us
    pallas_call x1, Pallas kernels, prefill_attention(): pl.pallas_call(attend_kernel, in_specs=[smem()] + [vmem()] * 3, out_specs...  8.62 us
    all_to_all x1, starting transfers between devices, per_device(): lax.all_to_all(message, 'role', split_axis=0, concat_axis=0, tiled=True)  8.29 us
  transfers between devices with their start and end apart: 16, of which 10 were waited for; matrix products, arithmetic and copies ran while one was open for 6% of the time, Pallas kernels for 33%

profile of v2, /device:TPU:10, one launch (start us, length us, event | category | flops | bytes accessed | tf_op | source)
XLA Modules:
  0.0 190.0 jit_solution(8587011748981536453)
XLA Ops:
  7.2 2.3 %pick_rows.1 = bf16[8,80,512]{2,1,0:T(8,128)(2,1)} custom-call(s32[1,256]{1,0:T(1,128)} %bitcast.60, s32[1,256]{1,0:T(1,128)} %bitcast.61, s32[1,64]{1,0:T(1,128)} %bitcast.62, bf16[256,512]{1,0:T(8,128)(2,1)} %rows_in.1), custom_call_target="tpu_custom_call" | custom-call | flops 200000000 | bytes 1048576 | tf_op jit(solution)/shard_map/pick_rows/pallas_call | solution.py:158
  9.5 8.3 %all-to-all-start = ((bf16[8,80,512]{2,1,0:T(8,128)(2,1)}), bf16[8,80,512]{2,1,0:T(8,128)(2,1)S(1)}, u32[]{:S(2)}, u32[]{:S(2)}) async-start(bf16[8,80,512]{2,1,0:T(8,128)(2,1)} %pick_rows.1), calls=%async_computation | async-start | bytes 1310720 | tf_op jit(solution)/shard_map/all_to_all | solution.py:727
  17.8 1.1 collective-permute-start
  18.9 7.8 %collective-permute-done = bf16[1,64,512]{2,1,0:T(8,128)(2,1)S(1)} collective-permute-done((bf16[1,64,512]{2,1,0:T(8,128)(2,1)S(1)}, bf16[1,64,512]{2,1,0:T(8,128)(2,1)S(1)}, u32[]{:S(2)}, u32[]{:S(2)}) %collective-permute-start) | collective-permute-done | bytes 65568 | tf_op jit(solution)/shard_map/ppermute | solution.py:45
  26.8 0.5 collective-permute-start.1
  27.3 4.5 %collective-permute-done.1 = bf16[2,64,512]{2,1,0:T(8,128)(2,1)S(1)} collective-permute-done((bf16[2,64,512]{2,1,0:T(8,128)(2,1)S(1)}, bf16[2,64,512]{2,1,0:T(8,128)(2,1)S(1)}, u32[]{:S(2)}, u32[]{:S(2)}) %collective-permute-start.1) | collective-permute-done | bytes 131104 | tf_op jit(solution)/shard_map/ppermute | solution.py:45
  31.9 1.9 %land_rows.1 = (bf16[1024,512]{1,0:T(8,128)(2,1)}, bf16[32,128]{1,0:T(8,128)(2,1)S(1)}) custom-call(s32[1]{0:T(128)} %bitcast.1.role, bf16[8,80,512]{2,1,0:T(8,128)(2,1)S(1)} %all-to-all-done.arrived, bf16[1024,512]{1,0:T(8,128)(2,1)S(1)} %copy-done), custom_call_target="tpu_custom_call" | custom-call | flops 1000000000 | bytes 6291456 | tf_op jit(solution)/shard_map/land_rows/pallas_call | solution.py:205
  33.8 0.1 collective-permute-start.4
  34.0 0.6 fusion.12.where
  34.6 0.2 select_reduce_fusion.5
  34.8 0.5 broadcast_xor_fusion.order
  35.3 0.6 reshape.273.gain
  35.9 0.1 pad.19.clone
  36.0 0.5 broadcast.273
  36.6 0.7 fusion.18
  37.4 1.6 collective-permute-start.2
  39.0 2.0 %find_pages.1 = (s32[1,640]{1,0:T(1,128)S(1)}, s32[1,640]{1,0:T(1,128)S(1)}) custom-call(s32[16,256]{1,0:T(8,128)S(1)} %copy-done.4, s32[16]{0:T(128)S(1)} %copy-done.5, f32[1,640]{1,0:T(1,128)S(1)} %add_convert_fusion.pages), custom_call_target="tpu_custom_call" | custom-call | flops 10000000 | bytes 65536 | tf_op jit(solution)/shard_map/find_pages/pallas_call | solution.py:643
  41.0 0.2 compare_reduce_fusion
  41.1 0.1 convert_reduce_fusion.2
  41.3 4.8 %collective-permute-done.2 = bf16[4,64,512]{2,1,0:T(8,128)(2,1)S(1)} collective-permute-done((bf16[4,64,512]{2,1,0:T(8,128)(2,1)S(1)}, bf16[4,64,512]{2,1,0:T(8,128)(2,1)S(1)}, u32[]{:S(2)}, u32[]{:S(2)}) %collective-permute-start.2) | collective-permute-done | bytes 262176 | tf_op jit(solution)/shard_map/ppermute | solution.py:45
  46.1 0.1 collective-permute-start.3
  46.3 2.0 %collective-permute-done.3 = bf16[8,64,512]{2,1,0:T(8,128)(2,1)S(1)} collective-permute-done((bf16[8,64,512]{2,1,0:T(8,128)(2,1)S(1)}, bf16[8,64,512]{2,1,0:T(8,128)(2,1)S(1)}, u32[]{:S(2)}, u32[]{:S(2)}) %collective-permute-start.3) | collective-permute-done | bytes 524320 | tf_op jit(solution)/shard_map/ppermute | solution.py:45
  48.3 1.1 pad_maximum_fusion.xs
  49.4 1.3 copy-done.7
  50.7 9.1 %step_project.1 = (bf16[64,512]{1,0:T(8,128)(2,1)}, bf16[64,128]{1,0:T(8,128)(2,1)}, bf16[64,128]{1,0:T(8,128)(2,1)}) custom-call(s32[4]{0:T(128)} %broadcast_xor_fusion.order, s32[1]{0:T(128)} %bitcast.14.low, bf16[16,64,512]{2,1,0:T(8,128)(2,1)} %pad_maximum_fusion.xs, bf16[4,4,1,512]{3,2,1,0:T(2,128)(2,1)} %reshape.273.gain, bf16[8192,512]{1,0:T(8,128)(2,1)} %wq.3, ...), custom_call_target="tpu_custom_call" | custom-call | flops 805306368 | bytes 14680064 | tf_op jit(solution)/shard_map/step_project/pallas_call | solution.py:259
  59.8 0.9 reshape.264
  60.7 1.6 collective-permute-start.5
  62.3 0.1 select_reduce_fusion.4.first_chunk
  62.4 2.9 %collective-permute-done.5 = bf16[1,288,128]{2,1,0:T(8,128)(2,1)S(1)} collective-permute-done((bf16[1,288,128]{2,1,0:T(8,128)(2,1)S(1)}, bf16[1,288,128]{2,1,0:T(8,128)(2,1)S(1)}, u32[]{:S(2)}, u32[]{:S(2)}) %collective-permute-start.5) | collective-permute-done | bytes 73760 | tf_op jit(solution)/shard_map/ppermute | solution.py:45
  65.3 3.5 %collective-permute-start.6 = (bf16[2,288,128]{2,1,0:T(8,128)(2,1)S(1)}, bf16[2,288,128]{2,1,0:T(8,128)(2,1)S(1)}, u32[]{:S(2)}, u32[]{:S(2)}) collective-permute-start(bf16[2,288,128]{2,1,0:T(8,128)(2,1)S(1)} %pad_maximum_fusion.6), channel_id=1, source_target_pairs={{0,4},{1,5},{2,6},{3,7},{4,0},{5,1},{6,2},{7,3},{8,12},{9,13},{10,... | collective-permute-start | bytes 442376 | tf_op jit(solution)/shard_map/ppermute | solution.py:45
  68.9 0.1 select_reduce_fusion.3
  68.9 0.2 convert_reduce_fusion.1
  69.1 7.1 %collective-permute-done.6 = bf16[2,288,128]{2,1,0:T(8,128)(2,1)S(1)} collective-permute-done((bf16[2,288,128]{2,1,0:T(8,128)(2,1)S(1)}, bf16[2,288,128]{2,1,0:T(8,128)(2,1)S(1)}, u32[]{:S(2)}, u32[]{:S(2)}) %collective-permute-start.6) | collective-permute-done | bytes 147488 | tf_op jit(solution)/shard_map/ppermute | solution.py:45
  76.3 2.4 %collective-permute-start.7 = (bf16[4,288,128]{2,1,0:T(8,128)(2,1)S(1)}, bf16[4,288,128]{2,1,0:T(8,128)(2,1)S(1)}, u32[]{:S(2)}, u32[]{:S(2)}) collective-permute-start(bf16[4,288,128]{2,1,0:T(8,128)(2,1)S(1)} %pad_maximum_fusion.3), channel_id=1, source_target_pairs={{0,12},{1,13},{2,14},{3,15},{4,8},{5,9},{6,10},{7,11},{8,4},{9,5},... | collective-permute-start | bytes 884744 | tf_op jit(solution)/shard_map/ppermute | solution.py:45
  78.7 0.7 select_reduce_fusion.1
  79.4 12.8 %collective-permute-done.7 = bf16[4,288,128]{2,1,0:T(8,128)(2,1)S(1)} collective-permute-done((bf16[4,288,128]{2,1,0:T(8,128)(2,1)S(1)}, bf16[4,288,128]{2,1,0:T(8,128)(2,1)S(1)}, u32[]{:S(2)}, u32[]{:S(2)}) %collective-permute-start.7) | collective-permute-done | bytes 294944 | tf_op jit(solution)/shard_map/ppermute | solution.py:45
  92.3 0.1 collective-permute-start.8
  92.4 3.7 %collective-permute-start.9 = (bf16[1,272,128]{2,1,0:T(8,128)(2,1)S(1)}, bf16[1,272,128]{2,1,0:T(8,128)(2,1)S(1)}, u32[]{:S(2)}, u32[]{:S(2)}) collective-permute-start(bf16[1,272,128]{2,1,0:T(8,128)(2,1)S(1)} %maximum_bitcast_fusion.1), channel_id=1, source_target_pairs={{0,64},{16,80},{32,96},{48,112},{64,0},{80,16},{96,32},{112,48},{1... | collective-permute-start | bytes 208904 | tf_op jit(solution)/shard_map/ppermute | solution.py:45
  96.1 2.7 %collective-permute-done.9 = bf16[1,272,128]{2,1,0:T(8,128)(2,1)S(1)} collective-permute-done((bf16[1,272,128]{2,1,0:T(8,128)(2,1)S(1)}, bf16[1,272,128]{2,1,0:T(8,128)(2,1)S(1)}, u32[]{:S(2)}, u32[]{:S(2)}) %collective-permute-start.9) | collective-permute-done | bytes 69664 | tf_op jit(solution)/shard_map/ppermute | solution.py:45
  98.9 0.1 constant_dynamic-update-slice_fusion.q
  99.0 1.0 copy-done.8
  100.0 17.0 %paged_attention.1 = bf16[16,272,128]{2,1,0:T(8,128)(2,1)} custom-call(s32[17]{0:T(128)} %copy-done.17, s32[256]{0:T(256)} %get-tuple-element.59.slot_page, s32[256]{0:T(256)} %get-tuple-element.58.slot_live, s32[16]{0:T(128)} %fusion.12.where, bf16[16,288,128]{2,1,0:T(8,128)(2,1)} %copy-done.8, bf16[128,16,2048]{2,1,0:T(8,128)(2,1)} %cache.1), custom_call_target="tpu_custom_call" | custom-call | flops 2000000000 | bytes 12582912 | tf_op jit(solution)/shard_map/paged_attention/pallas_call | solution.py:485
  117.1 0.1 collective-permute-start.10
  117.2 0.6 reshape.274.gain
  117.9 0.1 lt.102
  118.0 0.9 convert_reduce_fusion
  118.9 3.3 %collective-permute-done.10 = bf16[2,272,128]{2,1,0:T(8,128)(2,1)S(1)} collective-permute-done((bf16[2,272,128]{2,1,0:T(8,128)(2,1)S(1)}, bf16[2,272,128]{2,1,0:T(8,128)(2,1)S(1)}, u32[]{:S(2)}, u32[]{:S(2)}) %collective-permute-start.10) | collective-permute-done | bytes 139296 | tf_op jit(solution)/shard_map/ppermute | solution.py:45
  122.2 2.2 %collective-permute-start.11 = (bf16[4,272,128]{2,1,0:T(8,128)(2,1)S(1)}, bf16[4,272,128]{2,1,0:T(8,128)(2,1)S(1)}, u32[]{:S(2)}, u32[]{:S(2)}) collective-permute-start(bf16[4,272,128]{2,1,0:T(8,128)(2,1)S(1)} %pad_maximum_fusion.4), channel_id=1, source_target_pairs={{0,48},{16,32},{32,16},{48,0},{64,112},{80,96},{96,80},{112,64},{1... | collective-permute-start | bytes 835592 | tf_op jit(solution)/shard_map/ppermute | solution.py:45
  124.4 0.6 slice_add_fusion.ssq
  125.0 5.7 %all-to-all-start.1 = ((bf16[16,272,128]{2,1,0:T(8,128)(2,1)}), bf16[16,272,128]{2,1,0:T(8,128)(2,1)S(1)}, u32[]{:S(2)}, u32[]{:S(2)}) async-start(bf16[16,272,128]{2,1,0:T(8,128)(2,1)} %paged_attention.1), calls=%async_computation.1 | async-start | bytes 2228224 | tf_op jit(solution)/shard_map/all_to_all | solution.py:778
  130.9 0.1 dynamic-slice_convert_fusion
  131.0 0.3 select_reduce_fusion
  131.3 0.1 lt.121
  131.4 0.1 lt.122
  131.6 0.1 broadcast_in_dim.153
  131.7 0.1 broadcast_in_dim.154
  131.8 0.6 compare_select_fusion.token_row
  132.4 2.1 %all-gather.3.cloned.1.call-done = bf16[16384,512]{1,0:T(8,128)(2,1)} async-done(((bf16[1024,512]{1,0:T(8,128)(2,1)}), bf16[16384,512]{1,0:T(8,128)(2,1)}) %all-gather.3.cloned.1.call-update) | async-done | bytes 16777232 | tf_op jit(solution)/shard_map/all_gather | solution.py:731
  134.5 22.5 %keys_and_fresh_pages.1 = (bf16[1024,512]{1,0:T(8,128)(2,1)}, bf16[1024,128]{1,0:T(8,128)(2,1)}, bf16[1024,128]{1,0:T(8,128)(2,1)}, bf16[8,272,128]{2,1,0:T(8,128)(2,1)}) custom-call(s32[1]{0:T(128)} %bitcast.core, s32[8]{0:T(128)} %copy-done.14, s32[8]{0:T(128)} %copy-done.15, bf16[16,1024,512]{2,1,0:T(8,128)(2,1)} %bitcast.52, ...), custom_call_target="tpu_custom_call" | custom-call | flops 6000000000 | bytes 20971520 | tf_op jit(solution)/shard_map/keys_and_fresh_pages/pallas_call | solution.py:367
  157.0 11.7 %all-to-all-start.2 = ((bf16[8,272,128]{2,1,0:T(8,128)(2,1)}), bf16[8,272,128]{2,1,0:T(8,128)(2,1)S(1)}, u32[]{:S(2)}, u32[]{:S(2)}) async-start(bf16[8,272,128]{2,1,0:T(8,128)(2,1)} %get-tuple-element.51), calls=%async_computation.2 | async-start | bytes 1114112 | tf_op jit(solution)/shard_map/all_to_all | solution.py:803
  168.8 3.4 %merge_held_pages.1 = (f32[256,128]{1,0:T(8,128)S(1)}, f32[256,128]{1,0:T(8,128)S(1)}, f32[256,128]{1,0:T(8,128)S(1)}) custom-call(bf16[16,272,128]{2,1,0:T(8,128)(2,1)S(1)} %all-to-all-done.1.held, bf16[256,128]{1,0:T(8,128)(2,1)S(1)} %bitcast.50, bf16[64,128]{1,0:T(8,128)(2,1)S(1)} %get-tuple-element.63.new_keys, ...), custom_call_target="tpu_custom_call" | custom-call | flops 10000000 | bytes 2097152 | tf_op jit(solution)/shard_map/merge_held_pages/pallas_call | solution.py:581
  172.2 8.6 %prefill_attention.1 = bf16[1024,512]{1,0:T(8,128)(2,1)} custom-call(s32[1,8]{1,0:T(1,128)S(1)} %copy-done.6, bf16[1024,512]{1,0:T(8,128)(2,1)S(1)} %copy-done.1, bf16[1024,128]{1,0:T(8,128)(2,1)S(1)} %copy-done.2, bf16[1024,128]{1,0:T(8,128)(2,1)S(1)} %copy-done.3), custom_call_target="tpu_custom_call" | custom-call | flops 3000000000 | bytes 3145728 | tf_op jit(solution)/shard_map/prefill_attention/pallas_call | solution.py:399
  180.8 1.6 decode_merge.1
  182.5 0.6 copy.27
  (88 shorter events, 1.1 us)
Async XLA Ops:
  7.2 10.7 %copy-start.10 = (bf16[4,16,512]{2,1,0:T(8,128)(2,1)S(1)}, bf16[4,16,512]{2,1,0:T(8,128)(2,1)}, u32[]{:S(2)}) copy-start(bf16[4,16,512]{2,1,0:T(8,128)(2,1)} %param.24) | copy-start | bytes 196612
  9.5 22.3 %copy-start = (bf16[1024,512]{1,0:T(8,128)(2,1)S(1)}, bf16[1024,512]{1,0:T(8,128)(2,1)}, u32[]{:S(2)}) copy-start(bf16[1024,512]{1,0:T(8,128)(2,1)} %text.1) | copy-start | bytes 3145732
  9.5 22.3 %all-to-all-start = ((bf16[8,80,512]{2,1,0:T(8,128)(2,1)}), bf16[8,80,512]{2,1,0:T(8,128)(2,1)S(1)}, u32[]{:S(2)}, u32[]{:S(2)}) async-start(bf16[8,80,512]{2,1,0:T(8,128)(2,1)} %pick_rows.1), calls=%async_computation | async-start | bytes 1310720 | tf_op jit(solution)/shard_map/all_to_all | solution.py:727
  17.8 116.6 %all-gather.3.cloned.1.call-start = ((), (), s32[]{:S(2)}) async-start(), calls=%async_computation.3 | async-start | bytes 17825792 | tf_op jit(solution)/shard_map/all_gather | solution.py:731
  17.8 8.9 %collective-permute-start = (bf16[1,64,512]{2,1,0:T(8,128)(2,1)S(1)}, bf16[1,64,512]{2,1,0:T(8,128)(2,1)S(1)}, u32[]{:S(2)}, u32[]{:S(2)}) collective-permute-start(bf16[1,64,512]{2,1,0:T(8,128)(2,1)S(1)} %bitcast.53), channel_id=1, source_target_pairs={{0,2},{1,3},{2,0},{3,1},{4,6},{5,7},{6,4},{7,5},{8,10},{9,11},{10,... | collective-permute-start | bytes 196616 | tf_op jit(solution)/shard_map/ppermute | solution.py:45
  26.8 5.0 %collective-permute-start.1 = (bf16[2,64,512]{2,1,0:T(8,128)(2,1)S(1)}, bf16[2,64,512]{2,1,0:T(8,128)(2,1)S(1)}, u32[]{:S(2)}, u32[]{:S(2)}) collective-permute-start(bf16[2,64,512]{2,1,0:T(8,128)(2,1)S(1)} %pad_maximum_fusion.8), channel_id=1, source_target_pairs={{0,4},{1,5},{2,6},{3,7},{4,0},{5,1},{6,2},{7,3},{8,12},{9,13},{10,... | collective-permute-start | bytes 393224 | tf_op jit(solution)/shard_map/ppermute | solution.py:45
  31.9 2.7 %copy-start.16 = (s32[64]{0:T(128)S(1)}, s32[64]{0:T(128)}, u32[]{:S(2)}) copy-start(s32[64]{0:T(128)} %param.20) | copy-start | bytes 772
  31.9 2.7 %copy-start.19 = (s32[8]{0:T(128)S(1)}, s32[8]{0:T(128)}, u32[]{:S(2)}) copy-start(s32[8]{0:T(128)} %constant.169.clone) | copy-start | bytes 100
  31.9 2.9 %copy-start.18 = (s32[4]{0:T(128)S(1)}, s32[4]{0:T(128)}, u32[]{:S(2)}) copy-start(s32[4]{0:T(128)} %constant.168.clone) | copy-start | bytes 52
  31.9 3.4 %copy-start.11 = (bf16[8192]{0:T(1024)(128)(2,1)S(1)}, bf16[8192]{0:T(1024)(128)(2,1)}, u32[]{:S(2)}) copy-start(bf16[8192]{0:T(1024)(128)(2,1)} %param.25) | copy-start | bytes 49156
  33.8 5.2 %copy-start.4 = (s32[16,256]{1,0:T(8,128)S(1)}, s32[16,256]{1,0:T(8,128)}, u32[]{:S(2)}) copy-start(s32[16,256]{1,0:T(8,128)} %table.1) | copy-start | bytes 49156
  33.8 5.2 %copy-start.5 = (s32[16]{0:T(128)S(1)}, s32[16]{0:T(128)}, u32[]{:S(2)}) copy-start(s32[16]{0:T(128)} %length.1) | copy-start | bytes 196
  33.8 15.6 %collective-permute-start.4 = (bf16[8192,128]{1,0:T(8,128)(2,1)}, bf16[8192,128]{1,0:T(8,128)(2,1)S(1)}, u32[]{:S(2)}, u32[]{:S(2)}) collective-permute-start(bf16[8192,128]{1,0:T(8,128)(2,1)} %wa.3), channel_id=1, source_target_pairs={{0,1},{1,0},{2,3},{3,2},{4,5},{5,4},{6,7},{7,6},{8,9},{9,8},{10,11... | collective-permute-start | bytes 6291464 | tf_op jit(solution)/shard_map/ppermute | solution.py:45
  34.6 96.4 %copy-start.15 = (s32[8]{0:T(128)}, s32[8]{0:T(128)S(1)}, u32[]{:S(2)}) copy-start(s32[8]{0:T(128)S(1)} %broadcast_xor_fusion.1.group) | copy-start | bytes 100
  34.8 82.4 %copy-start.14 = (s32[8]{0:T(128)}, s32[8]{0:T(128)S(1)}, u32[]{:S(2)}) copy-start(s32[8]{0:T(128)S(1)} %broadcast_minimum_fusion.start) | copy-start | bytes 100
  37.4 8.7 %collective-permute-start.2 = (bf16[4,64,512]{2,1,0:T(8,128)(2,1)S(1)}, bf16[4,64,512]{2,1,0:T(8,128)(2,1)S(1)}, u32[]{:S(2)}, u32[]{:S(2)}) collective-permute-start(bf16[4,64,512]{2,1,0:T(8,128)(2,1)S(1)} %pad_maximum_fusion.5), channel_id=1, source_target_pairs={{0,12},{1,13},{2,14},{3,15},{4,8},{5,9},{6,10},{7,11},{8,4},{9,5},... | collective-permute-start | bytes 786440 | tf_op jit(solution)/shard_map/ppermute | solution.py:45
  46.1 2.2 %collective-permute-start.3 = (bf16[8,64,512]{2,1,0:T(8,128)(2,1)S(1)}, bf16[8,64,512]{2,1,0:T(8,128)(2,1)S(1)}, u32[]{:S(2)}, u32[]{:S(2)}) collective-permute-start(bf16[8,64,512]{2,1,0:T(8,128)(2,1)S(1)} %pad_maximum_fusion.2), channel_id=1, source_target_pairs={{0,1},{1,0},{2,3},{3,2},{4,5},{5,4},{6,7},{7,6},{8,9},{9,8},{10,11... | collective-permute-start | bytes 1572872 | tf_op jit(solution)/shard_map/ppermute | solution.py:45
  49.4 1.3 copy-start.7
  60.7 4.6 %collective-permute-start.5 = (bf16[1,288,128]{2,1,0:T(8,128)(2,1)S(1)}, bf16[1,288,128]{2,1,0:T(8,128)(2,1)S(1)}, u32[]{:S(2)}, u32[]{:S(2)}) collective-permute-start(bf16[1,288,128]{2,1,0:T(8,128)(2,1)S(1)} %maximum_bitcast_fusion), channel_id=1, source_target_pairs={{0,2},{1,3},{2,0},{3,1},{4,6},{5,7},{6,4},{7,5},{8,10},{9,11},{10,... | collective-permute-start | bytes 221192 | tf_op jit(solution)/shard_map/ppermute | solution.py:45
  62.4 33.6 %copy-start.17 = (s32[17]{0:T(128)}, s32[17]{0:T(128)S(1)}, u32[]{:S(2)}) copy-start(s32[17]{0:T(128)S(1)} %select_reduce_fusion.4.first_chunk) | copy-start | bytes 208
  65.3 10.9 %collective-permute-start.6 = (bf16[2,288,128]{2,1,0:T(8,128)(2,1)S(1)}, bf16[2,288,128]{2,1,0:T(8,128)(2,1)S(1)}, u32[]{:S(2)}, u32[]{:S(2)}) collective-permute-start(bf16[2,288,128]{2,1,0:T(8,128)(2,1)S(1)} %pad_maximum_fusion.6), channel_id=1, source_target_pairs={{0,4},{1,5},{2,6},{3,7},{4,0},{5,1},{6,2},{7,3},{8,12},{9,13},{10,... | collective-permute-start | bytes 442376 | tf_op jit(solution)/shard_map/ppermute | solution.py:45
  76.3 15.9 %collective-permute-start.7 = (bf16[4,288,128]{2,1,0:T(8,128)(2,1)S(1)}, bf16[4,288,128]{2,1,0:T(8,128)(2,1)S(1)}, u32[]{:S(2)}, u32[]{:S(2)}) collective-permute-start(bf16[4,288,128]{2,1,0:T(8,128)(2,1)S(1)} %pad_maximum_fusion.3), channel_id=1, source_target_pairs={{0,12},{1,13},{2,14},{3,15},{4,8},{5,9},{6,10},{7,11},{8,4},{9,5},... | collective-permute-start | bytes 884744 | tf_op jit(solution)/shard_map/ppermute | solution.py:45
  92.3 6.6 %collective-permute-start.8 = (bf16[8,288,128]{2,1,0:T(8,128)(2,1)S(1)}, bf16[8,288,128]{2,1,0:T(8,128)(2,1)S(1)}, u32[]{:S(2)}, u32[]{:S(2)}) collective-permute-start(bf16[8,288,128]{2,1,0:T(8,128)(2,1)S(1)} %pad_maximum_fusion.1), channel_id=1, source_target_pairs={{0,1},{1,0},{2,3},{3,2},{4,5},{5,4},{6,7},{7,6},{8,9},{9,8},{10,11... | collective-permute-start | bytes 1769480 | tf_op jit(solution)/shard_map/ppermute | solution.py:45
  92.4 6.4 %collective-permute-start.9 = (bf16[1,272,128]{2,1,0:T(8,128)(2,1)S(1)}, bf16[1,272,128]{2,1,0:T(8,128)(2,1)S(1)}, u32[]{:S(2)}, u32[]{:S(2)}) collective-permute-start(bf16[1,272,128]{2,1,0:T(8,128)(2,1)S(1)} %maximum_bitcast_fusion.1), channel_id=1, source_target_pairs={{0,64},{16,80},{32,96},{48,112},{64,0},{80,16},{96,32},{112,48},{1... | collective-permute-start | bytes 208904 | tf_op jit(solution)/shard_map/ppermute | solution.py:45
  99.0 1.0 copy-start.8
  117.1 5.1 %collective-permute-start.10 = (bf16[2,272,128]{2,1,0:T(8,128)(2,1)S(1)}, bf16[2,272,128]{2,1,0:T(8,128)(2,1)S(1)}, u32[]{:S(2)}, u32[]{:S(2)}) collective-permute-start(bf16[2,272,128]{2,1,0:T(8,128)(2,1)S(1)} %pad_maximum_fusion.7), channel_id=1, source_target_pairs={{0,16},{16,0},{32,48},{48,32},{64,80},{80,64},{96,112},{112,96},{1... | collective-permute-start | bytes 417800 | tf_op jit(solution)/shard_map/ppermute | solution.py:45
  122.2 8.5 %collective-permute-start.11 = (bf16[4,272,128]{2,1,0:T(8,128)(2,1)S(1)}, bf16[4,272,128]{2,1,0:T(8,128)(2,1)S(1)}, u32[]{:S(2)}, u32[]{:S(2)}) collective-permute-start(bf16[4,272,128]{2,1,0:T(8,128)(2,1)S(1)} %pad_maximum_fusion.4), channel_id=1, source_target_pairs={{0,48},{16,32},{32,16},{48,0},{64,112},{80,96},{96,80},{112,64},{1... | collective-permute-start | bytes 835592 | tf_op jit(solution)/shard_map/ppermute | solution.py:45
  125.0 32.0 %all-to-all-start.1 = ((bf16[16,272,128]{2,1,0:T(8,128)(2,1)}), bf16[16,272,128]{2,1,0:T(8,128)(2,1)S(1)}, u32[]{:S(2)}, u32[]{:S(2)}) async-start(bf16[16,272,128]{2,1,0:T(8,128)(2,1)} %paged_attention.1), calls=%async_computation.1 | async-start | bytes 2228224 | tf_op jit(solution)/shard_map/all_to_all | solution.py:778
  130.8 3.6 %copy-start.9 = (bf16[8,272,128]{2,1,0:T(8,128)(2,1)}, bf16[8,272,128]{2,1,0:T(8,128)(2,1)S(1)}, u32[]{:S(2)}) copy-start(bf16[8,272,128]{2,1,0:T(8,128)(2,1)S(1)} %constant_dynamic-update-slice_fusion.5.q) | copy-start | bytes 1671172
  134.4 34.3 %copy-start.12 = (bf16[64,128]{1,0:T(8,128)(2,1)S(1)}, bf16[64,128]{1,0:T(8,128)(2,1)}, u32[]{:S(2)}) copy-start(bf16[64,128]{1,0:T(8,128)(2,1)} %get-tuple-element.53) | copy-start | bytes 49156
  134.5 34.3 %copy-start.13 = (bf16[64,128]{1,0:T(8,128)(2,1)S(1)}, bf16[64,128]{1,0:T(8,128)(2,1)}, u32[]{:S(2)}) copy-start(bf16[64,128]{1,0:T(8,128)(2,1)} %get-tuple-element.54) | copy-start | bytes 49156
  157.0 15.1 %copy-start.1 = (bf16[1024,512]{1,0:T(8,128)(2,1)S(1)}, bf16[1024,512]{1,0:T(8,128)(2,1)}, u32[]{:S(2)}) copy-start(bf16[1024,512]{1,0:T(8,128)(2,1)} %get-tuple-element.46.q) | copy-start | bytes 3145732
  157.0 15.1 %copy-start.2 = (bf16[1024,128]{1,0:T(8,128)(2,1)S(1)}, bf16[1024,128]{1,0:T(8,128)(2,1)}, u32[]{:S(2)}) copy-start(bf16[1024,128]{1,0:T(8,128)(2,1)} %get-tuple-element.47.keys) | copy-start | bytes 786436
  157.0 15.1 %copy-start.6 = (s32[1,8]{1,0:T(1,128)S(1)}, s32[1,8]{1,0:T(1,128)}, u32[]{:S(2)}) copy-start(s32[1,8]{1,0:T(1,128)} %blocks_ref.1) | copy-start | bytes 100
  157.0 23.8 %all-to-all-start.2 = ((bf16[8,272,128]{2,1,0:T(8,128)(2,1)}), bf16[8,272,128]{2,1,0:T(8,128)(2,1)S(1)}, u32[]{:S(2)}, u32[]{:S(2)}) async-start(bf16[8,272,128]{2,1,0:T(8,128)(2,1)} %get-tuple-element.51), calls=%async_computation.2 | async-start | bytes 1114112 | tf_op jit(solution)/shard_map/all_to_all | solution.py:803
  168.7 3.4 %copy-start.3 = (bf16[1024,128]{1,0:T(8,128)(2,1)S(1)}, bf16[1024,128]{1,0:T(8,128)(2,1)}, u32[]{:S(2)}) copy-start(bf16[1024,128]{1,0:T(8,128)(2,1)} %get-tuple-element.48.values) | copy-start | bytes 786436
Sparse Core Ops, SparseCore 0:
  34.0 100.4 all-gather.2

commit v3 on v2

--- a/solution.py
+++ b/solution.py
@@ -296,7 +296,7 @@
         )
 
 
-def all_blocks(text, gain, weights, scale, xbuf, wbuf, xsem, wsem, acc):
+def all_blocks(text, ssq, gain, weights, scale, xbuf, wbuf, xsem, wsem, acc):
     blocks, rows = text.shape[0], text.shape[1]
     widths = [weight.shape[1] for weight in weights]
 
@@ -311,13 +311,15 @@
                 pltpu.make_async_copy(rows_of, part(n, k), wsem.at[n, k]).start()
 
     fetch(0)
+    fetch(1)
+    row_factors(ssq, 0, scale)
     for i in range(blocks // 4):
         for n in range(4 * i, 4 * i + 4):
             pltpu.make_async_copy(xbuf.at[n], xbuf.at[n], xsem.at[n]).wait()
             for k in range(len(weights)):
                 pltpu.make_async_copy(part(n, k), part(n, k), wsem.at[n, k]).wait()
-        if i + 1 < blocks // 4:
-            fetch(i + 1)
+        if i + 2 < blocks // 4:
+            fetch(i + 2)
         gains = [gain[4 * i + k].astype(F32) for k in range(4)]
         for r in range(rows // 256):
             at = slice(r * 256, (r + 1) * 256)
@@ -351,8 +353,7 @@
     core, start, group, text, ssq, gain, wq, wa, wb, q, token_row,
     queries, keys, values, out, xbuf, wbuf, scale, xsem, wsem, acc,
 ):
-    row_factors(ssq, 0, scale)
-    all_blocks(text, gain, (wq, wa, wb), scale, xbuf, wbuf, xsem, wsem, acc)
+    all_blocks(text, ssq, gain, (wq, wa, wb), scale, xbuf, wbuf, xsem, wsem, acc)
     for n in range(acc.shape[0] // 256):
         at = slice(n * 256, (n + 1) * 256)
         queries[at, :] = acc[at, :512].astype(BF)

time: 189 us -> 190 us (level)
  transfers between devices with their start and end apart: 16 -> 16, of which waited for: 10 -> 11; matrix products, arithmetic and copies ran while one was open for 6% -> 6% of each run, Pallas kernels for 33% -> 33%
where the time goes in v3:
time: 190 us
  Pallas kernels  67.7 us (36%)
  waiting for transfers between devices  51.5 us (27%)
  starting transfers between devices  41.7 us (22%)
  between operations  14.5 us (8%)
  other arithmetic  7.49 us (4%)
  local copies, waits for them, and re-layouts  6.72 us (4%)
    ppermute x12, waiting for transfers between devices, swap(): return lax.ppermute(x, axis, [(i, i ^ mask) for i in range(size)])  49.9 us
    pallas_call x1, Pallas kernels, finish_keys(): pl.pallas_call(keys_kernel, in_specs=[smem()] * 3 + [hbm()] + [vmem()] *...  23.1 us
    ppermute x12, starting transfers between devices, swap(): return lax.ppermute(x, axis, [(i, i ^ mask) for i in range(size)])  16.7 us
    pallas_call x1, Pallas kernels, paged_attention(): pl.pallas_call(paged_kernel, in_specs=[smem()] * 4 + [vmem(), hbm()], out...  15.7 us
    all_to_all x1, starting transfers between devices, per_device(): lax.all_to_all(fresh, 'role', split_axis=0, concat_axis=0, tiled=True)  10.9 us
    pallas_call x1, Pallas kernels, step_project(): pl.pallas_call(step_kernel, grid_spec=pltpu.PrefetchScalarGridSpec(num_sc...  9.08 us
    pallas_call x1, Pallas kernels, prefill_attention(): pl.pallas_call(attend_kernel, in_specs=[smem()] + [vmem()] * 3, out_specs...  8.62 us
    all_to_all x1, starting transfers between devices, per_device(): lax.all_to_all(message, 'role', split_axis=0, concat_axis=0, tiled=True)  8.29 us
  transfers between devices with their start and end apart: 16, of which 11 were waited for; matrix products, arithmetic and copies ran while one was open for 6% of the time, Pallas kernels for 33%

profile of v3, /device:TPU:10, one launch (start us, length us, event | category | flops | bytes accessed | tf_op | source)
XLA Modules:
  0.0 189.7 jit_solution(2934180231363122012)
XLA Ops:
  7.2 2.3 %pick_rows.1 = bf16[8,80,512]{2,1,0:T(8,128)(2,1)} custom-call(s32[1,256]{1,0:T(1,128)} %bitcast.60, s32[1,256]{1,0:T(1,128)} %bitcast.61, s32[1,64]{1,0:T(1,128)} %bitcast.62, bf16[256,512]{1,0:T(8,128)(2,1)} %rows_in.1), custom_call_target="tpu_custom_call" | custom-call | flops 200000000 | bytes 1048576 | tf_op jit(solution)/shard_map/pick_rows/pallas_call | solution.py:158
  9.5 8.3 %all-to-all-start = ((bf16[8,80,512]{2,1,0:T(8,128)(2,1)}), bf16[8,80,512]{2,1,0:T(8,128)(2,1)S(1)}, u32[]{:S(2)}, u32[]{:S(2)}) async-start(bf16[8,80,512]{2,1,0:T(8,128)(2,1)} %pick_rows.1), calls=%async_computation | async-start | bytes 1310720 | tf_op jit(solution)/shard_map/all_to_all | solution.py:728
  17.8 1.1 collective-permute-start
  18.9 7.8 %collective-permute-done = bf16[1,64,512]{2,1,0:T(8,128)(2,1)S(1)} collective-permute-done((bf16[1,64,512]{2,1,0:T(8,128)(2,1)S(1)}, bf16[1,64,512]{2,1,0:T(8,128)(2,1)S(1)}, u32[]{:S(2)}, u32[]{:S(2)}) %collective-permute-start) | collective-permute-done | bytes 65568 | tf_op jit(solution)/shard_map/ppermute | solution.py:45
  26.8 0.5 collective-permute-start.1
  27.3 4.5 %collective-permute-done.1 = bf16[2,64,512]{2,1,0:T(8,128)(2,1)S(1)} collective-permute-done((bf16[2,64,512]{2,1,0:T(8,128)(2,1)S(1)}, bf16[2,64,512]{2,1,0:T(8,128)(2,1)S(1)}, u32[]{:S(2)}, u32[]{:S(2)}) %collective-permute-start.1) | collective-permute-done | bytes 131104 | tf_op jit(solution)/shard_map/ppermute | solution.py:45
  31.9 1.9 %land_rows.1 = (bf16[1024,512]{1,0:T(8,128)(2,1)}, bf16[32,128]{1,0:T(8,128)(2,1)S(1)}) custom-call(s32[1]{0:T(128)} %bitcast.1.role, bf16[8,80,512]{2,1,0:T(8,128)(2,1)S(1)} %all-to-all-done.arrived, bf16[1024,512]{1,0:T(8,128)(2,1)S(1)} %copy-done), custom_call_target="tpu_custom_call" | custom-call | flops 1000000000 | bytes 6291456 | tf_op jit(solution)/shard_map/land_rows/pallas_call | solution.py:205
  33.8 0.1 collective-permute-start.4
  34.0 0.6 fusion.12.where
  34.6 0.2 select_reduce_fusion.5
  34.8 0.5 broadcast_xor_fusion.order
  35.3 0.6 reshape.273.gain
  36.0 0.5 broadcast.273
  36.6 0.7 fusion.18
  37.4 1.6 collective-permute-start.2
  39.0 2.0 %find_pages.1 = (s32[1,640]{1,0:T(1,128)S(1)}, s32[1,640]{1,0:T(1,128)S(1)}) custom-call(s32[16,256]{1,0:T(8,128)S(1)} %copy-done.4, s32[16]{0:T(128)S(1)} %copy-done.5, f32[1,640]{1,0:T(1,128)S(1)} %add_convert_fusion.pages), custom_call_target="tpu_custom_call" | custom-call | flops 10000000 | bytes 65536 | tf_op jit(solution)/shard_map/find_pages/pallas_call | solution.py:644
  41.0 0.2 compare_reduce_fusion
  41.1 0.1 convert_reduce_fusion.2
  41.3 4.8 %collective-permute-done.2 = bf16[4,64,512]{2,1,0:T(8,128)(2,1)S(1)} collective-permute-done((bf16[4,64,512]{2,1,0:T(8,128)(2,1)S(1)}, bf16[4,64,512]{2,1,0:T(8,128)(2,1)S(1)}, u32[]{:S(2)}, u32[]{:S(2)}) %collective-permute-start.2) | collective-permute-done | bytes 262176 | tf_op jit(solution)/shard_map/ppermute | solution.py:45
  46.1 0.1 collective-permute-start.3
  46.3 2.0 %collective-permute-done.3 = bf16[8,64,512]{2,1,0:T(8,128)(2,1)S(1)} collective-permute-done((bf16[8,64,512]{2,1,0:T(8,128)(2,1)S(1)}, bf16[8,64,512]{2,1,0:T(8,128)(2,1)S(1)}, u32[]{:S(2)}, u32[]{:S(2)}) %collective-permute-start.3) | collective-permute-done | bytes 524320 | tf_op jit(solution)/shard_map/ppermute | solution.py:45
  48.3 1.1 pad_maximum_fusion.xs
  49.4 1.3 copy-done.7
  50.7 9.1 %step_project.1 = (bf16[64,512]{1,0:T(8,128)(2,1)}, bf16[64,128]{1,0:T(8,128)(2,1)}, bf16[64,128]{1,0:T(8,128)(2,1)}) custom-call(s32[4]{0:T(128)} %broadcast_xor_fusion.order, s32[1]{0:T(128)} %bitcast.14.low, bf16[16,64,512]{2,1,0:T(8,128)(2,1)} %pad_maximum_fusion.xs, bf16[4,4,1,512]{3,2,1,0:T(2,128)(2,1)} %reshape.273.gain, bf16[8192,512]{1,0:T(8,128)(2,1)} %wq.3, ...), custom_call_target="tpu_custom_call" | custom-call | flops 805306368 | bytes 14680064 | tf_op jit(solution)/shard_map/step_project/pallas_call | solution.py:259
  59.8 0.9 reshape.264
  60.7 1.6 collective-permute-start.5
  62.3 0.1 select_reduce_fusion.4.first_chunk
  62.4 2.9 %collective-permute-done.5 = bf16[1,288,128]{2,1,0:T(8,128)(2,1)S(1)} collective-permute-done((bf16[1,288,128]{2,1,0:T(8,128)(2,1)S(1)}, bf16[1,288,128]{2,1,0:T(8,128)(2,1)S(1)}, u32[]{:S(2)}, u32[]{:S(2)}) %collective-permute-start.5) | collective-permute-done | bytes 73760 | tf_op jit(solution)/shard_map/ppermute | solution.py:45
  65.3 3.5 %collective-permute-start.6 = (bf16[2,288,128]{2,1,0:T(8,128)(2,1)S(1)}, bf16[2,288,128]{2,1,0:T(8,128)(2,1)S(1)}, u32[]{:S(2)}, u32[]{:S(2)}) collective-permute-start(bf16[2,288,128]{2,1,0:T(8,128)(2,1)S(1)} %pad_maximum_fusion.6), channel_id=1, source_target_pairs={{0,4},{1,5},{2,6},{3,7},{4,0},{5,1},{6,2},{7,3},{8,12},{9,13},{10,... | collective-permute-start | bytes 442376 | tf_op jit(solution)/shard_map/ppermute | solution.py:45
  68.9 0.1 select_reduce_fusion.3
  68.9 0.2 convert_reduce_fusion.1
  69.1 7.1 %collective-permute-done.6 = bf16[2,288,128]{2,1,0:T(8,128)(2,1)S(1)} collective-permute-done((bf16[2,288,128]{2,1,0:T(8,128)(2,1)S(1)}, bf16[2,288,128]{2,1,0:T(8,128)(2,1)S(1)}, u32[]{:S(2)}, u32[]{:S(2)}) %collective-permute-start.6) | collective-permute-done | bytes 147488 | tf_op jit(solution)/shard_map/ppermute | solution.py:45
  76.3 2.4 %collective-permute-start.7 = (bf16[4,288,128]{2,1,0:T(8,128)(2,1)S(1)}, bf16[4,288,128]{2,1,0:T(8,128)(2,1)S(1)}, u32[]{:S(2)}, u32[]{:S(2)}) collective-permute-start(bf16[4,288,128]{2,1,0:T(8,128)(2,1)S(1)} %pad_maximum_fusion.3), channel_id=1, source_target_pairs={{0,12},{1,13},{2,14},{3,15},{4,8},{5,9},{6,10},{7,11},{8,4},{9,5},... | collective-permute-start | bytes 884744 | tf_op jit(solution)/shard_map/ppermute | solution.py:45
  78.7 0.7 select_reduce_fusion.1
  79.4 12.8 %collective-permute-done.7 = bf16[4,288,128]{2,1,0:T(8,128)(2,1)S(1)} collective-permute-done((bf16[4,288,128]{2,1,0:T(8,128)(2,1)S(1)}, bf16[4,288,128]{2,1,0:T(8,128)(2,1)S(1)}, u32[]{:S(2)}, u32[]{:S(2)}) %collective-permute-start.7) | collective-permute-done | bytes 294944 | tf_op jit(solution)/shard_map/ppermute | solution.py:45
  92.3 0.1 collective-permute-start.8
  92.4 3.7 %collective-permute-start.9 = (bf16[1,272,128]{2,1,0:T(8,128)(2,1)S(1)}, bf16[1,272,128]{2,1,0:T(8,128)(2,1)S(1)}, u32[]{:S(2)}, u32[]{:S(2)}) collective-permute-start(bf16[1,272,128]{2,1,0:T(8,128)(2,1)S(1)} %maximum_bitcast_fusion.1), channel_id=1, source_target_pairs={{0,64},{16,80},{32,96},{48,112},{64,0},{80,16},{96,32},{112,48},{1... | collective-permute-start | bytes 208904 | tf_op jit(solution)/shard_map/ppermute | solution.py:45
  96.1 2.7 %collective-permute-done.9 = bf16[1,272,128]{2,1,0:T(8,128)(2,1)S(1)} collective-permute-done((bf16[1,272,128]{2,1,0:T(8,128)(2,1)S(1)}, bf16[1,272,128]{2,1,0:T(8,128)(2,1)S(1)}, u32[]{:S(2)}, u32[]{:S(2)}) %collective-permute-start.9) | collective-permute-done | bytes 69664 | tf_op jit(solution)/shard_map/ppermute | solution.py:45
  98.9 0.1 constant_dynamic-update-slice_fusion.q
  99.0 1.0 copy-done.8
  100.0 15.7 %paged_attention.1 = bf16[16,272,128]{2,1,0:T(8,128)(2,1)} custom-call(s32[17]{0:T(128)} %copy-done.17, s32[256]{0:T(256)} %get-tuple-element.59.slot_page, s32[256]{0:T(256)} %get-tuple-element.58.slot_live, s32[16]{0:T(128)} %fusion.12.where, bf16[16,288,128]{2,1,0:T(8,128)(2,1)} %copy-done.8, bf16[128,16,2048]{2,1,0:T(8,128)(2,1)} %cache.1), custom_call_target="tpu_custom_call" | custom-call | flops 2000000000 | bytes 12582912 | tf_op jit(solution)/shard_map/paged_attention/pallas_call | solution.py:486
  115.7 0.4 collective-permute-start.10
  116.2 0.6 reshape.274.gain
  116.8 0.1 lt.102
  116.9 0.9 convert_reduce_fusion
  117.8 4.4 %collective-permute-done.10 = bf16[2,272,128]{2,1,0:T(8,128)(2,1)S(1)} collective-permute-done((bf16[2,272,128]{2,1,0:T(8,128)(2,1)S(1)}, bf16[2,272,128]{2,1,0:T(8,128)(2,1)S(1)}, u32[]{:S(2)}, u32[]{:S(2)}) %collective-permute-start.10) | collective-permute-done | bytes 139296 | tf_op jit(solution)/shard_map/ppermute | solution.py:45
  122.2 1.7 collective-permute-start.11
  123.9 0.6 slice_add_fusion.ssq
  124.5 5.8 %all-to-all-start.1 = ((bf16[16,272,128]{2,1,0:T(8,128)(2,1)}), bf16[16,272,128]{2,1,0:T(8,128)(2,1)S(1)}, u32[]{:S(2)}, u32[]{:S(2)}) async-start(bf16[16,272,128]{2,1,0:T(8,128)(2,1)} %paged_attention.1), calls=%async_computation.1 | async-start | bytes 2228224 | tf_op jit(solution)/shard_map/all_to_all | solution.py:779
  130.4 0.8 collective-permute-done.11
  131.3 0.1 dynamic-slice_convert_fusion
  131.5 0.3 select_reduce_fusion
  131.8 0.1 lt.121
  131.9 0.1 lt.122
  132.0 0.1 broadcast_in_dim.153
  132.1 0.1 broadcast_in_dim.154
  132.2 0.6 compare_select_fusion.token_row
  132.8 1.6 all-gather.3.cloned.1.call-done
  134.5 23.1 %keys_and_fresh_pages.1 = (bf16[1024,512]{1,0:T(8,128)(2,1)}, bf16[1024,128]{1,0:T(8,128)(2,1)}, bf16[1024,128]{1,0:T(8,128)(2,1)}, bf16[8,272,128]{2,1,0:T(8,128)(2,1)}) custom-call(s32[1]{0:T(128)} %bitcast.core, s32[8]{0:T(128)} %copy-done.14, s32[8]{0:T(128)} %copy-done.15, bf16[16,1024,512]{2,1,0:T(8,128)(2,1)} %bitcast.52, ...), custom_call_target="tpu_custom_call" | custom-call | flops 6000000000 | bytes 20971520 | tf_op jit(solution)/shard_map/keys_and_fresh_pages/pallas_call | solution.py:368
  157.6 10.9 %all-to-all-start.2 = ((bf16[8,272,128]{2,1,0:T(8,128)(2,1)}), bf16[8,272,128]{2,1,0:T(8,128)(2,1)S(1)}, u32[]{:S(2)}, u32[]{:S(2)}) async-start(bf16[8,272,128]{2,1,0:T(8,128)(2,1)} %get-tuple-element.51), calls=%async_computation.2 | async-start | bytes 1114112 | tf_op jit(solution)/shard_map/all_to_all | solution.py:804
  168.5 3.4 %merge_held_pages.1 = (f32[256,128]{1,0:T(8,128)S(1)}, f32[256,128]{1,0:T(8,128)S(1)}, f32[256,128]{1,0:T(8,128)S(1)}) custom-call(bf16[16,272,128]{2,1,0:T(8,128)(2,1)S(1)} %all-to-all-done.1.held, bf16[256,128]{1,0:T(8,128)(2,1)S(1)} %bitcast.50, bf16[64,128]{1,0:T(8,128)(2,1)S(1)} %get-tuple-element.63.new_keys, ...), custom_call_target="tpu_custom_call" | custom-call | flops 10000000 | bytes 2097152 | tf_op jit(solution)/shard_map/merge_held_pages/pallas_call | solution.py:582
  171.9 8.6 %prefill_attention.1 = bf16[1024,512]{1,0:T(8,128)(2,1)} custom-call(s32[1,8]{1,0:T(1,128)S(1)} %copy-done.6, bf16[1024,512]{1,0:T(8,128)(2,1)S(1)} %copy-done.1, bf16[1024,128]{1,0:T(8,128)(2,1)S(1)} %copy-done.2, bf16[1024,128]{1,0:T(8,128)(2,1)S(1)} %copy-done.3), custom_call_target="tpu_custom_call" | custom-call | flops 3000000000 | bytes 3145728 | tf_op jit(solution)/shard_map/prefill_attention/pallas_call | solution.py:400
  180.5 1.6 decode_merge.1
  182.2 0.6 copy.27
  (88 shorter events, 1.2 us)
Async XLA Ops:
  7.2 10.7 %copy-start.10 = (bf16[4,16,512]{2,1,0:T(8,128)(2,1)S(1)}, bf16[4,16,512]{2,1,0:T(8,128)(2,1)}, u32[]{:S(2)}) copy-start(bf16[4,16,512]{2,1,0:T(8,128)(2,1)} %param.24) | copy-start | bytes 196612
  9.5 22.3 %copy-start = (bf16[1024,512]{1,0:T(8,128)(2,1)S(1)}, bf16[1024,512]{1,0:T(8,128)(2,1)}, u32[]{:S(2)}) copy-start(bf16[1024,512]{1,0:T(8,128)(2,1)} %text.1) | copy-start | bytes 3145732
  9.5 22.3 %all-to-all-start = ((bf16[8,80,512]{2,1,0:T(8,128)(2,1)}), bf16[8,80,512]{2,1,0:T(8,128)(2,1)S(1)}, u32[]{:S(2)}, u32[]{:S(2)}) async-start(bf16[8,80,512]{2,1,0:T(8,128)(2,1)} %pick_rows.1), calls=%async_computation | async-start | bytes 1310720 | tf_op jit(solution)/shard_map/all_to_all | solution.py:728
  17.8 116.6 %all-gather.3.cloned.1.call-start = ((), (), s32[]{:S(2)}) async-start(), calls=%async_computation.3 | async-start | bytes 17825792 | tf_op jit(solution)/shard_map/all_gather | solution.py:732
  17.8 8.9 %collective-permute-start = (bf16[1,64,512]{2,1,0:T(8,128)(2,1)S(1)}, bf16[1,64,512]{2,1,0:T(8,128)(2,1)S(1)}, u32[]{:S(2)}, u32[]{:S(2)}) collective-permute-start(bf16[1,64,512]{2,1,0:T(8,128)(2,1)S(1)} %bitcast.53), channel_id=1, source_target_pairs={{0,2},{1,3},{2,0},{3,1},{4,6},{5,7},{6,4},{7,5},{8,10},{9,11},{10,... | collective-permute-start | bytes 196616 | tf_op jit(solution)/shard_map/ppermute | solution.py:45
  26.8 5.0 %collective-permute-start.1 = (bf16[2,64,512]{2,1,0:T(8,128)(2,1)S(1)}, bf16[2,64,512]{2,1,0:T(8,128)(2,1)S(1)}, u32[]{:S(2)}, u32[]{:S(2)}) collective-permute-start(bf16[2,64,512]{2,1,0:T(8,128)(2,1)S(1)} %pad_maximum_fusion.8), channel_id=1, source_target_pairs={{0,4},{1,5},{2,6},{3,7},{4,0},{5,1},{6,2},{7,3},{8,12},{9,13},{10,... | collective-permute-start | bytes 393224 | tf_op jit(solution)/shard_map/ppermute | solution.py:45
  31.9 2.7 %copy-start.16 = (s32[64]{0:T(128)S(1)}, s32[64]{0:T(128)}, u32[]{:S(2)}) copy-start(s32[64]{0:T(128)} %param.20) | copy-start | bytes 772
  31.9 2.7 %copy-start.19 = (s32[8]{0:T(128)S(1)}, s32[8]{0:T(128)}, u32[]{:S(2)}) copy-start(s32[8]{0:T(128)} %constant.169.clone) | copy-start | bytes 100
  31.9 2.9 %copy-start.18 = (s32[4]{0:T(128)S(1)}, s32[4]{0:T(128)}, u32[]{:S(2)}) copy-start(s32[4]{0:T(128)} %constant.168.clone) | copy-start | bytes 52
  31.9 3.4 %copy-start.11 = (bf16[8192]{0:T(1024)(128)(2,1)S(1)}, bf16[8192]{0:T(1024)(128)(2,1)}, u32[]{:S(2)}) copy-start(bf16[8192]{0:T(1024)(128)(2,1)} %param.25) | copy-start | bytes 49156
  33.8 5.2 %copy-start.4 = (s32[16,256]{1,0:T(8,128)S(1)}, s32[16,256]{1,0:T(8,128)}, u32[]{:S(2)}) copy-start(s32[16,256]{1,0:T(8,128)} %table.1) | copy-start | bytes 49156
  33.8 5.2 %copy-start.5 = (s32[16]{0:T(128)S(1)}, s32[16]{0:T(128)}, u32[]{:S(2)}) copy-start(s32[16]{0:T(128)} %length.1) | copy-start | bytes 196
  33.8 15.6 %collective-permute-start.4 = (bf16[8192,128]{1,0:T(8,128)(2,1)}, bf16[8192,128]{1,0:T(8,128)(2,1)S(1)}, u32[]{:S(2)}, u32[]{:S(2)}) collective-permute-start(bf16[8192,128]{1,0:T(8,128)(2,1)} %wa.3), channel_id=1, source_target_pairs={{0,1},{1,0},{2,3},{3,2},{4,5},{5,4},{6,7},{7,6},{8,9},{9,8},{10,11... | collective-permute-start | bytes 6291464 | tf_op jit(solution)/shard_map/ppermute | solution.py:45
  34.6 96.8 %copy-start.15 = (s32[8]{0:T(128)}, s32[8]{0:T(128)S(1)}, u32[]{:S(2)}) copy-start(s32[8]{0:T(128)S(1)} %broadcast_xor_fusion.1.group) | copy-start | bytes 100
  34.8 81.3 %copy-start.14 = (s32[8]{0:T(128)}, s32[8]{0:T(128)S(1)}, u32[]{:S(2)}) copy-start(s32[8]{0:T(128)S(1)} %broadcast_minimum_fusion.start) | copy-start | bytes 100
  37.4 8.7 %collective-permute-start.2 = (bf16[4,64,512]{2,1,0:T(8,128)(2,1)S(1)}, bf16[4,64,512]{2,1,0:T(8,128)(2,1)S(1)}, u32[]{:S(2)}, u32[]{:S(2)}) collective-permute-start(bf16[4,64,512]{2,1,0:T(8,128)(2,1)S(1)} %pad_maximum_fusion.5), channel_id=1, source_target_pairs={{0,12},{1,13},{2,14},{3,15},{4,8},{5,9},{6,10},{7,11},{8,4},{9,5},... | collective-permute-start | bytes 786440 | tf_op jit(solution)/shard_map/ppermute | solution.py:45
  46.1 2.2 %collective-permute-start.3 = (bf16[8,64,512]{2,1,0:T(8,128)(2,1)S(1)}, bf16[8,64,512]{2,1,0:T(8,128)(2,1)S(1)}, u32[]{:S(2)}, u32[]{:S(2)}) collective-permute-start(bf16[8,64,512]{2,1,0:T(8,128)(2,1)S(1)} %pad_maximum_fusion.2), channel_id=1, source_target_pairs={{0,1},{1,0},{2,3},{3,2},{4,5},{5,4},{6,7},{7,6},{8,9},{9,8},{10,11... | collective-permute-start | bytes 1572872 | tf_op jit(solution)/shard_map/ppermute | solution.py:45
  49.4 1.3 copy-start.7
  60.7 4.6 %collective-permute-start.5 = (bf16[1,288,128]{2,1,0:T(8,128)(2,1)S(1)}, bf16[1,288,128]{2,1,0:T(8,128)(2,1)S(1)}, u32[]{:S(2)}, u32[]{:S(2)}) collective-permute-start(bf16[1,288,128]{2,1,0:T(8,128)(2,1)S(1)} %maximum_bitcast_fusion), channel_id=1, source_target_pairs={{0,2},{1,3},{2,0},{3,1},{4,6},{5,7},{6,4},{7,5},{8,10},{9,11},{10,... | collective-permute-start | bytes 221192 | tf_op jit(solution)/shard_map/ppermute | solution.py:45
  62.4 33.6 %copy-start.17 = (s32[17]{0:T(128)}, s32[17]{0:T(128)S(1)}, u32[]{:S(2)}) copy-start(s32[17]{0:T(128)S(1)} %select_reduce_fusion.4.first_chunk) | copy-start | bytes 208
  65.3 10.9 %collective-permute-start.6 = (bf16[2,288,128]{2,1,0:T(8,128)(2,1)S(1)}, bf16[2,288,128]{2,1,0:T(8,128)(2,1)S(1)}, u32[]{:S(2)}, u32[]{:S(2)}) collective-permute-start(bf16[2,288,128]{2,1,0:T(8,128)(2,1)S(1)} %pad_maximum_fusion.6), channel_id=1, source_target_pairs={{0,4},{1,5},{2,6},{3,7},{4,0},{5,1},{6,2},{7,3},{8,12},{9,13},{10,... | collective-permute-start | bytes 442376 | tf_op jit(solution)/shard_map/ppermute | solution.py:45
  76.3 15.9 %collective-permute-start.7 = (bf16[4,288,128]{2,1,0:T(8,128)(2,1)S(1)}, bf16[4,288,128]{2,1,0:T(8,128)(2,1)S(1)}, u32[]{:S(2)}, u32[]{:S(2)}) collective-permute-start(bf16[4,288,128]{2,1,0:T(8,128)(2,1)S(1)} %pad_maximum_fusion.3), channel_id=1, source_target_pairs={{0,12},{1,13},{2,14},{3,15},{4,8},{5,9},{6,10},{7,11},{8,4},{9,5},... | collective-permute-start | bytes 884744 | tf_op jit(solution)/shard_map/ppermute | solution.py:45
  92.3 6.6 %collective-permute-start.8 = (bf16[8,288,128]{2,1,0:T(8,128)(2,1)S(1)}, bf16[8,288,128]{2,1,0:T(8,128)(2,1)S(1)}, u32[]{:S(2)}, u32[]{:S(2)}) collective-permute-start(bf16[8,288,128]{2,1,0:T(8,128)(2,1)S(1)} %pad_maximum_fusion.1), channel_id=1, source_target_pairs={{0,1},{1,0},{2,3},{3,2},{4,5},{5,4},{6,7},{7,6},{8,9},{9,8},{10,11... | collective-permute-start | bytes 1769480 | tf_op jit(solution)/shard_map/ppermute | solution.py:45
  92.4 6.4 %collective-permute-start.9 = (bf16[1,272,128]{2,1,0:T(8,128)(2,1)S(1)}, bf16[1,272,128]{2,1,0:T(8,128)(2,1)S(1)}, u32[]{:S(2)}, u32[]{:S(2)}) collective-permute-start(bf16[1,272,128]{2,1,0:T(8,128)(2,1)S(1)} %maximum_bitcast_fusion.1), channel_id=1, source_target_pairs={{0,64},{16,80},{32,96},{48,112},{64,0},{80,16},{96,32},{112,48},{1... | collective-permute-start | bytes 208904 | tf_op jit(solution)/shard_map/ppermute | solution.py:45
  99.0 1.0 copy-start.8
  115.7 6.5 %collective-permute-start.10 = (bf16[2,272,128]{2,1,0:T(8,128)(2,1)S(1)}, bf16[2,272,128]{2,1,0:T(8,128)(2,1)S(1)}, u32[]{:S(2)}, u32[]{:S(2)}) collective-permute-start(bf16[2,272,128]{2,1,0:T(8,128)(2,1)S(1)} %pad_maximum_fusion.7), channel_id=1, source_target_pairs={{0,16},{16,0},{32,48},{48,32},{64,80},{80,64},{96,112},{112,96},{1... | collective-permute-start | bytes 417800 | tf_op jit(solution)/shard_map/ppermute | solution.py:45
  122.2 9.0 %collective-permute-start.11 = (bf16[4,272,128]{2,1,0:T(8,128)(2,1)S(1)}, bf16[4,272,128]{2,1,0:T(8,128)(2,1)S(1)}, u32[]{:S(2)}, u32[]{:S(2)}) collective-permute-start(bf16[4,272,128]{2,1,0:T(8,128)(2,1)S(1)} %pad_maximum_fusion.4), channel_id=1, source_target_pairs={{0,48},{16,32},{32,16},{48,0},{64,112},{80,96},{96,80},{112,64},{1... | collective-permute-start | bytes 835592 | tf_op jit(solution)/shard_map/ppermute | solution.py:45
  124.5 33.1 %all-to-all-start.1 = ((bf16[16,272,128]{2,1,0:T(8,128)(2,1)}), bf16[16,272,128]{2,1,0:T(8,128)(2,1)S(1)}, u32[]{:S(2)}, u32[]{:S(2)}) async-start(bf16[16,272,128]{2,1,0:T(8,128)(2,1)} %paged_attention.1), calls=%async_computation.1 | async-start | bytes 2228224 | tf_op jit(solution)/shard_map/all_to_all | solution.py:779
  131.3 3.2 %copy-start.9 = (bf16[8,272,128]{2,1,0:T(8,128)(2,1)}, bf16[8,272,128]{2,1,0:T(8,128)(2,1)S(1)}, u32[]{:S(2)}) copy-start(bf16[8,272,128]{2,1,0:T(8,128)(2,1)S(1)} %constant_dynamic-update-slice_fusion.5.q) | copy-start | bytes 1671172
  134.4 34.1 %copy-start.12 = (bf16[64,128]{1,0:T(8,128)(2,1)S(1)}, bf16[64,128]{1,0:T(8,128)(2,1)}, u32[]{:S(2)}) copy-start(bf16[64,128]{1,0:T(8,128)(2,1)} %get-tuple-element.53) | copy-start | bytes 49156
  134.5 34.1 %copy-start.13 = (bf16[64,128]{1,0:T(8,128)(2,1)S(1)}, bf16[64,128]{1,0:T(8,128)(2,1)}, u32[]{:S(2)}) copy-start(bf16[64,128]{1,0:T(8,128)(2,1)} %get-tuple-element.54) | copy-start | bytes 49156
  157.6 14.3 %copy-start.1 = (bf16[1024,512]{1,0:T(8,128)(2,1)S(1)}, bf16[1024,512]{1,0:T(8,128)(2,1)}, u32[]{:S(2)}) copy-start(bf16[1024,512]{1,0:T(8,128)(2,1)} %get-tuple-element.46.q) | copy-start | bytes 3145732
  157.6 14.3 %copy-start.2 = (bf16[1024,128]{1,0:T(8,128)(2,1)S(1)}, bf16[1024,128]{1,0:T(8,128)(2,1)}, u32[]{:S(2)}) copy-start(bf16[1024,128]{1,0:T(8,128)(2,1)} %get-tuple-element.47.keys) | copy-start | bytes 786436
  157.6 14.3 %copy-start.6 = (s32[1,8]{1,0:T(1,128)S(1)}, s32[1,8]{1,0:T(1,128)}, u32[]{:S(2)}) copy-start(s32[1,8]{1,0:T(1,128)} %blocks_ref.1) | copy-start | bytes 100
  157.6 22.9 %all-to-all-start.2 = ((bf16[8,272,128]{2,1,0:T(8,128)(2,1)}), bf16[8,272,128]{2,1,0:T(8,128)(2,1)S(1)}, u32[]{:S(2)}, u32[]{:S(2)}) async-start(bf16[8,272,128]{2,1,0:T(8,128)(2,1)} %get-tuple-element.51), calls=%async_computation.2 | async-start | bytes 1114112 | tf_op jit(solution)/shard_map/all_to_all | solution.py:804
  168.5 3.4 %copy-start.3 = (bf16[1024,128]{1,0:T(8,128)(2,1)S(1)}, bf16[1024,128]{1,0:T(8,128)(2,1)}, u32[]{:S(2)}) copy-start(bf16[1024,128]{1,0:T(8,128)(2,1)} %get-tuple-element.48.values) | copy-start | bytes 786436
Sparse Core Ops, SparseCore 0:
  34.0 100.4 all-gather.2
